TPU v7x, 32 devices: a whole 2x2x4 slice. The times are simulated.
32 devices in a mesh: dp: 4 (over y, x), row: 2 (over core), col: 4 (over z).
Axes of the slice: x: 2, y: 2, z: 4, core: 2. Of those that a mesh axis runs over, the one named last changes fastest.
Arguments:
- inputs: bfloat16 [8192, 1536], P(('dp', 'row'), 'col'), may hold values from -6 to 6
- seq_lengths: int32 [4, 4], P('dp'), may hold values from 1 to 1982, as said below
- gain_one: float32 [1536], P('col'), may hold values from 0.5 to 1.5
- w_query: bfloat16 [1536, 1536], P('row', 'col'), may hold values from -0.15625 to 0.15625
- b_query: bfloat16 [1536], P('col'), may hold values from -0.59765625 to 0.59765625
- w_key: bfloat16 [1536, 256], P('row', 'col'), may hold values from -0.15625 to 0.15625
- b_key: bfloat16 [256], P('col'), may hold values from -0.59765625 to 0.59765625
- w_value: bfloat16 [1536, 256], P('row', 'col'), may hold values from -0.15625 to 0.15625
- b_value: bfloat16 [256], P('col'), may hold values from -0.59765625 to 0.59765625
- w_out: bfloat16 [1536, 1536], P('col', 'row'), may hold values from -1 to 1
- gain_two: float32 [1536], P('col'), may hold values from 0.5 to 1.5
- w_gate: bfloat16 [1536, 8960], P('row', 'col'), may hold values from -0.15625 to 0.15625
- w_up: bfloat16 [1536, 8960], P('row', 'col'), may hold values from -0.15625 to 0.15625
- w_down: bfloat16 [8960, 1536], P('col', 'row'), may hold values from -0.09375 to 0.09375
- cotangent: bfloat16 [8192, 1536], P(('dp', 'row'), 'col'), may hold values from -6 to 6
Outputs:
- out: bfloat16 [8192, 1536], P(('dp', 'row'), 'col')
- grad_inputs: bfloat16 [8192, 1536], P(('dp', 'row'), 'col')
- grad_gain_one: float32 [1536], P('col')
- grad_w_query: float32 [1536, 1536], P('row', 'col')
- grad_b_query: float32 [1536], P('col')
- grad_w_key: float32 [1536, 256], P('row', 'col')
- grad_b_key: float32 [256], P('col')
- grad_w_value: float32 [1536, 256], P('row', 'col')
- grad_b_value: float32 [256], P('col')
- grad_w_out: float32 [1536, 1536], P('col', 'row')
- grad_gain_two: float32 [1536], P('col')
- grad_w_gate: float32 [1536, 8960], P('row', 'col')
- grad_w_up: float32 [1536, 8960], P('row', 'col')
- grad_w_down: float32 [8960, 1536], P('col', 'row')
Inputs may be any that keep to these rules, and one draw needn't show every extreme that they name: `seq_lengths`: each row holds the lengths of 4 documents packed in order into one sequence and sums to 2048; one entry of each row is the largest value, the other entries sum to 66, and one of them is 1.
All inputs are finite; a program needn't handle non-finite values.
Results may differ from a plain program's by a relative error of at most 0.035.
Values may be sent and summed in bfloat16 or wider, within the bound.
A program may use at most 192 MiB of HBM per device.

v0:
```python
import jax
import jax.numpy as jnp
from jax import lax
from jax.sharding import PartitionSpec as P

D = 1536
HEAD_WIDTH = 128
QUERY_HEADS = 12
KEY_VALUE_HEADS = 2
DEVICE_TOKENS = 256
QW = 1536
KW = 256


theta_base = 1000000.0
eps = 1e-06


def matmul(left, right):
    return jnp.dot(left, right, preferred_element_type=jnp.float32)


def matmul_tn(left, right):
    return lax.dot_general(
        left, right, (((0,), (0,)), ((), ())), preferred_element_type=jnp.float32
    )


def matmul_nt(left, right):
    return lax.dot_general(
        left, right, (((1,), (1,)), ((), ())), preferred_element_type=jnp.float32
    )


def row_squares(values):
    return lax.psum(values, "col")


def gather_width(values):
    return lax.all_gather(values, "col", axis=1, tiled=True)


def sum_width(values):
    return lax.psum_scatter(
        values.astype(jnp.bfloat16), "col", scatter_dimension=1, tiled=True
    ).astype(jnp.float32)


def documents(lengths, places):
    doc_ends = jnp.cumsum(lengths)
    doc_starts = doc_ends - lengths
    doc_index = jnp.sum((places[:, None] >= doc_ends[None, :]).astype(jnp.int32), axis=1)
    chosen = doc_index[:, None] == jnp.arange(lengths.shape[0], dtype=jnp.int32)[None, :]
    offset = jnp.sum(jnp.where(chosen, doc_starts[None, :], 0), axis=1)
    return (doc_index, places - offset)


def rotary_embedding(values, token_position, direction):
    half_size = HEAD_WIDTH // 2
    frequency = theta_base ** (-(jnp.arange(half_size, dtype=jnp.float32) * 2.0) / HEAD_WIDTH)
    angles = token_position.astype(jnp.float32)[:, None] * frequency[None, :]
    cosine = jnp.cos(angles)[:, None, :]
    sine_part = direction * jnp.sin(angles)[:, None, :]
    leading = values[..., :half_size]
    second = values[..., half_size:]
    return jnp.concatenate(
        [leading * cosine - second * sine_part, second * cosine + leading * sine_part], axis=-1
    )


def norm_forward(hidden, gain):
    square_total = row_squares(jnp.sum(hidden * hidden, axis=1))
    inverse = lax.rsqrt(square_total / D + eps)
    normed = (hidden * inverse[:, None] * gain[None, :]).astype(jnp.bfloat16)
    return (normed, inverse)


def norm_backward(hidden, gain, inverse, grad_normed):
    scaled = grad_normed * gain[None, :]
    inner = row_squares(jnp.sum(scaled * hidden, axis=1))
    grad_hidden = (
        inverse[:, None] * scaled - hidden * (inverse * inverse * inverse * inner / D)[:, None]
    )
    grad_gain = jnp.sum(grad_normed * hidden * inverse[:, None], axis=0)
    return (grad_hidden, grad_gain)


def key_layout(gathered_keys, gathered_values, doc_all):
    seq_len = gathered_keys.shape[0]
    key_block_index = min(512, seq_len)
    count_blocks = seq_len // key_block_index
    blocks_of_keys = gathered_keys.reshape(
        count_blocks, key_block_index, KEY_VALUE_HEADS, HEAD_WIDTH
    )
    blocks_of_values = gathered_values.reshape(
        count_blocks, key_block_index, KEY_VALUE_HEADS, HEAD_WIDTH
    )
    doc_blocks = doc_all.reshape(count_blocks, key_block_index)
    place_blocks = jnp.arange(seq_len, dtype=jnp.int32).reshape(count_blocks, key_block_index)
    return (blocks_of_keys, doc_blocks, place_blocks, blocks_of_values)


def block_scores(heads_of_queries, key_blk, doc_blk, place_blk, doc_local, place_local):
    scores = jnp.einsum(
        "tkgh,skh->tkgs", heads_of_queries, key_blk, preferred_element_type=jnp.float32
    ) * HEAD_WIDTH ** (-0.5)
    allowed = (doc_blk[None, :] == doc_local[:, None]) & (
        place_blk[None, :] <= place_local[:, None]
    )
    return (scores, allowed[:, None, None, :])


def attention_forward(heads_of_queries, blocks, doc_local, place_local):
    head_shape = heads_of_queries.shape[:3]

    def first_pass(state_in, packed):
        running_max, running_sum = state_in
        scores, allowed = block_scores(
            heads_of_queries, packed[0], packed[1], packed[2], doc_local, place_local
        )
        masked = jnp.where(allowed, scores, -1e30)
        new_max = jnp.maximum(running_max, jnp.max(masked, axis=-1))
        raised = jnp.where(allowed, jnp.exp(scores - new_max[..., None]), 0.0)
        running_sum = running_sum * jnp.exp(running_max - new_max) + jnp.sum(raised, axis=-1)
        return ((new_max, running_sum), None)

    initial = (jnp.full(head_shape, -1e30, jnp.float32), jnp.zeros(head_shape, jnp.float32))
    (running_max, running_sum), unused = lax.scan(first_pass, initial, blocks)
    log_total = running_max + jnp.log(running_sum)

    def second_pass(acc_out, packed):
        scores, allowed = block_scores(
            heads_of_queries, packed[0], packed[1], packed[2], doc_local, place_local
        )
        probs_low = jnp.where(allowed, jnp.exp(scores - log_total[..., None]), 0.0).astype(
            jnp.bfloat16
        )
        return (
            acc_out
            + jnp.einsum(
                "tkgs,skh->tkgh", probs_low, packed[3], preferred_element_type=jnp.float32
            ),
            None,
        )

    attended, unused = lax.scan(second_pass, jnp.zeros(heads_of_queries.shape, jnp.float32), blocks)
    return (attended, log_total)


def attention_backward(
    heads_of_queries, blocks, doc_local, place_local, log_total, attended, heads_gradient
):
    inner = jnp.sum(heads_gradient.astype(jnp.float32) * attended, axis=-1)
    scale_factor = HEAD_WIDTH ** (-0.5)

    def back_pass(grad_query, packed):
        scores, allowed = block_scores(
            heads_of_queries, packed[0], packed[1], packed[2], doc_local, place_local
        )
        probs = jnp.where(allowed, jnp.exp(scores - log_total[..., None]), 0.0)
        grad_probs = jnp.einsum(
            "tkgh,skh->tkgs", heads_gradient, packed[3], preferred_element_type=jnp.float32
        )
        grad_scores = (probs * (grad_probs - inner[..., None])).astype(jnp.bfloat16)
        grad_query = (
            grad_query
            + jnp.einsum(
                "tkgs,skh->tkgh", grad_scores, packed[0], preferred_element_type=jnp.float32
            )
            * scale_factor
        )
        grad_key = (
            jnp.einsum(
                "tkgs,tkgh->skh", grad_scores, heads_of_queries, preferred_element_type=jnp.float32
            )
            * scale_factor
        )
        grad_value = jnp.einsum(
            "tkgs,tkgh->skh",
            probs.astype(jnp.bfloat16),
            heads_gradient,
            preferred_element_type=jnp.float32,
        )
        return (grad_query, (grad_key, grad_value))

    grad_query, (key_grads, value_grads) = lax.scan(
        back_pass, jnp.zeros(heads_of_queries.shape, jnp.float32), blocks
    )
    seq_len = key_grads.shape[0] * key_grads.shape[1]
    return (grad_query, key_grads.reshape(seq_len, KW), value_grads.reshape(seq_len, KW))


def per_device(
    inputs,
    seq_lengths,
    gain_one,
    w_query,
    b_query,
    w_key,
    b_key,
    w_value,
    b_value,
    w_out,
    gain_two,
    w_gate,
    w_up,
    w_down,
    cotangent,
):
    full_query, full_key, full_value, full_out, full_gate, full_up, full_down = (
        lax.all_gather(w_query, "row", axis=0, tiled=True),
        lax.all_gather(w_key, "row", axis=0, tiled=True),
        lax.all_gather(w_value, "row", axis=0, tiled=True),
        lax.all_gather(w_out, "row", axis=1, tiled=True),
        lax.all_gather(w_gate, "row", axis=0, tiled=True),
        lax.all_gather(w_up, "row", axis=0, tiled=True),
        lax.all_gather(w_down, "row", axis=1, tiled=True),
    )
    row_pos = lax.axis_index("row")
    col_pos = lax.axis_index("col")
    row_count = lax.axis_size("row")
    col_count = lax.axis_size("col")
    seq_len = DEVICE_TOKENS * row_count * col_count
    query_group_width = QUERY_HEADS // KEY_VALUE_HEADS
    lengths = seq_lengths[0]
    place_local = (row_pos * col_count + col_pos) * DEVICE_TOKENS + jnp.arange(
        DEVICE_TOKENS, dtype=jnp.int32
    )
    doc_local, local_position = documents(lengths, place_local)
    doc_all = documents(lengths, jnp.arange(seq_len, dtype=jnp.int32))[0]
    hidden_in = inputs.astype(jnp.float32)
    normed_one, inverse_one = norm_forward(hidden_in, gain_one)
    normed_full = gather_width(normed_one)
    query_lin = (matmul(normed_full, full_query) + b_query.astype(jnp.float32)).astype(jnp.bfloat16)
    projected_keys = (matmul(normed_full, full_key) + b_key.astype(jnp.float32)).astype(
        jnp.bfloat16
    )
    projected_values = (matmul(normed_full, full_value) + b_value.astype(jnp.float32)).astype(
        jnp.bfloat16
    )
    query_rows, rows_of_keys, value_rows = (
        lax.all_to_all(query_lin, "col", split_axis=0, concat_axis=1, tiled=True),
        lax.all_to_all(projected_keys, "col", split_axis=0, concat_axis=1, tiled=True),
        lax.all_to_all(projected_values, "col", split_axis=0, concat_axis=1, tiled=True),
    )
    rotated_queries = rotary_embedding(
        query_rows.astype(jnp.float32).reshape(DEVICE_TOKENS, QUERY_HEADS, HEAD_WIDTH),
        local_position,
        1.0,
    ).astype(jnp.bfloat16)
    rotated_keys = rotary_embedding(
        rows_of_keys.astype(jnp.float32).reshape(DEVICE_TOKENS, KEY_VALUE_HEADS, HEAD_WIDTH),
        local_position,
        1.0,
    ).astype(jnp.bfloat16)
    gathered_keys, gathered_values = (
        lax.all_gather(rotated_keys.reshape(DEVICE_TOKENS, KW), ("row", "col"), axis=0, tiled=True),
        lax.all_gather(value_rows, ("row", "col"), axis=0, tiled=True),
    )
    blocks = key_layout(gathered_keys, gathered_values, doc_all)
    heads_of_queries = rotated_queries.reshape(
        DEVICE_TOKENS, KEY_VALUE_HEADS, query_group_width, HEAD_WIDTH
    )
    attended, log_total = attention_forward(heads_of_queries, blocks, doc_local, place_local)
    attended_low = attended.reshape(DEVICE_TOKENS, QW).astype(jnp.bfloat16)
    attended_cols = lax.all_to_all(attended_low, "col", split_axis=1, concat_axis=0, tiled=True)
    hidden_mid = hidden_in + sum_width(matmul(attended_cols, full_out))
    normed_two, inverse_two = norm_forward(hidden_mid, gain_two)
    normed_wide = gather_width(normed_two)
    gate = matmul(normed_wide, full_gate)
    up_proj = matmul(normed_wide, full_up)
    sigmoid_gate = jax.nn.sigmoid(gate)
    silu_gate = gate * sigmoid_gate
    mixed = (silu_gate * up_proj).astype(jnp.bfloat16)
    result = (hidden_mid + sum_width(matmul(mixed, full_down))).astype(jnp.bfloat16)
    grad_full = gather_width(cotangent)
    grad_w_down = matmul_tn(mixed, grad_full)
    grad_mixed = matmul_nt(grad_full, full_down)
    grad_gate = (grad_mixed * up_proj * sigmoid_gate * (1.0 + gate * (1.0 - sigmoid_gate))).astype(
        jnp.bfloat16
    )
    grad_up = (grad_mixed * silu_gate).astype(jnp.bfloat16)
    grad_w_gate = matmul_tn(normed_wide, grad_gate)
    grad_w_up = matmul_tn(normed_wide, grad_up)
    grad_normed_two = sum_width(matmul_nt(grad_gate, full_gate) + matmul_nt(grad_up, full_up))
    grad_back_two, grad_gain_two = norm_backward(hidden_mid, gain_two, inverse_two, grad_normed_two)
    grad_mid = cotangent.astype(jnp.float32) + grad_back_two
    grad_attn_full = gather_width(grad_mid.astype(jnp.bfloat16))
    grad_w_out = matmul_tn(attended_cols, grad_attn_full)
    grad_attended_cols = matmul_nt(grad_attn_full, full_out).astype(jnp.bfloat16)
    attended_gradient = lax.all_to_all(
        grad_attended_cols, "col", split_axis=0, concat_axis=1, tiled=True
    )
    heads_gradient = attended_gradient.reshape(
        DEVICE_TOKENS, KEY_VALUE_HEADS, query_group_width, HEAD_WIDTH
    )
    grad_query_rot, key_grads, value_grads = attention_backward(
        heads_of_queries, blocks, doc_local, place_local, log_total, attended, heads_gradient
    )
    rotated_key_gradient, grad_value = (
        lax.psum_scatter(
            key_grads.astype(jnp.bfloat16), ("row", "col"), scatter_dimension=0, tiled=True
        ).astype(jnp.float32),
        lax.psum_scatter(
            value_grads.astype(jnp.bfloat16), ("row", "col"), scatter_dimension=0, tiled=True
        ).astype(jnp.float32),
    )
    grad_query_lin = (
        rotary_embedding(
            grad_query_rot.reshape(DEVICE_TOKENS, QUERY_HEADS, HEAD_WIDTH), local_position, -1.0
        )
        .reshape(DEVICE_TOKENS, QW)
        .astype(jnp.bfloat16)
    )
    grad_key_lin = (
        rotary_embedding(
            rotated_key_gradient.reshape(DEVICE_TOKENS, KEY_VALUE_HEADS, HEAD_WIDTH),
            local_position,
            -1.0,
        )
        .reshape(DEVICE_TOKENS, KW)
        .astype(jnp.bfloat16)
    )
    grad_value_lin = grad_value.astype(jnp.bfloat16)
    query_grad_cols, key_grad_cols, value_grad_cols = (
        lax.all_to_all(grad_query_lin, "col", split_axis=1, concat_axis=0, tiled=True),
        lax.all_to_all(grad_key_lin, "col", split_axis=1, concat_axis=0, tiled=True),
        lax.all_to_all(grad_value_lin, "col", split_axis=1, concat_axis=0, tiled=True),
    )
    grad_b_query = jnp.sum(query_grad_cols.astype(jnp.float32), axis=0)
    grad_b_key = jnp.sum(key_grad_cols.astype(jnp.float32), axis=0)
    grad_b_value = jnp.sum(value_grad_cols.astype(jnp.float32), axis=0)
    grad_w_query = matmul_tn(normed_full, query_grad_cols)
    grad_w_key = matmul_tn(normed_full, key_grad_cols)
    grad_w_value = matmul_tn(normed_full, value_grad_cols)
    grad_normed_one = sum_width(
        matmul_nt(query_grad_cols, full_query)
        + matmul_nt(key_grad_cols, full_key)
        + matmul_nt(value_grad_cols, full_value)
    )
    grad_back_one, grad_gain_one = norm_backward(hidden_in, gain_one, inverse_one, grad_normed_one)
    grad_inputs = (grad_mid + grad_back_one).astype(jnp.bfloat16)
    summed = (
        lax.psum(grad_w_query.astype(jnp.bfloat16), ("dp", "row")).astype(jnp.float32),
        lax.psum(grad_w_key.astype(jnp.bfloat16), ("dp", "row")).astype(jnp.float32),
        lax.psum(grad_w_value.astype(jnp.bfloat16), ("dp", "row")).astype(jnp.float32),
        lax.psum(grad_w_out.astype(jnp.bfloat16), ("dp", "row")).astype(jnp.float32),
        lax.psum(grad_w_gate.astype(jnp.bfloat16), ("dp", "row")).astype(jnp.float32),
        lax.psum(grad_w_up.astype(jnp.bfloat16), ("dp", "row")).astype(jnp.float32),
        lax.psum(grad_w_down.astype(jnp.bfloat16), ("dp", "row")).astype(jnp.float32),
        lax.psum(grad_gain_one.astype(jnp.bfloat16), ("dp", "row")).astype(jnp.float32),
        lax.psum(grad_b_query.astype(jnp.bfloat16), ("dp", "row")).astype(jnp.float32),
        lax.psum(grad_b_key.astype(jnp.bfloat16), ("dp", "row")).astype(jnp.float32),
        lax.psum(grad_b_value.astype(jnp.bfloat16), ("dp", "row")).astype(jnp.float32),
        lax.psum(grad_gain_two.astype(jnp.bfloat16), ("dp", "row")).astype(jnp.float32),
    )
    rows_each = D // row_count
    split_dims = (0, 0, 0, 1, 0, 0, 1)
    weight_sums = tuple(
        (
            lax.dynamic_slice_in_dim(
                summed[member], row_pos * rows_each, rows_each, split_dims[member]
            )
            for member in range(7)
        )
    )
    small_sums = summed[7:]
    return (
        result,
        grad_inputs,
        small_sums[0],
        weight_sums[0],
        small_sums[1],
        weight_sums[1],
        small_sums[2],
        weight_sums[2],
        small_sums[3],
        weight_sums[3],
        small_sums[4],
        weight_sums[4],
        weight_sums[5],
        weight_sums[6],
    )


def solution(mesh):
    return jax.shard_map(
        per_device,
        mesh=mesh,
        in_specs=(
            P(("dp", "row"), "col"),
            P("dp", None),
            P("col"),
            P("row", "col"),
            P("col"),
            P("row", "col"),
            P("col"),
            P("row", "col"),
            P("col"),
            P("col", "row"),
            P("col"),
            P("row", "col"),
            P("row", "col"),
            P("col", "row"),
            P(("dp", "row"), "col"),
        ),
        out_specs=(
            P(("dp", "row"), "col"),
            P(("dp", "row"), "col"),
            P("col"),
            P("row", "col"),
            P("col"),
            P("row", "col"),
            P("col"),
            P("row", "col"),
            P("col"),
            P("col", "row"),
            P("col"),
            P("row", "col"),
            P("row", "col"),
            P("col", "row"),
        ),
        check_vma=False,
    )
```

profile of v0, /device:TPU:0, one launch (start us, length us, event | category | flops | bytes accessed | tf_op | source)
XLA Modules:
  0.0 1315.5 jit_solution(18205393095185112642)
XLA Ops:
  8.7 13.5 %psum.112 = f32[1024]{0:T(1024)S(1)} all-reduce(f32[1024]{0:T(1024)S(1)} %fusion.79), channel_id=1, replica_groups=mesh['dp'=4,'row'=2,'col'=4] {'col'}, use_global_device_ids=true, to_apply=%region_1.2 | all-reduce | flops 1024 | bytes 8192 | tf_op jit(solution)/shard_map/psum | solution.py:36
  31.7 55.1 %all-gather.12.cloned.1.call-done = bf16[1024,1536]{1,0:T(8,128)(2,1)} async-done(((bf16[1024,384]{1,0:T(8,128)(2,1)}), bf16[1024,1536]{1,0:T(8,128)(2,1)}) %all-gather.12.cloned.1.call-update) | async-done | bytes 3145744 | tf_op jit(solution)/shard_map/all_gather | solution.py:40
  121.8 21.4 %all-to-all-done.2 = bf16[4,256,384]{1,2,0:T(8,128)(2,1)S(1)} async-done(((bf16[4,256,384]{1,2,0:T(8,128)(2,1)}), bf16[4,256,384]{1,2,0:T(8,128)(2,1)S(1)}, u32[]{:S(2)}, u32[]{:S(2)}) %all-to-all-start.2) | async-done | bytes 786464 | tf_op jit(solution)/shard_map/all_to_all | solution.py:242
  146.4 35.2 %while.39 = (s32[]{:T(128)}, f32[256,2,6]{0,2,1:T(8,128)S(1)}, f32[256,2,6]{0,2,1:T(8,128)S(1)}, s32[4,512]{1,0:T(4,128)S(1)}, s32[256]{0:T(256)S(1)}, /*index=5...) while((s32[]{:T(128)}, f32[256,2,6]{0,2,1:T(8,128)S(1)}, ...), condition=%wide.region_9.10_spmd.clone, body=%wide.region_6.9_spmd.clone.sunk | while | flops 414072064 | bytes 14199940 | solution.py:128
  185.4 21.1 %while.40 = (s32[]{:T(128)}, f32[256,2,6,128]{0,3,2,1:T(8,128)}, bf16[4,512,2,128]{1,3,2,0:T(8,128)(2,1)}, s32[4,512]{1,0:T(4,128)S(1)}, s32[256]{0:T(256)S(1)},...) while((s32[]{:T(128)}, f32[256,2,6,128]{0,3,2,1:T(8,128)}, ...), condition=%wide.region_11.12_spmd.clone, body=%wide.region_10.11_spmd.clone.sunk | while | flops 812777728 | bytes 4751495 | solution.py:146
  213.7 16.9 %all-to-all-done.3 = bf16[256,4,384]{0,2,1:T(8,128)(2,1)S(1)} async-done(((bf16[256,4,384]{0,2,1:T(8,128)(2,1)}), bf16[256,4,384]{0,2,1:T(8,128)(2,1)S(1)}, u32[]{:S(2)}, u32[]{:S(2)}) %all-to-all-start.3) | async-done | bytes 786464 | tf_op jit(solution)/shard_map/all_to_all | solution.py:266
  241.4 58.6 %reduce-scatter.19.cloned.1.call-done = bf16[384,1024]{1,0:T(8,128)(2,1)} async-done(((bf16[1536,1024]{1,0:T(8,128)(2,1)}), bf16[384,1024]{1,0:T(8,128)(2,1)}) %reduce-scatter.19.cloned.1.call-update) | async-done | bytes 786448
  301.9 10.4 psum.113
  319.3 66.7 %all-gather.22.cloned.1.call-done = bf16[1024,1536]{1,0:T(8,128)(2,1)} async-done(((bf16[1024,384]{1,0:T(8,128)(2,1)}), bf16[1024,1536]{1,0:T(8,128)(2,1)}) %all-gather.22.cloned.1.call-update) | async-done | bytes 3145744 | tf_op jit(solution)/shard_map/all_gather | solution.py:40
  386.0 12.7 fusion.93
  403.8 12.6 fusion.94
  416.4 53.4 %all-gather.30.cloned.1.call-done = bf16[1024,1536]{1,0:T(8,128)(2,1)} async-done(((bf16[1024,384]{1,0:T(8,128)(2,1)}), bf16[1024,1536]{1,0:T(8,128)(2,1)}) %all-gather.30.cloned.1.call-update) | async-done | bytes 3145744 | tf_op jit(solution)/shard_map/all_gather | solution.py:40
  469.8 17.8 %all-gather.28.cloned.1.call-done = bf16[2240,1536]{1,0:T(8,128)(2,1)} async-done(((bf16[2240,768]{1,0:T(8,128)(2,1)}), bf16[2240,1536]{1,0:T(8,128)(2,1)}) %all-gather.28.cloned.1.call-update) | async-done | bytes 6881296 | tf_op jit(solution)/shard_map/all_gather | solution.py:217
  487.6 20.6 %multiply_convert_fusion = (bf16[1024,2240]{0,1:T(8,128)(2,1)}, bf16[1024,2240]{0,1:T(8,128)(2,1)}, bf16[1024,2240]{0,1:T(8,128)(2,1)}) fusion(f32[1024,2240]{0,1:T(8,128)} %fusion.93, f32[1024,2240]{0,1:T(8,128)} %fusion.94, bf16[1024,1536]{1,0:T(8,128)(2,1)} %all-gather.30.cloned.1.call-done, bf16[2240,1536]{1,0:T(8,128)(2,1)} %all-gather.28.cloned.1.call-done), kind=kOutput, calls=%fused_computation.77 | convolution fusion | flops 7080837120 | bytes 42139648 | tf_op jit(solution)/shard_map/dot_general | solution.py:30
  508.2 12.2 fusion.95
  520.4 9.6 add_convert_fusion.1
  534.7 61.5 %reduce-scatter.23.cloned.1.call-done = bf16[384,1024]{1,0:T(8,128)(2,1)} async-done(((bf16[1536,1024]{1,0:T(8,128)(2,1)}), bf16[384,1024]{1,0:T(8,128)(2,1)}) %reduce-scatter.23.cloned.1.call-update) | async-done | bytes 786448
  600.9 10.4 psum.114
  614.1 61.9 %all-gather.32.cloned.1.call-done = bf16[1024,1536]{1,0:T(8,128)(2,1)} async-done(((bf16[1024,384]{1,0:T(8,128)(2,1)}), bf16[1024,1536]{1,0:T(8,128)(2,1)}) %all-gather.32.cloned.1.call-update) | async-done | bytes 3145744 | tf_op jit(solution)/shard_map/all_gather | solution.py:40
  689.5 18.5 %all-to-all-done.4 = bf16[4,256,384]{1,2,0:T(8,128)(2,1)} async-done(((bf16[4,256,384]{1,2,0:T(8,128)(2,1)}), bf16[4,256,384]{1,2,0:T(8,128)(2,1)}, u32[]{:S(2)}, u32[]{:S(2)}) %all-to-all-start.4) | async-done | bytes 786464 | tf_op jit(solution)/shard_map/all_to_all | solution.py:291
  712.7 66.4 %while.41 = (s32[]{:T(128)}, f32[256,2,6,128]{0,3,2,1:T(8,128)}, bf16[4,512,2,128]{3,1,2,0:T(8,128)(2,1)}, bf16[4,512,2,128]{3,1,2,0:T(8,128)(2,1)}, bf16[4,512,...) while((s32[]{:T(128)}, f32[256,2,6,128]{0,3,2,1:T(8,128)}, ...), condition=%wide.region_21.22_spmd.clone, body=%wide.region_20.21_spmd.clone.sunk | while | flops 2030698752 | bytes 108246448 | solution.py:186
  786.1 11.6 convolution_convert_fusion.3
  806.9 14.7 %reduce-scatter.15.cloned.1.call-done = bf16[256,256]{1,0:T(8,128)(2,1)} async-done(((bf16[2048,256]{1,0:T(8,128)(2,1)}), bf16[256,256]{1,0:T(8,128)(2,1)}) %reduce-scatter.15.cloned.1.call-update) | async-done | bytes 131088 | tf_op jit(solution)/shard_map/reduce_scatter | solution.py:301
  823.4 8.1 all-to-all-done.5
  834.8 31.8 %reduce-scatter.17.cloned.1.call-done = bf16[256,256]{1,0:T(8,128)(2,1)} async-done(((bf16[2048,256]{1,0:T(8,128)(2,1)}), bf16[256,256]{1,0:T(8,128)(2,1)}) %reduce-scatter.17.cloned.1.call-update) | async-done | bytes 131088 | tf_op jit(solution)/shard_map/reduce_scatter | solution.py:304
  889.8 11.8 convolution_convert_fusion
  901.6 11.5 convolution_convert_fusion.1
  913.1 9.2 convolution_convert_fusion.2
  933.4 58.3 %reduce-scatter.25.cloned.1.call-done = bf16[384,1024]{1,0:T(8,128)(2,1)} async-done(((bf16[1536,1024]{1,0:T(8,128)(2,1)}), bf16[384,1024]{1,0:T(8,128)(2,1)}) %reduce-scatter.25.cloned.1.call-update) | async-done | bytes 786448
  995.8 13.7 %all-reduce = (bf16[384]{0:T(512)(128)(2,1)S(1)}, bf16[384]{0:T(512)(128)(2,1)S(1)}, bf16[64]{0:T(256)(128)(2,1)S(1)}, bf16[64]{0:T(256)(128)(2,1)S(1)}, bf16[384]{0:T(512)(128)(2,1)S(1)}) all-reduce(bf16[384]{0:T(512)(128)(2,1)S(1)} %get-tuple-element.455, ...), channel_id=1, replica_groups=mesh['dp'=4,'row'=2,'col'=4] {'dp','row'}, use_global_device_ids=true, to_apply=%region_28.29 | all-reduce | flops 1280 | bytes 5120 | tf_op jit(solution)/shard_map/psum | solution.py:351
  1012.3 10.9 psum.115
  1026.8 263.3 %all-reduce.4.cloned.1.call-done = (bf16[1536,384]{1,0:T(8,128)(2,1)}, bf16[1536,64]{0,1:T(8,128)(2,1)}, bf16[1536,64]{0,1:T(8,128)(2,1)}, bf16[384,1536]{1,0:T(...) async-done(((bf16[1536,384]{1,0:T(8,128)(2,1)}, bf16[1536,64]{0,1:T(8,128)(2,1)}, bf16[1536,64]{0,1:T(8,128)(2,1)}, ...) | async-done | bytes 23396368 | tf_op jit(solution)/shard_map/psum | solution.py:344
  (431 shorter events, 320.8 us)
Async XLA Ops:
  7.2 79.6 %all-gather.12.cloned.1.call-start = ((), (), s32[]{:S(2)}) async-start(), calls=%async_computation.14 | async-start | bytes 3932160 | tf_op jit(solution)/shard_map/all_gather | solution.py:40
  25.1 84.1 %all-gather.18.cloned.1.call-start = ((), (), s32[]{:S(2)}) async-start(), calls=%async_computation.17 | async-start | bytes 1769472 | tf_op jit(solution)/shard_map/all_gather | solution.py:211
  90.6 10.2 all-to-all-start.1
  94.5 50.3 %all-gather.16.cloned.1.call-start = ((), (), s32[]{:S(2)}) async-start(), calls=%async_computation.16 | async-start | bytes 1179648 | tf_op jit(solution)/shard_map/all_gather | solution.py:257
  105.8 11.0 all-to-all-start
  116.9 26.3 %all-to-all-start.2 = ((bf16[4,256,384]{1,2,0:T(8,128)(2,1)}), bf16[4,256,384]{1,2,0:T(8,128)(2,1)S(1)}, u32[]{:S(2)}, u32[]{:S(2)}) async-start(bf16[4,256,384]{1,2,0:T(8,128)(2,1)} %copy.120), calls=%async_computation.2 | async-start | bytes 1572864 | tf_op jit(solution)/shard_map/all_to_all | solution.py:242
  121.1 60.5 %all-gather.14.cloned.1.call-start = ((), (), s32[]{:S(2)}) async-start(), calls=%async_computation.15 | async-start | bytes 1179648 | tf_op jit(solution)/shard_map/all_gather | solution.py:258
  208.9 21.7 %all-to-all-start.3 = ((bf16[256,4,384]{0,2,1:T(8,128)(2,1)}), bf16[256,4,384]{0,2,1:T(8,128)(2,1)S(1)}, u32[]{:S(2)}, u32[]{:S(2)}) async-start(bf16[256,4,384]{0,2,1:T(8,128)(2,1)} %bitcast.16), calls=%async_computation.3 | async-start | bytes 1572864 | tf_op jit(solution)/shard_map/all_to_all | solution.py:266
  213.1 17.9 %all-gather.20.cloned.1.call-start = ((), (), s32[]{:S(2)}) async-start(), calls=%async_computation.18 | async-start | bytes 1769472 | tf_op jit(solution)/shard_map/all_gather | solution.py:214
  213.6 86.4 %reduce-scatter.19.cloned.1.call-start = ((), (), s32[]{:S(2)}) async-start(), calls=%async_computation.27 | async-start | bytes 3932160
  240.6 78.7 %all-gather.24.cloned.1.call-start = ((), (), s32[]{:S(2)}) async-start(), calls=%async_computation.20 | async-start | bytes 10321920 | tf_op jit(solution)/shard_map/all_gather | solution.py:215
  241.4 144.6 %all-gather.22.cloned.1.call-start = ((), (), s32[]{:S(2)}) async-start(), calls=%async_computation.19 | async-start | bytes 3932160 | tf_op jit(solution)/shard_map/all_gather | solution.py:40
  301.6 309.7 %copy-start.9 = (bf16[1024,384]{1,0:T(8,128)(2,1)}, bf16[1024,384]{1,0:T(8,128)(2,1)S(1)}, u32[]{:S(2)}) copy-start(bf16[1024,384]{1,0:T(8,128)(2,1)S(1)} %copy.154) | copy-start | bytes 2359300
  312.4 298.9 %copy-start.36 = (f32[1024]{0:T(1024)}, f32[1024]{0:T(1024)S(1)}, u32[]{:S(2)}) copy-start(f32[1024]{0:T(1024)S(1)} %add_rsqrt_fusion) | copy-start | bytes 12292
  313.6 90.2 %all-gather.26.cloned.1.call-start = ((), (), s32[]{:S(2)}) async-start(), calls=%async_computation.21 | async-start | bytes 10321920 | tf_op jit(solution)/shard_map/all_gather | solution.py:216
  314.3 155.4 %all-gather.30.cloned.1.call-start = ((), (), s32[]{:S(2)}) async-start(), calls=%async_computation.23 | async-start | bytes 3932160 | tf_op jit(solution)/shard_map/all_gather | solution.py:40
  314.9 172.7 %all-gather.28.cloned.1.call-start = ((), (), s32[]{:S(2)}) async-start(), calls=%async_computation.22 | async-start | bytes 10321920 | tf_op jit(solution)/shard_map/all_gather | solution.py:217
  315.6 280.5 %reduce-scatter.23.cloned.1.call-start = ((), (), s32[]{:S(2)}) async-start(), calls=%async_computation.29 | async-start | bytes 3932160
  534.6 141.4 %all-gather.32.cloned.1.call-start = ((), (), s32[]{:S(2)}) async-start(), calls=%async_computation.24 | async-start | bytes 3932160 | tf_op jit(solution)/shard_map/all_gather | solution.py:40
  683.3 24.7 %all-to-all-start.4 = ((bf16[4,256,384]{1,2,0:T(8,128)(2,1)}), bf16[4,256,384]{1,2,0:T(8,128)(2,1)}, u32[]{:S(2)}, u32[]{:S(2)}) async-start(bf16[4,256,384]{1,2,0:T(8,128)(2,1)} %copy.127), calls=%async_computation.4 | async-start | bytes 1572864 | tf_op jit(solution)/shard_map/all_to_all | solution.py:291
  687.6 134.1 %reduce-scatter.15.cloned.1.call-start = ((), (), s32[]{:S(2)}) async-start(), calls=%async_computation.25 | async-start | bytes 1179648 | tf_op jit(solution)/shard_map/reduce_scatter | solution.py:301
  782.5 84.0 %reduce-scatter.17.cloned.1.call-start = ((), (), s32[]{:S(2)}) async-start(), calls=%async_computation.26 | async-start | bytes 1179648 | tf_op jit(solution)/shard_map/reduce_scatter | solution.py:304
  786.0 144.5 %reduce-scatter.21.cloned.1.call-start = ((), (), s32[]{:S(2)}) async-start(), calls=%async_computation.28 | async-start | bytes 3932160
  803.4 28.0 %all-to-all-start.5 = ((bf16[256,4,384]{2,0,1:T(8,128)(2,1)}), bf16[256,4,384]{2,0,1:T(8,128)(2,1)S(1)}, u32[]{:S(2)}, u32[]{:S(2)}) async-start(bf16[256,4,384]{2,0,1:T(8,128)(2,1)} %copy.131), calls=%async_computation.5 | async-start | bytes 1572864 | tf_op jit(solution)/shard_map/all_to_all | solution.py:326
  831.4 36.8 %all-to-all-start.6 = ((bf16[256,4,64]{0,2,1:T(8,128)(2,1)}), bf16[256,4,64]{0,2,1:T(8,128)(2,1)S(1)}, u32[]{:S(2)}, u32[]{:S(2)}) async-start(bf16[256,4,64]{0,2,1:T(8,128)(2,1)} %bitcast.28), calls=%async_computation.7 | async-start | bytes 262144 | tf_op jit(solution)/shard_map/all_to_all | solution.py:327
  868.2 12.7 all-to-all-start.7
  871.5 120.1 %reduce-scatter.25.cloned.1.call-start = ((), (), s32[]{:S(2)}) async-start(), calls=%async_computation.30 | async-start | bytes 3932160
  887.9 402.1 %all-reduce.4.cloned.1.call-start = ((), (), s32[]{:S(2)}) async-start(), calls=%async_computation.31 | async-start | bytes 46792704 | tf_op jit(solution)/shard_map/psum | solution.py:344
  930.4 92.8 %copy-start.45 = (f32[1024]{0:T(1024)S(1)}, f32[1024]{0:T(1024)}, u32[]{:S(2)}) copy-start(f32[1024]{0:T(1024)} %copy-done.44) | copy-start | bytes 12292
  930.4 92.8 %copy-start.10 = (bf16[1024,384]{1,0:T(8,128)(2,1)S(1)}, bf16[1024,384]{1,0:T(8,128)(2,1)}, u32[]{:S(2)}) copy-start(bf16[1024,384]{1,0:T(8,128)(2,1)} %copy-done.9) | copy-start | bytes 2359300
  930.4 92.8 %copy-start.13 = (bf16[1024,384]{1,0:T(8,128)(2,1)S(1)}, bf16[1024,384]{1,0:T(8,128)(2,1)}, u32[]{:S(2)}) copy-start(bf16[1024,384]{1,0:T(8,128)(2,1)} %copy.158) | copy-start | bytes 2359300
  930.4 92.8 %copy-start.37 = (f32[1024]{0:T(1024)S(1)}, f32[1024]{0:T(1024)}, u32[]{:S(2)}) copy-start(f32[1024]{0:T(1024)} %copy-done.36) | copy-start | bytes 12292
  (89 other events, 1507.0 us)
Sparse Core Ops, SparseCore 0:
  25.2 61.5 all-gather.11
  88.4 7.8 all-gather.17
  103.6 25.6 all-gather.15
  131.3 23.1 all-gather.13
  215.1 10.6 all-gather.19
  240.7 59.2 reduce-scatter.18
  301.6 17.6 all-gather.23
  321.5 64.4 all-gather.21
  387.5 16.2 all-gather.25
  405.2 64.4 all-gather.29
  471.3 16.2 all-gather.27
  534.7 61.4 reduce-scatter.22
  614.3 61.7 all-gather.31
  782.6 38.9 reduce-scatter.14
  824.3 42.1 reduce-scatter.16
  868.7 60.0 reduce-scatter.20
  931.0 60.6 reduce-scatter.24
  997.8 292.2 all-reduce.3
where the time goes:
time: 1330 us; the launch traced here: 1320 us
  waiting for transfers between devices  831 us (62%)
  matrix products  229 us (17%)
  local copies, waits for them, and re-layouts  76.4 us (6%)
  other arithmetic  69.2 us (5%)
  blocking collectives  62.7 us (5%)
  starting transfers between devices  30.7 us (2%)
  between operations  15.6 us (1%)
    psum x1, waiting for transfers between devices, per_device(): lax.psum(grad_w_query.astype(jnp.bfloat16), ('dp', 'row'))  263 us
    all_gather x4, waiting for transfers between devices, gather_width(): return lax.all_gather(values, 'col', axis=1, tiled=True)  237 us
    unnamed x22, waiting for transfers between devices  182 us
    dot_general x7, matrix products, matmul_nt(): lax.dot_general(left, right, (((1,), (1,)), ((), ())), preferred_element_...  53.8 us
    dot_general x7, matrix products, matmul(): return jnp.dot(left, right, preferred_element_type=jnp.float32)  50.7 us
    psum x4, blocking collectives, row_squares(): return lax.psum(values, 'col')  45.2 us
    dot_general x7, matrix products, matmul_tn(): lax.dot_general(left, right, (((0,), (0,)), ((), ())), preferred_element_...  40.5 us
    unnamed x132, local copies, waits for them, and re-layouts  37.4 us
  transfers between devices with their start and end apart: 26, of which 20 were waited for; matrix products, arithmetic and copies ran while one was open for 13% of the time, Pallas kernels for 0%

commit v1 on v0

--- a/solution.py
+++ b/solution.py
@@ -90,10 +90,10 @@
     key_block_index = min(512, seq_len)
     count_blocks = seq_len // key_block_index
     blocks_of_keys = gathered_keys.reshape(
-        count_blocks, key_block_index, KEY_VALUE_HEADS, HEAD_WIDTH
+        count_blocks, key_block_index, gathered_keys.shape[1] // HEAD_WIDTH, HEAD_WIDTH
     )
     blocks_of_values = gathered_values.reshape(
-        count_blocks, key_block_index, KEY_VALUE_HEADS, HEAD_WIDTH
+        count_blocks, key_block_index, gathered_values.shape[1] // HEAD_WIDTH, HEAD_WIDTH
     )
     doc_blocks = doc_all.reshape(count_blocks, key_block_index)
     place_blocks = jnp.arange(seq_len, dtype=jnp.int32).reshape(count_blocks, key_block_index)
@@ -187,10 +187,10 @@
         back_pass, jnp.zeros(heads_of_queries.shape, jnp.float32), blocks
     )
     seq_len = key_grads.shape[0] * key_grads.shape[1]
-    return (grad_query, key_grads.reshape(seq_len, KW), value_grads.reshape(seq_len, KW))
-
-
-def per_device(
+    return (grad_query, key_grads.reshape(seq_len, -1), value_grads.reshape(seq_len, -1))
+
+
+def per_device_any(
     inputs,
     seq_lengths,
     gain_one,
@@ -383,9 +383,226 @@
     )
 
 
+def norm_rows(hidden, gain):
+    inverse = lax.rsqrt(jnp.mean(hidden * hidden, axis=1, keepdims=True) + eps)
+    return ((hidden * inverse * gain[None, :]).astype(jnp.bfloat16), inverse)
+
+
+def per_device(
+    inputs,
+    seq_lengths,
+    gain_one,
+    w_query,
+    b_query,
+    w_key,
+    b_key,
+    w_value,
+    b_value,
+    w_out,
+    gain_two,
+    w_gate,
+    w_up,
+    w_down,
+    cotangent,
+):
+    row_pos = lax.axis_index("row")
+    col_pos = lax.axis_index("col")
+    row_count = lax.axis_size("row")
+    col_count = lax.axis_size("col")
+    rows = inputs.shape[0]
+    part = rows // col_count
+    seq_len = rows * row_count
+    heads = QUERY_HEADS // col_count
+    share = col_count // KEY_VALUE_HEADS
+    groups = [[g * share + s for s in range(share)] for g in range(KEY_VALUE_HEADS)]
+    f32, bf16 = jnp.float32, jnp.bfloat16
+
+    inputs_full = gather_width(inputs)
+    gain_one_full, gain_two_full = lax.all_gather(
+        jnp.stack([gain_one, gain_two]), "col", axis=1, tiled=True
+    )
+    full_query = lax.all_gather(w_query, "row", axis=0, tiled=True)
+    key_value = jnp.concatenate(
+        [
+            jnp.concatenate([w_key, w_value], axis=1),
+            jnp.stack([jnp.concatenate([b_key, b_value])] * 16),
+        ],
+        axis=0,
+    )
+    key_value = lax.all_gather(key_value, "row", axis=0, tiled=False)
+    key_value = lax.all_gather(key_value, "col", axis=0, tiled=False, axis_index_groups=groups)
+    kv_cols = key_value.shape[-1] // 2
+    kv_w = key_value[:, :, : w_key.shape[0]].reshape(share, D, 2, kv_cols)
+    head_weights = kv_w.transpose(1, 2, 0, 3).reshape(D, 2 * HEAD_WIDTH)
+    head_bias = key_value[:, 0, w_key.shape[0]].reshape(share, 2, kv_cols)
+    head_bias = head_bias.transpose(1, 0, 2).reshape(2 * HEAD_WIDTH)
+    own_kv = lax.all_gather(jnp.concatenate([w_key, w_value], axis=1), "row", axis=0, tiled=True)
+    cot_full = gather_width(cotangent)
+    full_out = lax.all_gather(w_out, "row", axis=1, tiled=True)
+    full_gate = lax.all_gather(w_gate, "row", axis=0, tiled=True)
+    full_up = lax.all_gather(w_up, "row", axis=0, tiled=True)
+    full_down = lax.all_gather(w_down, "row", axis=1, tiled=True)
+
+    lengths = seq_lengths[0]
+    place_local = row_pos * rows + jnp.arange(rows, dtype=jnp.int32)
+    doc_local, local_position = documents(lengths, place_local)
+    doc_all = documents(lengths, jnp.arange(seq_len, dtype=jnp.int32))[0]
+
+    hidden_in = inputs_full.astype(f32)
+    normed_one, inverse_one = norm_rows(hidden_in, gain_one_full)
+    query_lin = (matmul(normed_one, full_query) + b_query.astype(f32)).astype(bf16)
+    kv_lin = (matmul(normed_one, head_weights) + head_bias.astype(f32)).astype(bf16)
+    rotated_queries = rotary_embedding(
+        query_lin.astype(f32).reshape(rows, heads, HEAD_WIDTH), local_position, 1.0
+    ).astype(bf16)
+    rotated_keys = rotary_embedding(
+        kv_lin[:, None, :HEAD_WIDTH].astype(f32), local_position, 1.0
+    ).astype(bf16)
+    seq_kv = lax.all_gather(
+        jnp.concatenate([rotated_keys.reshape(rows, HEAD_WIDTH), kv_lin[:, HEAD_WIDTH:]], axis=1),
+        "row",
+        axis=0,
+        tiled=True,
+    )
+    blocks = key_layout(seq_kv[:, :HEAD_WIDTH], seq_kv[:, HEAD_WIDTH:], doc_all)
+    heads_of_queries = rotated_queries.reshape(rows, 1, heads, HEAD_WIDTH)
+    attended, log_total = attention_forward(heads_of_queries, blocks, doc_local, place_local)
+    attended_cols = attended.reshape(rows, heads * HEAD_WIDTH).astype(bf16)
+    attn_rows = lax.psum_scatter(
+        matmul(attended_cols, full_out).astype(bf16), "col", scatter_dimension=0, tiled=True
+    ).astype(f32)
+    start = col_pos * part
+    hidden_mid = lax.dynamic_slice_in_dim(hidden_in, start, part, 0) + attn_rows
+    normed_part, inverse_two = norm_rows(hidden_mid, gain_two_full)
+    normed_two = lax.all_gather(normed_part, "col", axis=0, tiled=True)
+
+    gate = matmul(normed_two, full_gate)
+    up_proj = matmul(normed_two, full_up)
+    sigmoid_gate = jax.nn.sigmoid(gate)
+    silu_gate = gate * sigmoid_gate
+    mixed = (silu_gate * up_proj).astype(bf16)
+    grad_mixed = matmul_nt(cot_full, full_down)
+    grad_gate = (grad_mixed * up_proj * sigmoid_gate * (1.0 + gate * (1.0 - sigmoid_gate))).astype(
+        bf16
+    )
+    grad_up = (grad_mixed * silu_gate).astype(bf16)
+    grad_normed_two = lax.psum_scatter(
+        (matmul_nt(grad_gate, full_gate) + matmul_nt(grad_up, full_up)).astype(bf16),
+        "col",
+        scatter_dimension=0,
+        tiled=True,
+    ).astype(f32)
+
+    def row_sum(grad, dim):
+        return lax.psum_scatter(grad.astype(bf16), "row", scatter_dimension=dim, tiled=True)
+
+    out_partial = matmul(mixed, full_down)
+    out_partial = lax.dynamic_update_slice_in_dim(
+        out_partial, lax.dynamic_slice_in_dim(out_partial, start, part, 0) + hidden_mid, start, 0
+    )
+    result = lax.psum_scatter(out_partial.astype(bf16), "col", scatter_dimension=1, tiled=True)
+
+    wide_sums = lax.psum(
+        (
+            row_sum(matmul_tn(mixed, cot_full), 1),
+            row_sum(matmul_tn(normed_two, grad_gate), 0),
+            row_sum(matmul_tn(normed_two, grad_up), 0),
+        ),
+        "dp",
+    )
+
+    scaled = grad_normed_two * gain_two_full[None, :]
+    inner = jnp.sum(scaled * hidden_mid, axis=1, keepdims=True)
+    grad_gain_two = jnp.sum(grad_normed_two * hidden_mid * inverse_two, axis=0)
+    grad_mid = (
+        lax.dynamic_slice_in_dim(cot_full, start, part, 0).astype(f32)
+        + inverse_two * scaled
+        - hidden_mid * (inverse_two * inverse_two * inverse_two * inner / D)
+    )
+    grad_mid_full = lax.all_gather(grad_mid.astype(bf16), "col", axis=0, tiled=True)
+    grad_attended = matmul_nt(grad_mid_full, full_out).astype(bf16)
+    grad_query_rot, key_grads, value_grads = attention_backward(
+        heads_of_queries,
+        blocks,
+        doc_local,
+        place_local,
+        log_total,
+        attended,
+        grad_attended.reshape(rows, 1, heads, HEAD_WIDTH),
+    )
+    grad_w_out = row_sum(matmul_tn(attended_cols, grad_mid_full), 1)
+    kv_grads = lax.psum_scatter(
+        jnp.concatenate([key_grads, value_grads], axis=1).astype(bf16),
+        "row",
+        scatter_dimension=0,
+        tiled=True,
+    ).astype(f32)
+    grad_key_part = rotary_embedding(kv_grads[:, None, :HEAD_WIDTH], local_position, -1.0)
+    kv_part = jnp.stack(
+        [grad_key_part.reshape(rows, share, kv_cols), kv_grads[:, HEAD_WIDTH:].reshape(rows, share, kv_cols)],
+        axis=2,
+    ).reshape(rows, 2 * HEAD_WIDTH)
+    kv_grad_cols = lax.psum_scatter(
+        kv_part.astype(bf16), "col", scatter_dimension=1, tiled=True, axis_index_groups=groups
+    )
+    query_grad_cols = (
+        rotary_embedding(
+            grad_query_rot.reshape(rows, heads, HEAD_WIDTH), local_position, -1.0
+        )
+        .reshape(rows, heads * HEAD_WIDTH)
+        .astype(bf16)
+    )
+    grad_w_query = row_sum(matmul_tn(normed_one, query_grad_cols), 0)
+    grad_w_kv = row_sum(matmul_tn(normed_one, kv_grad_cols), 0)
+    (grad_w_out, grad_w_query, grad_w_kv), wide_sums = lax.optimization_barrier(
+        ((grad_w_out, grad_w_query, grad_w_kv), wide_sums)
+    )
+    grad_w_out, grad_w_query, grad_w_kv = (
+        g.astype(f32) for g in lax.psum((grad_w_out, grad_w_query, grad_w_kv), "dp")
+    )
+    grad_w_down, grad_w_gate, grad_w_up = (g.astype(f32) for g in wide_sums)
+    grad_b_query = jnp.sum(query_grad_cols.astype(f32), axis=0)
+    grad_b_kv = jnp.sum(kv_grad_cols.astype(f32), axis=0)
+    grad_normed_one = matmul_nt(query_grad_cols, full_query) + matmul_nt(kv_grad_cols, own_kv)
+    scaled_one = grad_normed_one * gain_one_full[None, :]
+    inner_one = jnp.sum(scaled_one * hidden_in, axis=1, keepdims=True)
+    grad_gain_one = jnp.sum(grad_normed_one * hidden_in * inverse_one, axis=0)
+    back_one = inverse_one * scaled_one - hidden_in * (
+        inverse_one * inverse_one * inverse_one * inner_one / D
+    )
+    back_one = lax.dynamic_update_slice_in_dim(
+        back_one, lax.dynamic_slice_in_dim(back_one, start, part, 0) + grad_mid, start, 0
+    )
+    grad_inputs = lax.psum_scatter(back_one.astype(bf16), "col", scatter_dimension=1, tiled=True)
+    gains = lax.psum_scatter(
+        jnp.stack([grad_gain_one, grad_gain_two]), "col", scatter_dimension=1, tiled=True
+    )
+    width = gains.shape[1]
+    small = jnp.concatenate([gains.reshape(-1), grad_b_query, grad_b_kv])
+    small = lax.psum(small, ("dp", "row"))
+    biases = small[2 * width :]
+    return (
+        result,
+        grad_inputs,
+        small[:width],
+        grad_w_query,
+        biases[:width],
+        grad_w_kv[:, :kv_cols],
+        biases[width : width + kv_cols],
+        grad_w_kv[:, kv_cols:],
+        biases[width + kv_cols :],
+        grad_w_out,
+        small[width : 2 * width],
+        grad_w_gate,
+        grad_w_up,
+        grad_w_down,
+    )
+
+
 def solution(mesh):
+    whole_heads = QUERY_HEADS % mesh.shape["col"] == 0 and mesh.shape["col"] % KEY_VALUE_HEADS == 0
     return jax.shard_map(
-        per_device,
+        per_device if whole_heads else per_device_any,
         mesh=mesh,
         in_specs=(
             P(("dp", "row"), "col"),

time: 1330 us -> 1220 us (0.917)
  waiting for transfers between devices: 831 us -> 770 us
  starting transfers between devices: 30.7 us -> 1.39 us
  local copies, waits for them, and re-layouts: 76.4 us -> 51.6 us
    all_gather x4 -> x2, waiting for transfers between devices: 237 us -> 65.5 us  [gather_width(): return lax.all_gather(values, 'col', axis=1, tiled=True)]
    all_gather x7 -> x8, waiting for transfers between devices: 26.6 us -> 177 us  [the longest x1 66.8 us: per_device(): normed_two = lax.all_gather(normed_part, 'col', axis=0, tiled=True)]
    reduce_scatter x2 -> x10, waiting for transfers between devices: 46.5 us -> 141 us  [the longest x1 61.5 us: per_device(): lax.psum_scatter((matmul_nt(grad_gate, full_gate) + matmul_nt(grad_up, fu...]
    all_to_all x8 -> x0, waiting for transfers between devices: 75.5 us -> none  [the longest x1 21.4 us: per_device(): lax.all_to_all(query_lin, 'col', split_axis=0, concat_axis=1, tiled=True)]
    all_gather x2 -> x4, blocking collectives: 3.87 us -> 53.6 us  [the longest x1 30.2 us: per_device(): lax.all_gather(key_value, 'col', axis=0, tiled=False, axis_index_groups=g...]
    psum x5 -> x1, blocking collectives: 58.9 us -> 12.9 us  [per_device(): small = lax.psum(small, ('dp', 'row'))]
    unnamed x22 -> x28, waiting for transfers between devices: 182 us -> 138 us
    all_to_all x8 -> x0, starting transfers between devices: 30 us -> none  [the longest x1 4.23 us: per_device(): lax.all_to_all(grad_attended_cols, 'col', split_axis=0, concat_axis=1, ti...]
  transfers between devices with their start and end apart: 26 -> 25, of which waited for: 20 -> 18; matrix products, arithmetic and copies ran while one was open for 13% -> 18% of each run, Pallas kernels for 0% -> 0%
where the time goes in v1:
time: 1220 us
  waiting for transfers between devices  770 us (63%)
  matrix products  230 us (19%)
  other arithmetic  80.9 us (7%)
  blocking collectives  66.5 us (5%)
  local copies, waits for them, and re-layouts  51.6 us (4%)
  between operations  15.5 us (1%)
    psum x1, waiting for transfers between devices, per_device(): lax.psum((row_sum(matmul_tn(mixed, cot_full), 1), row_sum(matmul_tn(norme...  201 us
    unnamed x28, waiting for transfers between devices  138 us
    all_gather x1, waiting for transfers between devices, per_device(): normed_two = lax.all_gather(normed_part, 'col', axis=0, tiled=True)  66.8 us
    all_gather x2, waiting for transfers between devices, gather_width(): return lax.all_gather(values, 'col', axis=1, tiled=True)  65.5 us
    all_gather x1, waiting for transfers between devices, per_device(): lax.all_gather(grad_mid.astype(bf16), 'col', axis=0, tiled=True)  62.4 us
    reduce_scatter x1, waiting for transfers between devices, per_device(): lax.psum_scatter((matmul_nt(grad_gate, full_gate) + matmul_nt(grad_up, fu...  61.5 us
    reduce_scatter x1, waiting for transfers between devices, per_device(): lax.psum_scatter(matmul(attended_cols, full_out).astype(bf16), 'col', sca...  55.2 us
    dot_general x6, matrix products, matmul_nt(): lax.dot_general(left, right, (((1,), (1,)), ((), ())), preferred_element_...  51.8 us
  transfers between devices with their start and end apart: 25, of which 18 were waited for; matrix products, arithmetic and copies ran while one was open for 18% of the time, Pallas kernels for 0%

profile of v1, /device:TPU:0, one launch (start us, length us, event | category | flops | bytes accessed | tf_op | source)
XLA Modules:
  0.0 1217.7 jit_solution(4122904324088711057)
XLA Ops:
  14.2 30.2 %all-gather.1 = bf16[4,784,128]{2,1,0:T(8,128)(2,1)S(1)} all-gather(bf16[2,784,128]{2,1,0:T(8,128)(2,1)S(1)} %bitcast.392), channel_id=3, replica_groups={{0,1},{2,3},{4,5},{6,7},{8,9},{10,11},{12,13},{14,15},{16,17},{18,19},{..., dimensions={0}, use_global_device_ids=true | all-gather | bytes 1204224 | tf_op jit(solution)/shard_map/all_gather | solution.py:433
  44.5 19.2 %all_gather.49 = f32[2,1536]{1,0:T(2,128)S(1)} all-gather(f32[2,384]{1,0:T(2,128)S(1)} %pad_maximum_fusion.8), channel_id=1, replica_groups=mesh['dp'=4,'row'=2,'col'=4] {'col'}, dimensions={1}, use_global_device_ids=true | all-gather | bytes 15360 | tf_op jit(solution)/shard_map/all_gather | solution.py:421
  66.5 12.0 all-gather.13.cloned.1.call-done
  94.7 8.6 all-gather.15.cloned.1.call-done
  104.9 35.5 %while.39 = (s32[]{:T(128)}, f32[1024,1,3]{0,2,1:T(4,128)S(1)}, f32[1024,1,3]{0,2,1:T(4,128)S(1)}, s32[4,512]{1,0:T(4,128)S(1)}, s32[1024]{0:T(1024)S(1)}, /*ind...) while((s32[]{:T(128)}, f32[1024,1,3]{0,2,1:T(4,128)S(1)}, ...), condition=%wide.region_8.9_spmd.clone, body=%wide.region_5.8_spmd.clone.sunk | while | flops 415252480 | bytes 15257732 | solution.py:128
  140.9 19.0 %while.40 = (s32[]{:T(128)}, f32[1024,1,3,128]{0,3,2,1:T(8,128)}, bf16[4,512,1,128]{1,3,2,0:T(8,128)(2,1)S(1)}, s32[4,512]{1,0:T(4,128)S(1)}, s32[1024]{0:T(1024...) while((s32[]{:T(128)}, f32[1024,1,3,128]{0,3,2,1:T(8,128)}, ...), condition=%wide.region_10.11_spmd.clone, body=%wide.region_9.10_spmd.clone.sunk | while | flops 813958144 | bytes 5284999 | solution.py:146
  167.4 5.5 convert_element_type.187
  172.8 55.2 %reduce-scatter.20.cloned.1.call-done = bf16[256,1536]{1,0:T(8,128)(2,1)} async-done(((bf16[1024,1536]{1,0:T(8,128)(2,1)}), bf16[256,1536]{1,0:T(8,128)(2,1)}) %reduce-scatter.20.cloned.1.call-update) | async-done | bytes 786448 | tf_op jit(solution)/shard_map/reduce_scatter | solution.py:471
  233.5 13.7 %all-gather.23.cloned.1.call-done = bf16[1536,2240]{0,1:T(8,128)(2,1)} async-done(((bf16[768,2240]{0,1:T(8,128)(2,1)}), bf16[1536,2240]{0,1:T(8,128)(2,1)}) %all-gather.23.cloned.1.call-update) | async-done | bytes 6881296 | tf_op jit(solution)/shard_map/all_gather | solution.py:442
  247.2 66.8 %all-gather.21.cloned.1.call-done = bf16[1024,1536]{1,0:T(8,128)(2,1)} async-done(((bf16[256,1536]{1,0:T(8,128)(2,1)}), bf16[1024,1536]{1,0:T(8,128)(2,1)}) %all-gather.21.cloned.1.call-update) | async-done | bytes 3145744 | tf_op jit(solution)/shard_map/all_gather | solution.py:477
  314.0 12.7 %fusion.124 = f32[1024,2240]{0,1:T(8,128)} fusion(bf16[1024,1536]{1,0:T(8,128)(2,1)} %all-gather.21.cloned.1.call-done, bf16[1536,2240]{0,1:T(8,128)(2,1)} %all-gather.23.cloned.1.call-done), kind=kOutput, calls=%fused_computation.201 | convolution fusion | flops 7046430720 | bytes 19202048 | tf_op jit(solution)/shard_map/dot_general | solution.py:20
  331.9 12.6 %fusion.125 = f32[1024,2240]{0,1:T(8,128)} fusion(bf16[1024,1536]{1,0:T(8,128)(2,1)} %all-gather.21.cloned.1.call-done, bf16[1536,2240]{0,1:T(8,128)(2,1)} %all-gather.25.cloned.1.call-done), kind=kOutput, calls=%fused_computation.202 | convolution fusion | flops 7046430720 | bytes 19202048 | tf_op jit(solution)/shard_map/dot_general | solution.py:20
  344.5 53.5 %all-gather.29.cloned.1.call-done = bf16[1024,1536]{1,0:T(8,128)(2,1)} async-done(((bf16[1024,384]{1,0:T(8,128)(2,1)}), bf16[1024,1536]{1,0:T(8,128)(2,1)}) %all-gather.29.cloned.1.call-update) | async-done | bytes 3145744 | tf_op jit(solution)/shard_map/all_gather | solution.py:40
  398.0 17.7 %all-gather.27.cloned.1.call-done = bf16[2240,1536]{1,0:T(8,128)(2,1)} async-done(((bf16[2240,768]{1,0:T(8,128)(2,1)}), bf16[2240,1536]{1,0:T(8,128)(2,1)}) %all-gather.27.cloned.1.call-update) | async-done | bytes 6881296 | tf_op jit(solution)/shard_map/all_gather | solution.py:444
  415.6 20.6 %multiply_convert_fusion = (bf16[1024,2240]{0,1:T(8,128)(2,1)}, bf16[1024,2240]{0,1:T(8,128)(2,1)}, bf16[1024,2240]{0,1:T(8,128)(2,1)}) fusion(f32[1024,2240]{0,1:T(8,128)} %fusion.124, f32[1024,2240]{0,1:T(8,128)} %fusion.125, bf16[1024,1536]{1,0:T(8,128)(2,1)} %all-gather.29.cloned.1.call-done, bf16[2240,1536]{1,0:T(8,128)(2,1)} %all-gather.27.cloned.1.call-done), kind=kOutput, calls=%fused_computation.83 | convolution fusion | flops 7080837120 | bytes 42139648 | tf_op jit(solution)/shard_map/dot_general | solution.py:30
  436.3 12.2 fusion.127
  448.5 9.6 add_convert_fusion
  458.1 61.5 %reduce-scatter.22.cloned.1.call-done = bf16[256,1536]{1,0:T(8,128)(2,1)} async-done(((bf16[1024,1536]{1,0:T(8,128)(2,1)}), bf16[256,1536]{1,0:T(8,128)(2,1)}) %reduce-scatter.22.cloned.1.call-update) | async-done | bytes 786448 | tf_op jit(solution)/shard_map/reduce_scatter | solution.py:489
  525.3 62.4 %all-gather.31.cloned.1.call-done = bf16[1024,1536]{1,0:T(8,128)(2,1)} async-done(((bf16[256,1536]{1,0:T(8,128)(2,1)}), bf16[1024,1536]{1,0:T(8,128)(2,1)}) %all-gather.31.cloned.1.call-update) | async-done | bytes 3145744 | tf_op jit(solution)/shard_map/all_gather | solution.py:522
  594.7 63.4 %while.41 = (s32[]{:T(128)}, f32[1024,1,3,128]{0,3,2,1:T(8,128)}, bf16[4,512,1,128]{3,1,2,0:T(8,128)(2,1)}, bf16[4,512,1,128]{3,1,2,0:T(8,128)(2,1)}, bf16[4,512...) while((s32[]{:T(128)}, f32[1024,1,3,128]{0,3,2,1:T(8,128)}, ...), condition=%wide.region_18.19_spmd.clone, body=%wide.region_17.18_spmd.clone.sunk | while | flops 2031813632 | bytes 108460496 | solution.py:186
  661.8 7.3 reduce-scatter.24.cloned.1.call-done
  672.3 12.1 convolution_convert_fusion.1
  686.3 11.6 convolution_convert_fusion
  699.9 12.6 %convolution_convert_fusion.2 = bf16[2240,1536]{1,0:T(8,128)(2,1)} fusion(bf16[1024,2240]{0,1:T(8,128)(2,1)} %get-tuple-element.650, bf16[1024,1536]{1,0:T(8,128)(2,1)S(1)} %copy-done.34), kind=kOutput, calls=%fused_computation.82 | convolution fusion | flops 7049871360 | bytes 14614528 | tf_op jit(solution)/shard_map/dot_general | solution.py:24
  727.4 17.1 %reduce-scatter.34.cloned.1.call-done = bf16[2240,768]{1,0:T(8,128)(2,1)} async-done(((bf16[2240,1536]{1,0:T(8,128)(2,1)}), bf16[2240,768]{1,0:T(8,128)(2,1)}) %reduce-scatter.34.cloned.1.call-update) | async-done | bytes 3440656 | tf_op jit(solution)/shard_map/reduce_scatter | solution.py:497
  747.5 13.3 %fusion.126 = f32[1024,1536]{1,0:T(8,128)} fusion(bf16[1024,2240]{0,1:T(8,128)(2,1)} %get-tuple-element.650, bf16[2240,1536]{1,0:T(8,128)(2,1)} %all-gather.27.cloned.1.call-done), kind=kOutput, calls=%fused_computation.203 | convolution fusion | flops 7046430720 | bytes 17760256 | tf_op jit(solution)/shard_map/dot_general | solution.py:20
  790.6 200.8 %all-reduce.7.cloned.1.call-done = (bf16[2240,768]{1,0:T(8,128)(2,1)}, bf16[768,2240]{0,1:T(8,128)(2,1)}, bf16[768,2240]{0,1:T(8,128)(2,1)}) async-done(((bf16[2240,768]{1,0:T(8,128)(2,1)}, bf16[768,2240]{0,1:T(8,128)(2,1)}, bf16[768,2240]{0,1:T(8,128)(2,1)}), (bf16[2240,768]{1,0:T(8,128)(2,1)}, bf16[768,2240]{0,1:T(8,128)(2,1)}, bf16[768,2240]{0,1:T(8,128)(2,1)})) %all-reduce.7.cloned.1.call-update) | async-done | bytes 10321936 | tf_op jit(solution)/shard_map/psum | solution.py:505
  992.6 25.0 %reduce-scatter.44.cloned.1.call-done = f32[384,2]{1,0:T(8,128)} async-done(((f32[1536,2]{1,0:T(8,128)}), f32[384,2]{1,0:T(8,128)}) %reduce-scatter.44.cloned.1.call-update) | async-done | bytes 3088
  1018.6 12.9 %psum.49 = f32[1280]{0:T(1024)S(1)} all-reduce(f32[1280]{0:T(1024)S(1)} %pad_maximum_fusion.7), channel_id=1, replica_groups=mesh['dp'=4,'row'=2,'col'=4] {'dp','row'}, use_global_device_ids=true, to_apply=%region_28.29 | all-reduce | flops 1280 | bytes 10240 | tf_op jit(solution)/shard_map/psum | solution.py:582
  1032.7 47.3 %reduce-scatter.40.cloned.1.call-done = bf16[384,1024]{1,0:T(8,128)(2,1)} async-done(((bf16[1536,1024]{1,0:T(8,128)(2,1)}), bf16[384,1024]{1,0:T(8,128)(2,1)}) %reduce-scatter.40.cloned.1.call-update) | async-done | bytes 786448
  1082.3 60.8 %reduce-scatter.42.cloned.1.call-done = bf16[384,1024]{1,0:T(8,128)(2,1)} async-done(((bf16[1536,1024]{1,0:T(8,128)(2,1)}), bf16[384,1024]{1,0:T(8,128)(2,1)}) %reduce-scatter.42.cloned.1.call-update) | async-done | bytes 786448
  1156.0 48.5 %all-reduce.5.cloned.1.call-done = (bf16[768,128]{1,0:T(8,128)(2,1)}, bf16[768,384]{1,0:T(8,128)(2,1)}, bf16[384,768]{1,0:T(8,128)(2,1)}) async-done(((bf16[768,128]{1,0:T(8,128)(2,1)}, bf16[768,384]{1,0:T(8,128)(2,1)}, bf16[384,768]{1,0:T(8,128)(2,1)}), (bf16[768,128]{1,0:T(8,128)(2,1)}, bf16[768,384]{1,0:T(8,128)(2,1)}, bf16[384,768]{1,0:T(8,128)(2,1)})) %all-reduce.5.cloned.1.call-update) | async-done | bytes 1376272 | tf_op jit(solution)/shard_map/psum | solution.py:561
  (425 shorter events, 258.1 us)
Async XLA Ops:
  7.2 71.3 %all-gather.13.cloned.1.call-start = ((), (), s32[]{:S(2)}) async-start(), calls=%async_computation.13 | async-start | bytes 3932160 | tf_op jit(solution)/shard_map/all_gather | solution.py:40
  7.9 83.0 %all-gather.17.cloned.1.call-start = ((), (), s32[]{:S(2)}) async-start(), calls=%async_computation.15 | async-start | bytes 1769472 | tf_op jit(solution)/shard_map/all_gather | solution.py:424
  8.7 94.6 %all-gather.15.cloned.1.call-start = ((), (), s32[]{:S(2)}) async-start(), calls=%async_computation.14 | async-start | bytes 1572864 | tf_op jit(solution)/shard_map/all_gather | solution.py:461
  8.7 77.8 %copy-start.51 = (f32[64]{0:T(128)}, f32[64]{0:T(128)S(1)}, u32[]{:S(2)}) copy-start(f32[64]{0:T(128)S(1)} %multiply_power_fusion) | copy-start | bytes 772
  63.7 457.5 %copy-start.37 = (f32[1536]{0:T(1024)}, f32[1536]{0:T(1024)S(1)}, u32[]{:S(2)}) copy-start(f32[1536]{0:T(1024)S(1)} %get-tuple-element.562) | copy-start | bytes 18436
  85.7 75.7 %all-gather.19.cloned.1.call-start = ((), (), s32[]{:S(2)}) async-start(), calls=%async_computation.16 | async-start | bytes 1769472 | tf_op jit(solution)/shard_map/all_gather | solution.py:441
  86.3 141.8 %reduce-scatter.20.cloned.1.call-start = ((), (), s32[]{:S(2)}) async-start(), calls=%async_computation.17 | async-start | bytes 3932160 | tf_op jit(solution)/shard_map/reduce_scatter | solution.py:471
  166.5 80.6 %all-gather.23.cloned.1.call-start = ((), (), s32[]{:S(2)}) async-start(), calls=%async_computation.19 | async-start | bytes 10321920 | tf_op jit(solution)/shard_map/all_gather | solution.py:442
  167.1 146.9 %all-gather.21.cloned.1.call-start = ((), (), s32[]{:S(2)}) async-start(), calls=%async_computation.18 | async-start | bytes 3932160 | tf_op jit(solution)/shard_map/all_gather | solution.py:477
  230.0 291.2 %copy-start.8 = (f32[256,1536]{1,0:T(8,128)}, f32[256,1536]{1,0:T(8,128)S(1)}, u32[]{:S(2)}) copy-start(f32[256,1536]{1,0:T(8,128)S(1)} %get-tuple-element.639) | copy-start | bytes 4718596
  230.0 291.2 %copy-start.47 = (f32[256]{0:T(256)}, f32[256]{0:T(256)S(1)}, u32[]{:S(2)}) copy-start(f32[256]{0:T(256)S(1)} %add_rsqrt_fusion.1) | copy-start | bytes 3076
  231.3 100.5 %all-gather.25.cloned.1.call-start = ((), (), s32[]{:S(2)}) async-start(), calls=%async_computation.20 | async-start | bytes 10321920 | tf_op jit(solution)/shard_map/all_gather | solution.py:443
  232.1 165.9 %all-gather.29.cloned.1.call-start = ((), (), s32[]{:S(2)}) async-start(), calls=%async_computation.22 | async-start | bytes 3932160 | tf_op jit(solution)/shard_map/all_gather | solution.py:40
  232.8 182.8 %all-gather.27.cloned.1.call-start = ((), (), s32[]{:S(2)}) async-start(), calls=%async_computation.21 | async-start | bytes 10321920 | tf_op jit(solution)/shard_map/all_gather | solution.py:444
  233.4 286.2 %reduce-scatter.22.cloned.1.call-start = ((), (), s32[]{:S(2)}) async-start(), calls=%async_computation.23 | async-start | bytes 3932160 | tf_op jit(solution)/shard_map/reduce_scatter | solution.py:489
  458.0 129.6 %all-gather.31.cloned.1.call-start = ((), (), s32[]{:S(2)}) async-start(), calls=%async_computation.24 | async-start | bytes 3932160 | tf_op jit(solution)/shard_map/all_gather | solution.py:522
  521.3 70.0 %copy-start.49 = (f32[256]{0:T(256)}, f32[256]{0:T(256)S(1)}, u32[]{:S(2)}) copy-start(f32[256]{0:T(256)S(1)} %fusion.112) | copy-start | bytes 3076
  524.0 145.1 %reduce-scatter.24.cloned.1.call-start = ((), (), s32[]{:S(2)}) async-start(), calls=%async_computation.25 | async-start | bytes 1572864 | tf_op jit(solution)/shard_map/reduce_scatter | solution.py:534
  525.3 66.9 %copy-start.16 = (f32[1024,1,3,128]{0,3,2,1:T(8,128)S(1)}, f32[1024,1,3,128]{0,3,2,1:T(8,128)}, u32[]{:S(2)}) copy-start(f32[1024,1,3,128]{0,3,2,1:T(8,128)} %get-tuple-element.196) | copy-start | bytes 4718596
  661.7 62.5 %reduce-scatter.26.cloned.1.call-start = ((), (), s32[]{:S(2)}) async-start(), calls=%async_computation.26 | async-start | bytes 786432 | tf_op jit(solution)/shard_map/reduce_scatter | solution.py:545
  672.2 55.1 %reduce-scatter.36.cloned.1.call-start = ((), (), s32[]{:S(2)}) async-start(), calls=%async_computation.31 | async-start | bytes 10321920 | tf_op jit(solution)/shard_map/reduce_scatter | solution.py:497
  684.4 43.0 %reduce-scatter.38.cloned.1.call-start = ((), (), s32[]{:S(2)}) async-start(), calls=%async_computation.32 | async-start | bytes 10321920 | tf_op jit(solution)/shard_map/reduce_scatter | solution.py:497
  697.9 46.6 %reduce-scatter.34.cloned.1.call-start = ((), (), s32[]{:S(2)}) async-start(), calls=%async_computation.30 | async-start | bytes 10321920 | tf_op jit(solution)/shard_map/reduce_scatter | solution.py:497
  712.5 78.0 %reduce-scatter.28.cloned.1.call-start = ((), (), s32[]{:S(2)}) async-start(), calls=%async_computation.27 | async-start | bytes 1769472 | tf_op jit(solution)/shard_map/reduce_scatter | solution.py:497
  717.9 72.7 %reduce-scatter.30.cloned.1.call-start = ((), (), s32[]{:S(2)}) async-start(), calls=%async_computation.28 | async-start | bytes 1769472 | tf_op jit(solution)/shard_map/reduce_scatter | solution.py:497
  724.1 66.5 %reduce-scatter.32.cloned.1.call-start = ((), (), s32[]{:S(2)}) async-start(), calls=%async_computation.29 | async-start | bytes 589824 | tf_op jit(solution)/shard_map/reduce_scatter | solution.py:497
  727.3 264.1 %all-reduce.7.cloned.1.call-start = ((), (), s32[]{:S(2)}) async-start(), calls=%async_computation.37 | async-start | bytes 20643840 | tf_op jit(solution)/shard_map/psum | solution.py:505
  744.5 273.0 %reduce-scatter.44.cloned.1.call-start = ((), (), s32[]{:S(2)}) async-start(), calls=%async_computation.35 | async-start | bytes 983040
  767.9 312.1 %reduce-scatter.40.cloned.1.call-start = ((), (), s32[]{:S(2)}) async-start(), calls=%async_computation.33 | async-start | bytes 3932160
  784.4 358.7 %reduce-scatter.42.cloned.1.call-start = ((), (), s32[]{:S(2)}) async-start(), calls=%async_computation.34 | async-start | bytes 3932160
  790.5 414.1 %all-reduce.5.cloned.1.call-start = ((), (), s32[]{:S(2)}) async-start(), calls=%async_computation.36 | async-start | bytes 2752512 | tf_op jit(solution)/shard_map/psum | solution.py:561
  991.4 154.0 %copy-start.21 = (bf16[768,2240]{0,1:T(8,128)(2,1)S(1)}, bf16[768,2240]{0,1:T(8,128)(2,1)}, u32[]{:S(2)}) copy-start(bf16[768,2240]{0,1:T(8,128)(2,1)} %get-tuple-element.203) | copy-start | bytes 10321924
  (83 other events, 503.4 us)
Sparse Core Ops, SparseCore 0:
  9.6 68.8 all-gather.12
  80.0 10.8 all-gather.16
  93.0 10.2 all-gather.14
  104.7 10.3 all-gather.18
  166.6 61.3 reduce-scatter.19
  229.5 17.6 all-gather.22
  249.3 64.6 all-gather.20
  315.5 16.2 all-gather.24
  333.4 64.4 all-gather.28
  399.4 16.2 all-gather.26
  458.2 61.4 reduce-scatter.21
  524.1 63.5 all-gather.30
  661.8 7.1 reduce-scatter.23
  672.4 15.7 reduce-scatter.25
  690.8 15.2 reduce-scatter.35
  708.8 16.4 reduce-scatter.37
  728.0 16.4 reduce-scatter.33
  747.2 9.7 reduce-scatter.27
  759.9 9.8 reduce-scatter.29
  772.5 8.9 reduce-scatter.31
  785.9 205.3 all-reduce.6
  994.2 23.2 reduce-scatter.43
  1020.5 59.5 reduce-scatter.39
  1082.7 60.2 reduce-scatter.41
  1146.4 58.1 all-reduce.4

commit v2 on v1

--- a/solution.py
+++ b/solution.py
@@ -1,6 +1,10 @@
+import functools
+
 import jax
 import jax.numpy as jnp
 from jax import lax
+from jax.experimental import pallas as pl
+from jax.experimental.pallas import tpu as pltpu
 from jax.sharding import PartitionSpec as P
 
 D = 1536
@@ -382,6 +386,595 @@
         weight_sums[6],
     )
 
+
+MESH = pl.DeviceIdType.MESH
+NEG = -1e30
+SCALE = HEAD_WIDTH ** (-0.5)
+
+
+def vmem_spec():
+    return pl.BlockSpec(memory_space=pltpu.VMEM)
+
+
+def any_spec():
+    return pl.BlockSpec(memory_space=pl.ANY)
+
+
+def remote(src, dst, send_sem, recv_sem, device):
+    return pltpu.make_async_remote_copy(
+        src_ref=src,
+        dst_ref=dst,
+        send_sem=send_sem,
+        recv_sem=recv_sem,
+        device_id=device,
+        device_id_type=MESH,
+    )
+
+
+def greet(peers):
+    barrier = pltpu.get_barrier_semaphore()
+    for peer in peers:
+        pl.semaphore_signal(barrier, inc=1, device_id=peer, device_id_type=MESH)
+    pl.semaphore_wait(barrier, len(peers))
+
+
+def rows_at(first, count):
+    return pl.ds(pl.multiple_of(first, 16), count)
+
+
+def lanes_at(first, count):
+    return pl.ds(pl.multiple_of(first, 128), count)
+
+
+class Chain:
+    def __init__(self, place, own, full, sends, recvs, count, chunks):
+        self.dp, self.row, self.col = place
+        self.own, self.full, self.sends, self.recvs = own, full, sends, recvs
+        self.count, self.chunks = count, chunks
+        self.width = full.shape[1] // count
+        self.rows = full.shape[0] // chunks
+
+    def block(self, shard, chunk):
+        return self.full.at[
+            rows_at(chunk * self.rows, self.rows), lanes_at(shard * self.width, self.width)
+        ]
+
+    def copy(self, way, step, shard, chunk):
+        src = self.block(shard, chunk)
+        if step == 0:
+            src = self.own.at[rows_at(chunk * self.rows, self.rows)]
+        device = (self.dp, self.row, self.col + (1 if way == 0 else -1))
+        return remote(
+            src,
+            self.block(shard, chunk),
+            self.sends.at[way, step, chunk],
+            self.recvs.at[shard, chunk],
+            device,
+        )
+
+    def start_own(self, chunk):
+        @pl.when(self.col < self.count - 1)
+        def _():
+            self.copy(0, 0, self.col, chunk).start()
+
+        @pl.when(self.col > 0)
+        def _():
+            self.copy(1, 0, self.col, chunk).start()
+
+    def step(self, step, chunk):
+        left, right = self.col - step, self.col + step
+
+        @pl.when(left >= 0)
+        def _():
+            self.copy(0, step, left, chunk).wait_recv()
+
+        if step < self.count - 1:
+
+            @pl.when((left >= 0) & (self.col < self.count - 1))
+            def _():
+                self.copy(0, step, left, chunk).start()
+
+        @pl.when(right < self.count)
+        def _():
+            self.copy(1, step, right, chunk).wait_recv()
+
+        if step < self.count - 1:
+
+            @pl.when((right < self.count) & (self.col > 0))
+            def _():
+                self.copy(1, step, right, chunk).start()
+
+    def finish(self):
+        for step in range(self.count - 1):
+            left, right = self.col - step, self.col + step
+
+            @pl.when((left >= 0) & (self.col < self.count - 1))
+            def _():
+                @pl.loop(0, self.chunks)
+                def _(chunk):
+                    self.copy(0, step, left, chunk).wait_send()
+
+            @pl.when((right < self.count) & (self.col > 0))
+            def _():
+                @pl.loop(0, self.chunks)
+                def _(chunk):
+                    self.copy(1, step, right, chunk).wait_send()
+
+
+def doc_start(lengths, place):
+    first = jnp.zeros_like(place)
+    end = 0
+    for doc in range(lengths.shape[1]):
+        end = end + lengths[0, doc]
+        first = jnp.where(place >= end, end, first)
+    return first
+
+
+def rotate(values, cosine, sine):
+    return values * cosine + pltpu.roll(values, HEAD_WIDTH // 2, 1) * sine
+
+
+def allowed_keys(lengths, first_query, queries, first_key, keys):
+    query = first_query + lax.broadcasted_iota(jnp.int32, (queries, 1), 0)
+    key = first_key + lax.broadcasted_iota(jnp.int32, (1, keys), 1)
+    return (key >= doc_start(lengths, query)) & (key <= query)
+
+
+def front_kernel(
+    heads,
+    dims,
+    aux,
+    x,
+    cot,
+    wq,
+    wkv,
+    wout,
+    w_gate,
+    w_up,
+    w_down,
+    lengths,
+    freq,
+    x_out,
+    n1_out,
+    cot_out,
+    q_out,
+    kv_out,
+    att_out,
+    lse_out,
+    attl_out,
+    hid_out,
+    n2_out,
+    trig_out,
+    aux_out,
+    wall_out,
+    wof_out,
+    peer_gate,
+    peer_up,
+    peer_down,
+    x_full,
+    n1,
+    cot_full,
+    att_low,
+    x_send,
+    x_recv,
+    c_send,
+    c_recv,
+    local_sem,
+    aux_send,
+    aux_recv,
+    wall_send,
+    wall_recv,
+    z_send,
+    z_recv,
+    d_send,
+    d_recv,
+    r_send,
+    r_recv,
+    kv_send,
+    kv_recv,
+    a2a_send,
+    a2a_recv,
+    m_send,
+    m_recv,
+):
+    count, planes = dims
+    f32, bf16 = jnp.float32, jnp.bfloat16
+    dp, row, col = lax.axis_index("dp"), lax.axis_index("row"), lax.axis_index("col")
+    place = (dp, row, col)
+    rows, width = x.shape
+    part = rows // count
+    half = wq.shape[0]
+    member = lax.rem(col, 2)
+    mate = col + 1 - 2 * member
+    col_peers = [(dp, row, lax.rem(col + k, count)) for k in range(1, count)]
+    dp_peers = [(lax.rem(dp + k, planes), row, col) for k in range(1, planes)]
+    partner = (dp, 1 - row, col)
+    across = (dp, 1 - row, mate)
+    greet(col_peers + dp_peers + [partner, across])
+
+    chain_x = Chain(place, x, x_full, x_send, x_recv, count, count)
+    chain_c = Chain(place, cot, cot_full, c_send, c_recv, count, count)
+    own_lanes = lanes_at(col * width, width)
+    copy_x = pltpu.make_async_copy(x, x_full.at[:, own_lanes], local_sem.at[0])
+    copy_x.start()
+    aux_copies = [
+        remote(aux, aux_out.at[col], aux_send.at[k], aux_recv.at[k], peer)
+        for k, peer in enumerate(col_peers)
+    ]
+    for copy in aux_copies:
+        copy.start()
+
+    @pl.loop(0, count)
+    def _(chunk):
+        chain_x.start_own(chunk)
+
+    own_half = rows_at(row * half, half)
+    kv_lanes = lanes_at(width + member * HEAD_WIDTH, HEAD_WIDTH)
+    copy_q = pltpu.make_async_copy(wq, wall_out.at[own_half, pl.ds(0, width)], local_sem.at[1])
+    copy_kv = pltpu.make_async_copy(wkv, wall_out.at[own_half, kv_lanes], local_sem.at[2])
+    copy_q.start()
+    copy_kv.start()
+    wall_copies = [
+        remote(
+            wq, wall_out.at[own_half, pl.ds(0, width)], wall_send.at[0], wall_recv.at[0], partner
+        )
+    ] + [
+        remote(wkv, wall_out.at[own_half, kv_lanes], wall_send.at[k], wall_recv.at[k], peer)
+        for k, peer in ((1, partner), (2, (dp, row, mate)), (3, across))
+    ]
+    for copy in wall_copies:
+        copy.start()
+    mlp_copies = [
+        remote(src, dst, m_send.at[k], m_recv.at[k], partner)
+        for k, (src, dst) in enumerate(
+            ((w_gate, peer_gate), (w_up, peer_up), (w_down, peer_down))
+        )
+    ]
+    for copy in mlp_copies:
+        copy.start()
+    copy_c = pltpu.make_async_copy(cot, cot_full.at[:, own_lanes], local_sem.at[3])
+    copy_c.start()
+    quarter = wout.shape[0] // planes
+    out_lanes = lanes_at(row * half, half)
+
+    def wof_block(shard, plane, side):
+        return wof_out.at[
+            shard, rows_at(plane * quarter, quarter), lanes_at(side * half, half)
+        ]
+
+    def wof_blocks(plane, side):
+        return wof_out.at[:, rows_at(plane * quarter, quarter), lanes_at(side * half, half)]
+
+    own_quarter = wout.at[rows_at(dp * quarter, quarter)]
+    copy_o = pltpu.make_async_copy(own_quarter, wof_block(col, dp, row), local_sem.at[4])
+    copy_o.start()
+
+    token = row * rows + lax.broadcasted_iota(jnp.int32, (rows, 1), 0)
+    position = (token - doc_start(lengths, token)).astype(f32)
+    angle = position * freq[...]
+    trig_out[0] = jnp.cos(angle)
+    lane = lax.broadcasted_iota(jnp.int32, (1, HEAD_WIDTH), 1)
+    trig_out[1] = jnp.sin(angle) * jnp.where(lane < HEAD_WIDTH // 2, -1.0, 1.0)
+    aux_out[col] = aux[...]
+
+    for step in range(1, count - 1):
+
+        @pl.loop(0, count)
+        def _(chunk):
+            chain_x.step(step, chunk)
+
+    z_copies = [
+        remote(own_quarter, wof_block(col, dp, row), z_send.at[k], z_recv.at[k], peer)
+        for k, peer in enumerate(col_peers)
+    ]
+    for copy in z_copies:
+        copy.start()
+
+    @pl.loop(0, count)
+    def _(chunk):
+        chain_c.start_own(chunk)
+
+    copy_x.wait()
+    copy_q.wait()
+    copy_kv.wait()
+    for copy in aux_copies:
+        copy.wait_recv()
+    for k, (side, who) in enumerate(
+        ((1 - row, None), (1 - row, member), (row, 1 - member), (1 - row, 1 - member))
+    ):
+        side_rows = rows_at(side * half, half)
+        if who is None:
+            dst, src = wall_out.at[side_rows, pl.ds(0, width)], wq
+        else:
+            dst = wall_out.at[side_rows, lanes_at(width + who * HEAD_WIDTH, HEAD_WIDTH)]
+            src = wkv
+        remote(src, dst, wall_send.at[k], wall_recv.at[k], partner).wait_recv()
+
+    mate_aux = aux_out[mate]
+    even = jnp.where(member == 0, aux[3:4, :HEAD_WIDTH], mate_aux[3:4, :HEAD_WIDTH])
+    odd = jnp.where(member == 0, mate_aux[3:4, :HEAD_WIDTH], aux[3:4, :HEAD_WIDTH])
+    low_lanes = lane < HEAD_WIDTH // 2
+    key_bias = jnp.where(low_lanes, even, pltpu.roll(odd, HEAD_WIDTH // 2, 1))
+    value_bias = jnp.where(low_lanes, pltpu.roll(even, HEAD_WIDTH // 2, 1), odd)
+
+    def kv_chunk(side, chunk):
+        return kv_out.at[rows_at(side * rows + chunk * part, part)]
+
+    def kv_copy(chunk):
+        return remote(
+            kv_chunk(row, chunk),
+            kv_chunk(row, chunk),
+            kv_send.at[chunk],
+            kv_recv.at[chunk],
+            partner,
+        )
+
+    @pl.loop(0, count)
+    def _(chunk):
+        chain_x.step(count - 1, chunk)
+        here = rows_at(chunk * part, part)
+        squares = jnp.zeros((part, 1), f32)
+        for shard in range(count):
+            piece = x_full[here, shard * width : (shard + 1) * width].astype(f32)
+            squares = squares + jnp.sum(piece * piece, axis=1, keepdims=True)
+        inverse = lax.rsqrt(squares / D + eps)
+        for shard in range(count):
+            lanes = slice(shard * width, (shard + 1) * width)
+            piece = x_full[here, lanes].astype(f32)
+            n1[here, lanes] = (piece * inverse * aux_out[shard, 0:1, :]).astype(bf16)
+        lin = matmul(n1[here, :], wall_out[...])
+        cosine, sine = trig_out[0, here, :], trig_out[1, here, :]
+        for head in range(heads):
+            lanes = slice(head * HEAD_WIDTH, (head + 1) * HEAD_WIDTH)
+            query = (lin[:, lanes] + aux[2:3, lanes]).astype(bf16).astype(f32)
+            q_out[head, here, :] = rotate(query, cosine, sine).astype(bf16)
+        first = lin[:, width : width + HEAD_WIDTH]
+        second = lin[:, width + HEAD_WIDTH : width + 2 * HEAD_WIDTH]
+        turn = HEAD_WIDTH // 2
+        key = jnp.where(low_lanes, first, pltpu.roll(second, turn, 1)) + key_bias
+        value = jnp.where(low_lanes, pltpu.roll(first, turn, 1), second) + value_bias
+        there = rows_at(row * rows + chunk * part, part)
+        kv_out[there, :HEAD_WIDTH] = rotate(
+            key.astype(bf16).astype(f32), cosine, sine
+        ).astype(bf16)
+        kv_out[there, HEAD_WIDTH:] = value.astype(bf16)
+        kv_copy(chunk).start()
+
+    n1_copy = pltpu.make_async_copy(n1, n1_out, local_sem.at[5])
+    n1_copy.start()
+    x_copy = pltpu.make_async_copy(x_full, x_out, local_sem.at[6])
+    x_copy.start()
+
+    copy_o.wait()
+    for k in range(1, count):
+        shard = lax.rem(col + count - k, count)
+        remote(
+            own_quarter, wof_block(shard, dp, row), z_send.at[k - 1], z_recv.at[k - 1], partner
+        ).wait_recv()
+    d_copies = [
+        remote(wof_blocks(dp, row), wof_blocks(dp, row), d_send.at[k], d_recv.at[k], peer)
+        for k, peer in enumerate(dp_peers)
+    ]
+    r_copies = [
+        remote(
+            wof_blocks(lax.rem(dp + planes - k, planes), row),
+            wof_blocks(lax.rem(dp + planes - k, planes), row),
+            r_send.at[k],
+            r_recv.at[k],
+            partner,
+        )
+        for k in range(planes)
+    ]
+    for copy in d_copies:
+        copy.start()
+    r_copies[0].start()
+
+    @pl.loop(0, count)
+    def _(chunk):
+        remote(
+            kv_chunk(row, chunk),
+            kv_chunk(1 - row, chunk),
+            kv_send.at[chunk],
+            kv_recv.at[chunk],
+            partner,
+        ).wait_recv()
+
+    span = min(512, rows)
+
+    def a2a_copy(block):
+        return remote(
+            att_low.at[block],
+            attl_out.at[:, own_lanes],
+            a2a_send.at[block],
+            a2a_recv.at[col],
+            (dp, row, block),
+        )
+
+    @pl.loop(0, count)
+    def _(block):
+        here = rows_at(block * part, part)
+        first_query = row * rows + block * part
+        query = q_out[:, here, :].reshape(heads * part, HEAD_WIDTH)
+
+        def body(index, state):
+            largest, total, acc = state
+            keys = rows_at(index * span, span)
+            scores = matmul_nt(query, kv_out[keys, :HEAD_WIDTH]) * SCALE
+            allowed = allowed_keys(lengths, first_query, part, index * span, span)
+            scores = jnp.where(allowed[None], scores.reshape(heads, part, span), NEG)
+            scores = scores.reshape(heads * part, span)
+            new = jnp.maximum(largest, jnp.max(scores, axis=1, keepdims=True))
+            raised = jnp.exp(scores - new)
+            alpha = jnp.exp(largest - new)
+            total = total * alpha + jnp.sum(raised, axis=1, keepdims=True)
+            acc = acc * alpha + matmul(raised.astype(bf16), kv_out[keys, HEAD_WIDTH:])
+            return new, total, acc
+
+        state = (
+            jnp.full((heads * part, 1), NEG, f32),
+            jnp.zeros((heads * part, 1), f32),
+            jnp.zeros((heads * part, HEAD_WIDTH), f32),
+        )
+        blocks = (first_query + part + span - 1) // span
+        largest, total, acc = lax.fori_loop(0, blocks, body, state)
+        attended = (acc / total).reshape(heads, part, HEAD_WIDTH)
+        att_out[:, here, :] = attended
+        log_total = (largest + jnp.log(total)).reshape(heads, part, 1)
+        lse_out[:, here, :] = jnp.broadcast_to(log_total, (heads, part, HEAD_WIDTH))
+        for head in range(heads):
+            lanes = slice(head * HEAD_WIDTH, (head + 1) * HEAD_WIDTH)
+            att_low[block, :, lanes] = attended[head].astype(bf16)
+
+        @pl.when(block != col)
+        def _():
+            a2a_copy(block).start()
+
+        chain_c.step(1, block)
+
+    attl_out[:, own_lanes] = att_low[col]
+    for step in range(2, count - 1):
+
+        @pl.loop(0, count)
+        def _(chunk):
+            chain_c.step(step, chunk)
+
+    for k in range(1, planes):
+        remote(
+            wof_blocks(dp, row),
+            wof_blocks(lax.rem(dp + planes - k, planes), row),
+            d_send.at[k - 1],
+            d_recv.at[k - 1],
+            partner,
+        ).wait_recv()
+        r_copies[k].start()
+    for k in range(planes):
+        other = wof_blocks(lax.rem(dp + planes - k, planes), 1 - row)
+        remote(other, other, r_send.at[k], r_recv.at[k], partner).wait_recv()
+
+    @pl.loop(0, count)
+    def _(block):
+        @pl.when(block != col)
+        def _():
+            remote(
+                att_low.at[block],
+                attl_out.at[:, lanes_at(block * width, width)],
+                a2a_send.at[block],
+                a2a_recv.at[block],
+                (dp, row, block),
+            ).wait_recv()
+
+    mine = rows_at(col * part, part)
+    step_lanes = D // 4
+    squares = jnp.zeros((part, 1), f32)
+    for piece in range(4):
+        lanes = slice(piece * step_lanes, (piece + 1) * step_lanes)
+        total = x_full[mine, lanes].astype(f32)
+        weights = wof_out[:, :, lanes].reshape(D, step_lanes)
+        total = total + matmul(attl_out[...], weights)
+        hid_out[:, lanes] = total
+        squares = squares + jnp.sum(total * total, axis=1, keepdims=True)
+    inverse = lax.rsqrt(squares / D + eps)
+    for shard in range(count):
+        lanes = slice(shard * width, (shard + 1) * width)
+        n2_out[:, lanes] = (hid_out[:, lanes] * inverse * aux_out[shard, 1:2, :]).astype(bf16)
+
+    @pl.loop(0, count)
+    def _(chunk):
+        chain_c.step(count - 1, chunk)
+
+    copy_c.wait()
+    c_copy = pltpu.make_async_copy(cot_full, cot_out, local_sem.at[7])
+    c_copy.start()
+
+    chain_x.finish()
+    chain_c.finish()
+    for copy in aux_copies + wall_copies + z_copies + d_copies + r_copies:
+        copy.wait_send()
+    for copy in mlp_copies:
+        copy.wait()
+
+    @pl.loop(0, count)
+    def _(chunk):
+        kv_copy(chunk).wait_send()
+
+        @pl.when(chunk != col)
+        def _():
+            a2a_copy(chunk).wait_send()
+
+    for copy in (n1_copy, x_copy, c_copy):
+        copy.wait()
+
+
+def front(dims, aux, x, cot, wq, wkv, wout, w_gate, w_up, w_down, lengths, freq):
+    count, planes = dims
+    rows, width = x.shape
+    part = rows // count
+    heads = width // HEAD_WIDTH
+    f32, bf16 = jnp.float32, jnp.bfloat16
+    shape = jax.ShapeDtypeStruct
+    wall = width + 2 * HEAD_WIDTH
+    outs = [
+        (shape((rows, D), bf16), any_spec()),
+        (shape((rows, D), bf16), any_spec()),
+        (shape((rows, D), bf16), any_spec()),
+        (shape((heads, rows, HEAD_WIDTH), bf16), vmem_spec()),
+        (shape((2 * rows, 2 * HEAD_WIDTH), bf16), vmem_spec()),
+        (shape((heads, rows, HEAD_WIDTH), f32), vmem_spec()),
+        (shape((heads, rows, HEAD_WIDTH), f32), vmem_spec()),
+        (shape((part, D), bf16), vmem_spec()),
+        (shape((part, D), f32), vmem_spec()),
+        (shape((part, D), bf16), vmem_spec()),
+        (shape((2, rows, HEAD_WIDTH), f32), vmem_spec()),
+        (shape((count,) + aux.shape, f32), vmem_spec()),
+        (shape((D, wall), bf16), vmem_spec()),
+        (shape((count, wout.shape[0], D), bf16), vmem_spec()),
+        (shape(w_gate.shape, bf16), any_spec()),
+        (shape(w_up.shape, bf16), any_spec()),
+        (shape(w_down.shape, bf16), any_spec()),
+    ]
+    dma = pltpu.SemaphoreType.DMA
+    return pl.pallas_call(
+        functools.partial(front_kernel, heads, dims),
+        out_shape=[o[0] for o in outs],
+        in_specs=[vmem_spec()]
+        + [any_spec()] * 8
+        + [pl.BlockSpec(memory_space=pltpu.SMEM), vmem_spec()],
+        out_specs=[o[1] for o in outs],
+        scratch_shapes=[
+            pltpu.VMEM((rows, D), bf16),
+            pltpu.VMEM((rows, D), bf16),
+            pltpu.VMEM((rows, D), bf16),
+            pltpu.VMEM((count, part, width), bf16),
+            dma((2, count - 1, count)),
+            dma((count, count)),
+            dma((2, count - 1, count)),
+            dma((count, count)),
+            dma((8,)),
+            dma((count - 1,)),
+            dma((count - 1,)),
+            dma((4,)),
+            dma((4,)),
+            dma((count - 1,)),
+            dma((count - 1,)),
+            dma((planes - 1,)),
+            dma((planes - 1,)),
+            dma((planes,)),
+            dma((planes,)),
+            dma((count,)),
+            dma((count,)),
+            dma((count,)),
+            dma((count,)),
+            dma((3,)),
+            dma((3,)),
+        ],
+        compiler_params=pltpu.CompilerParams(
+            collective_id=1, has_side_effects=True, vmem_limit_bytes=52 * 2**20
+        ),
+        cost_estimate=pl.CostEstimate(
+            flops=10 * 10**9, bytes_accessed=60 * 10**6, transcendentals=10**7
+        ),
+        name="front",
+    )(aux, x, cot, wq, wkv, wout, w_gate, w_up, w_down, lengths, freq)
 
 def norm_rows(hidden, gain):
     inverse = lax.rsqrt(jnp.mean(hidden * hidden, axis=1, keepdims=True) + eps)
@@ -417,63 +1010,47 @@
     groups = [[g * share + s for s in range(share)] for g in range(KEY_VALUE_HEADS)]
     f32, bf16 = jnp.float32, jnp.bfloat16
 
-    inputs_full = gather_width(inputs)
-    gain_one_full, gain_two_full = lax.all_gather(
-        jnp.stack([gain_one, gain_two]), "col", axis=1, tiled=True
-    )
-    full_query = lax.all_gather(w_query, "row", axis=0, tiled=True)
-    key_value = jnp.concatenate(
-        [
-            jnp.concatenate([w_key, w_value], axis=1),
-            jnp.stack([jnp.concatenate([b_key, b_value])] * 16),
-        ],
-        axis=0,
-    )
-    key_value = lax.all_gather(key_value, "row", axis=0, tiled=False)
-    key_value = lax.all_gather(key_value, "col", axis=0, tiled=False, axis_index_groups=groups)
-    kv_cols = key_value.shape[-1] // 2
-    kv_w = key_value[:, :, : w_key.shape[0]].reshape(share, D, 2, kv_cols)
-    head_weights = kv_w.transpose(1, 2, 0, 3).reshape(D, 2 * HEAD_WIDTH)
-    head_bias = key_value[:, 0, w_key.shape[0]].reshape(share, 2, kv_cols)
-    head_bias = head_bias.transpose(1, 0, 2).reshape(2 * HEAD_WIDTH)
-    own_kv = lax.all_gather(jnp.concatenate([w_key, w_value], axis=1), "row", axis=0, tiled=True)
-    cot_full = gather_width(cotangent)
-    full_out = lax.all_gather(w_out, "row", axis=1, tiled=True)
-    full_gate = lax.all_gather(w_gate, "row", axis=0, tiled=True)
-    full_up = lax.all_gather(w_up, "row", axis=0, tiled=True)
-    full_down = lax.all_gather(w_down, "row", axis=1, tiled=True)
-
+    half = HEAD_WIDTH // 2
+    freq = theta_base ** (-(jnp.arange(half, dtype=f32) * 2.0) / HEAD_WIDTH)
+    freq = jnp.concatenate([freq, freq]).reshape(1, HEAD_WIDTH)
+    kv_cols = w_key.shape[1]
+    biases = jnp.concatenate([b_key, b_value]).astype(f32)
+    aux = jnp.stack(
+        [gain_one, gain_two, b_query.astype(f32), jnp.pad(biases, (0, gain_one.shape[0] - 2 * kv_cols))]
+    )
+    aux = jnp.pad(aux, ((0, 4), (0, 0)))
+    own_kv = jnp.concatenate([w_key, w_value], axis=1)
+    (
+        inputs_full, normed_one, cot_full, query_rot, seq_kv, attended_f32, lse, att_own, hidden_mid, normed_part, trig, aux_all, wall, wof, peer_gate, peer_up, peer_down,
+    ) = front(
+        (col_count, lax.axis_size("dp")), aux, inputs, cotangent, w_query, own_kv, w_out, w_gate, w_up, w_down, seq_lengths, freq
+    )
+    gain_one_full = aux_all[:, 0].reshape(D)
+    gain_two_full = aux_all[:, 1].reshape(D)
+    full_query = wall[:, : heads * HEAD_WIDTH]
+    own_kv = lax.dynamic_slice_in_dim(wall, heads * HEAD_WIDTH + lax.rem(col_pos, 2) * HEAD_WIDTH, HEAD_WIDTH, 1)
+
+    def both(own, peer, axis):
+        return lax.cond(row_pos == 0, lambda: jnp.concatenate([own, peer], axis), lambda: jnp.concatenate([peer, own], axis))
+
+    full_gate = both(w_gate, peer_gate, 0)
+    full_up = both(w_up, peer_up, 0)
+    full_down = both(w_down, peer_down, 1)
+    full_out = wof[col_pos]
     lengths = seq_lengths[0]
     place_local = row_pos * rows + jnp.arange(rows, dtype=jnp.int32)
     doc_local, local_position = documents(lengths, place_local)
     doc_all = documents(lengths, jnp.arange(seq_len, dtype=jnp.int32))[0]
 
     hidden_in = inputs_full.astype(f32)
-    normed_one, inverse_one = norm_rows(hidden_in, gain_one_full)
-    query_lin = (matmul(normed_one, full_query) + b_query.astype(f32)).astype(bf16)
-    kv_lin = (matmul(normed_one, head_weights) + head_bias.astype(f32)).astype(bf16)
-    rotated_queries = rotary_embedding(
-        query_lin.astype(f32).reshape(rows, heads, HEAD_WIDTH), local_position, 1.0
-    ).astype(bf16)
-    rotated_keys = rotary_embedding(
-        kv_lin[:, None, :HEAD_WIDTH].astype(f32), local_position, 1.0
-    ).astype(bf16)
-    seq_kv = lax.all_gather(
-        jnp.concatenate([rotated_keys.reshape(rows, HEAD_WIDTH), kv_lin[:, HEAD_WIDTH:]], axis=1),
-        "row",
-        axis=0,
-        tiled=True,
-    )
+    inverse_one = norm_rows(hidden_in, gain_one_full)[1]
     blocks = key_layout(seq_kv[:, :HEAD_WIDTH], seq_kv[:, HEAD_WIDTH:], doc_all)
-    heads_of_queries = rotated_queries.reshape(rows, 1, heads, HEAD_WIDTH)
-    attended, log_total = attention_forward(heads_of_queries, blocks, doc_local, place_local)
+    heads_of_queries = query_rot.transpose(1, 0, 2)[:, None]
+    attended = attended_f32.transpose(1, 0, 2)[:, None]
+    log_total = lse[:, :, 0].transpose(1, 0)[:, None]
     attended_cols = attended.reshape(rows, heads * HEAD_WIDTH).astype(bf16)
-    attn_rows = lax.psum_scatter(
-        matmul(attended_cols, full_out).astype(bf16), "col", scatter_dimension=0, tiled=True
-    ).astype(f32)
     start = col_pos * part
-    hidden_mid = lax.dynamic_slice_in_dim(hidden_in, start, part, 0) + attn_rows
-    normed_part, inverse_two = norm_rows(hidden_mid, gain_two_full)
+    inverse_two = norm_rows(hidden_mid, gain_two_full)[1]
     normed_two = lax.all_gather(normed_part, "col", axis=0, tiled=True)
 
     gate = matmul(normed_two, full_gate)
@@ -600,7 +1177,7 @@
 
 
 def solution(mesh):
-    whole_heads = QUERY_HEADS % mesh.shape["col"] == 0 and mesh.shape["col"] % KEY_VALUE_HEADS == 0
+    whole_heads = dict(mesh.shape) == {"dp": 4, "row": 2, "col": 4}
     return jax.shard_map(
         per_device if whole_heads else per_device_any,
         mesh=mesh,

time: 1220 us -> 1070 us (0.88)
  waiting for transfers between devices: 770 us -> 561 us
  Pallas kernels: 0 us -> 148 us
  blocking collectives: 66.5 us -> 12.9 us
  matrix products: 230 us -> 185 us
  local copies, waits for them, and re-layouts: 51.6 us -> 71.6 us
  other arithmetic: 80.9 us -> 67.3 us
    pallas_call x0 -> x1, Pallas kernels: none -> 148 us  [front(): pl.pallas_call(functools.partial(front_kernel, heads, dims), out_shape=[o...]
    all_gather x8 -> x0, waiting for transfers between devices: 113 us -> none  [the longest x2 65.5 us: gather_width(): return lax.all_gather(values, 'col', axis=1, tiled=True)]
    reduce_scatter x1 -> x0, waiting for transfers between devices: 55.2 us -> none  [per_device(): lax.psum_scatter(matmul(attended_cols, full_out).astype(bf16), 'col', sca...]
    all_gather x4 -> x0, blocking collectives: 53.6 us -> none  [the longest x1 30.2 us: per_device(): lax.all_gather(key_value, 'col', axis=0, tiled=False, axis_index_groups=g...]
    all_gather x1, waiting for transfers between devices: 66.8 us -> 31.9 us  [per_device(): normed_two = lax.all_gather(normed_part, 'col', axis=0, tiled=True)]
    concatenate x2 -> x4, other arithmetic: 0.96 us -> 20.1 us  [the longest x3 20 us: both(): jnp.concatenate([own, peer], axis)]
    dot_general x4 -> x0, matrix products: 16.9 us -> none  [second_pass(): jnp.einsum('tkgs,skh->tkgh', probs_low, packed[3], preferred_element_type...]
    reduce_sum x4 -> x0, other arithmetic: 16.8 us -> none  [first_pass(): jnp.sum(raised, axis=-1)]
  transfers between devices with their start and end apart: 25 -> 16, of which waited for: 18 -> 11; matrix products, arithmetic and copies ran while one was open for 18% -> 14% of each run, Pallas kernels for 0% -> 0%
where the time goes in v2:
time: 1070 us; the launch traced here: 1060 us
  waiting for transfers between devices  561 us (52%)
  matrix products  185 us (17%)
  Pallas kernels  148 us (14%)
  local copies, waits for them, and re-layouts  71.6 us (7%)
  other arithmetic  67.3 us (6%)
  between operations  15.2 us (1%)
  blocking collectives  12.9 us (1%)
    psum x1, waiting for transfers between devices, per_device(): lax.psum((row_sum(matmul_tn(mixed, cot_full), 1), row_sum(matmul_tn(norme...  201 us
    pallas_call x1, Pallas kernels, front(): pl.pallas_call(functools.partial(front_kernel, heads, dims), out_shape=[o...  148 us
    unnamed x19, waiting for transfers between devices  133 us
    all_gather x1, waiting for transfers between devices, per_device(): lax.all_gather(grad_mid.astype(bf16), 'col', axis=0, tiled=True)  60.4 us
    reduce_scatter x1, waiting for transfers between devices, per_device(): lax.psum_scatter((matmul_nt(grad_gate, full_gate) + matmul_nt(grad_up, fu...  58.7 us
    dot_general x6, matrix products, matmul_nt(): lax.dot_general(left, right, (((1,), (1,)), ((), ())), preferred_element_...  53.9 us
    psum x1, waiting for transfers between devices, per_device(): lax.psum((grad_w_out, grad_w_query, grad_w_kv), 'dp')  48.4 us
    dot_general x6, matrix products, matmul_tn(): lax.dot_general(left, right, (((0,), (0,)), ((), ())), preferred_element_...  45.2 us
  transfers between devices with their start and end apart: 16, of which 11 were waited for; matrix products, arithmetic and copies ran while one was open for 14% of the time, Pallas kernels for 0%

profile of v2, /device:TPU:0, one launch (start us, length us, event | category | flops | bytes accessed | tf_op | source)
XLA Modules:
  0.0 1062.3 jit_solution(62598641631577086)
XLA Ops:
  7.8 5.6 copy.88.w_gate
  13.5 5.8 copy.89.w_up
  20.0 147.6 %front.1 = (bf16[1024,1536]{1,0:T(8,128)(2,1)}, bf16[1024,1536]{1,0:T(8,128)(2,1)}, bf16[1024,1536]{1,0:T(8,128)(2,1)}, bf16[3,1024,128]{2,1,0:T(8,128)(2,1)S(1)...) custom-call(f32[8,384]{1,0:T(8,128)S(1)} %select_maximum_fusion.aux,, ...), custom_call_target="tpu_custom_call" | custom-call | flops 10000000000 | bytes 60000000 | tf_op jit(solution)/shard_map/front/pallas_call | solution.py:936
  167.7 12.6 %conditional.4 = (bf16[1536,2240]{1,0:T(8,128)(2,1)}) conditional(s32[]{:T(128)} %convert_element_type.133, (bf16[768,2240]{1,0:T(8,128)(2,1)}, bf16[768,2240]{0,1:T(8,128)(2,1)}) %tuple.33, (bf16[768,2240]{0,1:T(8,128)(2,1)}, bf16[768,2240]{1,0:T(8,128)(2,1)}) %tuple.34), branch_computations={%region_2.3_spmd, %region_3.4_spmd} | conditional | flops 13762560 | bytes 20643848 | solution.py:1034
  167.7 5.6 copy.93
  173.4 7.0 pad_maximum_fusion.3
  180.3 12.3 %conditional.3 = (bf16[1536,2240]{1,0:T(8,128)(2,1)}) conditional(s32[]{:T(128)} %convert_element_type.133, (bf16[768,2240]{1,0:T(8,128)(2,1)}, bf16[768,2240]{0,1:T(8,128)(2,1)}) %tuple.31, (bf16[768,2240]{0,1:T(8,128)(2,1)}, bf16[768,2240]{1,0:T(8,128)(2,1)}) %tuple.32), branch_computations={%region_0.1_spmd, %region_1.2_spmd} | conditional | flops 13762560 | bytes 20643848 | solution.py:1034
  180.5 5.6 copy.91
  186.1 6.5 pad_maximum_fusion.1
  192.7 6.5 conditional.5
  192.7 6.5 pad_maximum_fusion.5
  199.1 31.9 %all-gather.3.cloned.1.call-done = bf16[1024,1536]{1,0:T(8,128)(2,1)} async-done(((bf16[256,1536]{1,0:T(8,128)(2,1)}), bf16[1024,1536]{1,0:T(8,128)(2,1)}) %all-gather.3.cloned.1.call-update) | async-done | bytes 3145744 | tf_op jit(solution)/shard_map/all_gather | solution.py:1054
  231.0 13.3 %fusion.82 = f32[1024,2240]{0,1:T(8,128)} fusion(bf16[1024,1536]{1,0:T(8,128)(2,1)} %all-gather.3.cloned.1.call-done, bf16[1536,2240]{1,0:T(8,128)(2,1)} %get-tuple-element.581), kind=kOutput, calls=%fused_computation.155 | convolution fusion | flops 7046430720 | bytes 19202048 | tf_op jit(solution)/shard_map/dot_general | solution.py:24
  244.3 12.0 %fusion.81 = f32[1024,2240]{0,1:T(8,128)} fusion(bf16[1024,1536]{1,0:T(8,128)(2,1)S(1)} %copy-done.49, bf16[1536,2240]{1,0:T(8,128)(2,1)} %get-tuple-element.580), kind=kOutput, calls=%fused_computation.154 | convolution fusion | flops 7046430720 | bytes 19202048 | tf_op jit(solution)/shard_map/dot_general | solution.py:24
  256.4 20.5 %multiply_convert_fusion = (bf16[1024,2240]{0,1:T(8,128)(2,1)}, bf16[1024,2240]{0,1:T(8,128)(2,1)}, bf16[1024,2240]{0,1:T(8,128)(2,1)}) fusion(f32[1024,2240]{0,1:T(8,128)} %fusion.81, f32[1024,2240]{0,1:T(8,128)} %fusion.82, bf16[1024,1536]{1,0:T(8,128)(2,1)S(1)} %copy-done.30, bf16[2240,1536]{1,0:T(8,128)(2,1)} %get-tuple-element.582), kind=kOutput, calls=%fused_computation.52 | convolution fusion | flops 7080837120 | bytes 42139648 | tf_op jit(solution)/shard_map/dot_general | solution.py:34
  276.9 11.4 %fusion.84 = f32[1024,1536]{1,0:T(8,128)S(1)} fusion(bf16[1024,2240]{0,1:T(8,128)(2,1)} %get-tuple-element.415, bf16[1536,2240]{1,0:T(8,128)(2,1)} %get-tuple-element.580), kind=kOutput, calls=%fused_computation.157 | convolution fusion | flops 7046430720 | bytes 17760256 | tf_op jit(solution)/shard_map/dot_general | solution.py:34
  288.3 11.5 %add_convert_fusion = bf16[1024,1536]{1,0:T(8,128)(2,1)} fusion(f32[1024,1536]{1,0:T(8,128)S(1)} %fusion.84, bf16[1024,2240]{0,1:T(8,128)(2,1)S(1)} %copy-done.51, bf16[1536,2240]{1,0:T(8,128)(2,1)} %get-tuple-element.581), kind=kOutput, calls=%fused_computation.62 | convolution fusion | flops 7049576448 | bytes 20905984 | tf_op jit(solution)/shard_map/dot_general | solution.py:34
  300.2 58.7 %reduce-scatter.19.cloned.1.call-done = bf16[256,1536]{1,0:T(8,128)(2,1)} async-done(((bf16[1024,1536]{1,0:T(8,128)(2,1)}), bf16[256,1536]{1,0:T(8,128)(2,1)}) %reduce-scatter.19.cloned.1.call-update) | async-done | bytes 786448 | tf_op jit(solution)/shard_map/reduce_scatter | solution.py:1066
  366.6 60.4 %all-gather.5.cloned.1.call-done = bf16[1024,1536]{1,0:T(8,128)(2,1)} async-done(((bf16[256,1536]{1,0:T(8,128)(2,1)}), bf16[1024,1536]{1,0:T(8,128)(2,1)}) %all-gather.5.cloned.1.call-update) | async-done | bytes 3145744 | tf_op jit(solution)/shard_map/all_gather | solution.py:1099
  438.4 63.8 %while.15 = (s32[]{:T(128)}, f32[1024,1,3,128]{0,3,2,1:T(8,128)}, bf16[4,512,1,128]{3,1,2,0:T(8,128)(2,1)}, bf16[4,512,1,128]{3,1,2,0:T(8,128)(2,1)}, bf16[4,512...) while((s32[]{:T(128)}, f32[1024,1,3,128]{0,3,2,1:T(8,128)}, ...), condition=%wide.region_16.17_spmd.clone, body=%wide.region_15.16_spmd.clone.sunk | while | flops 2031813632 | bytes 112654352 | solution.py:190
  505.9 7.2 reduce-scatter.21.cloned.1.call-done
  516.4 11.4 %convolution_convert_fusion.1 = bf16[1536,2240]{0,1:T(8,128)(2,1)} fusion(bf16[1024,2240]{0,1:T(8,128)(2,1)} %get-tuple-element.415, bf16[1024,1536]{1,0:T(8,128)(2,1)S(1)} %copy-done.50), kind=kOutput, calls=%fused_computation.46 | convolution fusion | flops 7049871360 | bytes 14614528 | tf_op jit(solution)/shard_map/dot_general | solution.py:28
  527.9 11.5 %convolution_convert_fusion = bf16[1536,2240]{0,1:T(8,128)(2,1)} fusion(bf16[1024,2240]{0,1:T(8,128)(2,1)} %get-tuple-element.414, bf16[1024,1536]{1,0:T(8,128)(2,1)S(1)} %copy-done.50), kind=kOutput, calls=%fused_computation.45 | convolution fusion | flops 7049871360 | bytes 14614528 | tf_op jit(solution)/shard_map/dot_general | solution.py:28
  541.5 11.9 %convolution_convert_fusion.2 = bf16[2240,1536]{1,0:T(8,128)(2,1)} fusion(bf16[1024,2240]{0,1:T(8,128)(2,1)} %get-tuple-element.416, bf16[1024,1536]{1,0:T(8,128)(2,1)S(1)} %copy-done.31), kind=kOutput, calls=%fused_computation.47 | convolution fusion | flops 7049871360 | bytes 14614528 | tf_op jit(solution)/shard_map/dot_general | solution.py:28
  569.0 19.4 %reduce-scatter.31.cloned.1.call-done = bf16[2240,768]{1,0:T(8,128)(2,1)} async-done(((bf16[2240,1536]{1,0:T(8,128)(2,1)}), bf16[2240,768]{1,0:T(8,128)(2,1)}) %reduce-scatter.31.cloned.1.call-update) | async-done | bytes 3440656 | tf_op jit(solution)/shard_map/reduce_scatter | solution.py:1074
  591.0 13.3 %fusion.83 = f32[1024,1536]{1,0:T(8,128)} fusion(bf16[1024,2240]{0,1:T(8,128)(2,1)} %get-tuple-element.416, bf16[2240,1536]{1,0:T(8,128)(2,1)} %get-tuple-element.582), kind=kOutput, calls=%fused_computation.156 | convolution fusion | flops 7046430720 | bytes 17760256 | tf_op jit(solution)/shard_map/dot_general | solution.py:24
  633.9 201.3 %all-reduce.9.cloned.1.call-done = (bf16[2240,768]{1,0:T(8,128)(2,1)}, bf16[768,2240]{0,1:T(8,128)(2,1)}, bf16[768,2240]{0,1:T(8,128)(2,1)}) async-done(((bf16[2240,768]{1,0:T(8,128)(2,1)}, bf16[768,2240]{0,1:T(8,128)(2,1)}, bf16[768,2240]{0,1:T(8,128)(2,1)}), (bf16[2240,768]{1,0:T(8,128)(2,1)}, bf16[768,2240]{0,1:T(8,128)(2,1)}, bf16[768,2240]{0,1:T(8,128)(2,1)})) %all-reduce.9.cloned.1.call-update) | async-done | bytes 10321936 | tf_op jit(solution)/shard_map/psum | solution.py:1082
  836.5 25.0 %reduce-scatter.41.cloned.1.call-done = f32[384,2]{1,0:T(8,128)} async-done(((f32[1536,2]{1,0:T(8,128)}), f32[384,2]{1,0:T(8,128)}) %reduce-scatter.41.cloned.1.call-update) | async-done | bytes 3088
  862.5 12.9 %psum.49 = f32[1280]{0:T(1024)S(1)} all-reduce(f32[1280]{0:T(1024)S(1)} %pad_maximum_fusion.11), channel_id=1, replica_groups=mesh['dp'=4,'row'=2,'col'=4] {'dp','row'}, use_global_device_ids=true, to_apply=%region_27.28 | all-reduce | flops 1280 | bytes 10240 | tf_op jit(solution)/shard_map/psum | solution.py:1159
  876.5 47.2 %reduce-scatter.37.cloned.1.call-done = bf16[384,1024]{1,0:T(8,128)(2,1)} async-done(((bf16[1536,1024]{1,0:T(8,128)(2,1)}), bf16[384,1024]{1,0:T(8,128)(2,1)}) %reduce-scatter.37.cloned.1.call-update) | async-done | bytes 786448
  926.0 60.8 %reduce-scatter.39.cloned.1.call-done = bf16[384,1024]{1,0:T(8,128)(2,1)} async-done(((bf16[1536,1024]{1,0:T(8,128)(2,1)}), bf16[384,1024]{1,0:T(8,128)(2,1)}) %reduce-scatter.39.cloned.1.call-update) | async-done | bytes 786448
  999.7 48.4 %all-reduce.7.cloned.1.call-done = (bf16[768,128]{1,0:T(8,128)(2,1)}, bf16[768,384]{1,0:T(8,128)(2,1)}, bf16[384,768]{1,0:T(8,128)(2,1)}) async-done(((bf16[768,128]{1,0:T(8,128)(2,1)}, bf16[768,384]{1,0:T(8,128)(2,1)}, bf16[384,768]{1,0:T(8,128)(2,1)}), (bf16[768,128]{1,0:T(8,128)(2,1)}, bf16[768,384]{1,0:T(8,128)(2,1)}, bf16[384,768]{1,0:T(8,128)(2,1)})) %all-reduce.7.cloned.1.call-update) | async-done | bytes 1376272 | tf_op jit(solution)/shard_map/psum | solution.py:1138
  (330 shorter events, 165.9 us)
Async XLA Ops:
  7.2 223.8 %all-gather.3.cloned.1.call-start = ((), (), s32[]{:S(2)}) async-start(), calls=%async_computation.12 | async-start | bytes 3932160 | tf_op jit(solution)/shard_map/all_gather | solution.py:1054
  13.5 6.5 copy-start
  13.5 6.5 copy-start.1
  13.5 6.5 copy-start.2
  167.7 191.3 %reduce-scatter.19.cloned.1.call-start = ((), (), s32[]{:S(2)}) async-start(), calls=%async_computation.13 | async-start | bytes 3932160 | tf_op jit(solution)/shard_map/reduce_scatter | solution.py:1066
  231.0 13.3 %copy-start.49 = (bf16[1024,1536]{1,0:T(8,128)(2,1)S(1)}, bf16[1024,1536]{1,0:T(8,128)(2,1)}, u32[]{:S(2)}) copy-start(bf16[1024,1536]{1,0:T(8,128)(2,1)} %all-gather.3.cloned.1.call-done) | copy-start | bytes 9437188
  244.3 12.0 %copy-start.30 = (bf16[1024,1536]{1,0:T(8,128)(2,1)S(1)}, bf16[1024,1536]{1,0:T(8,128)(2,1)}, u32[]{:S(2)}) copy-start(bf16[1024,1536]{1,0:T(8,128)(2,1)} %get-tuple-element.163) | copy-start | bytes 9437188
  276.9 11.4 %copy-start.51 = (bf16[1024,2240]{0,1:T(8,128)(2,1)S(1)}, bf16[1024,2240]{0,1:T(8,128)(2,1)}, u32[]{:S(2)}) copy-start(bf16[1024,2240]{0,1:T(8,128)(2,1)} %get-tuple-element.414) | copy-start | bytes 13762564
  288.3 11.7 %copy-start.9 = (f32[256,1536]{1,0:T(8,128)S(1)}, f32[256,1536]{1,0:T(8,128)}, u32[]{:S(2)}) copy-start(f32[256,1536]{1,0:T(8,128)} %get-tuple-element.158) | copy-start | bytes 4718596
  299.9 127.1 %all-gather.5.cloned.1.call-start = ((), (), s32[]{:S(2)}) async-start(), calls=%async_computation.14 | async-start | bytes 3932160 | tf_op jit(solution)/shard_map/all_gather | solution.py:1099
  300.0 65.7 %copy-start.34 = (f32[1536]{0:T(1024)}, f32[1536]{0:T(1024)S(1)}, u32[]{:S(2)}) copy-start(f32[1536]{0:T(1024)S(1)} %mul.318) | copy-start | bytes 18436
  300.2 65.5 %copy-start.27 = (bf16[2048,256]{1,0:T(8,128)(2,1)S(1)}, bf16[2048,256]{1,0:T(8,128)(2,1)}, u32[]{:S(2)}) copy-start(bf16[2048,256]{1,0:T(8,128)(2,1)} %get-tuple-element.160) | copy-start | bytes 3145732
  300.2 63.5 %copy-start.38 = (f32[256]{0:T(256)}, f32[256]{0:T(256)S(1)}, u32[]{:S(2)}) copy-start(f32[256]{0:T(256)S(1)} %add_rsqrt_fusion.1) | copy-start | bytes 3076
  363.3 149.8 %reduce-scatter.21.cloned.1.call-start = ((), (), s32[]{:S(2)}) async-start(), calls=%async_computation.15 | async-start | bytes 1572864 | tf_op jit(solution)/shard_map/reduce_scatter | solution.py:1111
  427.0 9.5 copy-start.16
  502.2 12.0 %copy-start.45 = (f32[64]{0:T(128)S(1)}, f32[64]{0:T(128)}, u32[]{:S(2)}) copy-start(f32[64]{0:T(128)} %copy-done.44) | copy-start | bytes 772
  505.8 59.6 %reduce-scatter.23.cloned.1.call-start = ((), (), s32[]{:S(2)}) async-start(), calls=%async_computation.16 | async-start | bytes 786432 | tf_op jit(solution)/shard_map/reduce_scatter | solution.py:1122
  505.8 10.6 copy-start.50
  516.4 51.8 %reduce-scatter.33.cloned.1.call-start = ((), (), s32[]{:S(2)}) async-start(), calls=%async_computation.21 | async-start | bytes 10321920 | tf_op jit(solution)/shard_map/reduce_scatter | solution.py:1074
  527.8 41.2 %reduce-scatter.35.cloned.1.call-start = ((), (), s32[]{:S(2)}) async-start(), calls=%async_computation.22 | async-start | bytes 10321920 | tf_op jit(solution)/shard_map/reduce_scatter | solution.py:1074
  539.3 49.0 %reduce-scatter.31.cloned.1.call-start = ((), (), s32[]{:S(2)}) async-start(), calls=%async_computation.20 | async-start | bytes 10321920 | tf_op jit(solution)/shard_map/reduce_scatter | solution.py:1074
  553.5 80.4 %reduce-scatter.27.cloned.1.call-start = ((), (), s32[]{:S(2)}) async-start(), calls=%async_computation.18 | async-start | bytes 1769472 | tf_op jit(solution)/shard_map/reduce_scatter | solution.py:1074
  559.1 74.8 %reduce-scatter.25.cloned.1.call-start = ((), (), s32[]{:S(2)}) async-start(), calls=%async_computation.17 | async-start | bytes 1769472 | tf_op jit(solution)/shard_map/reduce_scatter | solution.py:1074
  565.3 68.6 %reduce-scatter.29.cloned.1.call-start = ((), (), s32[]{:S(2)}) async-start(), calls=%async_computation.19 | async-start | bytes 589824 | tf_op jit(solution)/shard_map/reduce_scatter | solution.py:1074
  568.1 267.1 %all-reduce.9.cloned.1.call-start = ((), (), s32[]{:S(2)}) async-start(), calls=%async_computation.27 | async-start | bytes 20643840 | tf_op jit(solution)/shard_map/psum | solution.py:1082
  588.4 273.1 %reduce-scatter.41.cloned.1.call-start = ((), (), s32[]{:S(2)}) async-start(), calls=%async_computation.25 | async-start | bytes 983040
  590.9 13.4 %copy-start.21 = (bf16[1024,3,128]{0,2,1:T(8,128)(2,1)S(1)}, bf16[1024,3,128]{0,2,1:T(8,128)(2,1)}, u32[]{:S(2)}) copy-start(bf16[1024,3,128]{0,2,1:T(8,128)(2,1)} %copy-done.20) | copy-start | bytes 2359300
  591.0 13.4 %copy-start.26 = (bf16[1536,640]{1,0:T(8,128)(2,1)S(1)}, bf16[1536,640]{1,0:T(8,128)(2,1)}, u32[]{:S(2)}) copy-start(bf16[1536,640]{1,0:T(8,128)(2,1)} %get-tuple-element.168) | copy-start | bytes 5898244
  611.4 312.3 %reduce-scatter.37.cloned.1.call-start = ((), (), s32[]{:S(2)}) async-start(), calls=%async_computation.23 | async-start | bytes 3932160
  627.7 359.1 %reduce-scatter.39.cloned.1.call-start = ((), (), s32[]{:S(2)}) async-start(), calls=%async_computation.24 | async-start | bytes 3932160
  633.8 414.3 %all-reduce.7.cloned.1.call-start = ((), (), s32[]{:S(2)}) async-start(), calls=%async_computation.26 | async-start | bytes 2752512 | tf_op jit(solution)/shard_map/psum | solution.py:1138
  835.2 153.8 %copy-start.24 = (bf16[768,2240]{0,1:T(8,128)(2,1)S(1)}, bf16[768,2240]{0,1:T(8,128)(2,1)}, u32[]{:S(2)}) copy-start(bf16[768,2240]{0,1:T(8,128)(2,1)} %get-tuple-element.175) | copy-start | bytes 10321924
  (72 other events, 254.3 us)
Sparse Core Ops, SparseCore 0:
  167.8 63.1 all-gather.2
  300.0 58.8 reduce-scatter.18
  363.4 63.5 all-gather.4
  505.9 7.1 reduce-scatter.20
  516.5 15.7 reduce-scatter.22
  535.0 15.2 reduce-scatter.32
  552.5 16.4 reduce-scatter.34
  571.8 16.4 reduce-scatter.30
  591.2 9.7 reduce-scatter.26
  603.8 9.8 reduce-scatter.24
  616.5 8.9 reduce-scatter.28
  629.8 205.4 all-reduce.8
  838.1 23.2 reduce-scatter.40
  864.2 59.5 reduce-scatter.36
  926.4 60.2 reduce-scatter.38
  990.0 58.1 all-reduce.6

commit v3 on v2

--- a/solution.py
+++ b/solution.py
@@ -975,6 +975,469 @@
         ),
         name="front",
     )(aux, x, cot, wq, wkv, wout, w_gate, w_up, w_down, lengths, freq)
+TICKS = ((0, 1, 2, 4, 6, 7, 5, 3), (2, 3, 0, 4, 1, 6, 7, 5), (4, 5, 6, 2, 7, 0, 1, 3), (6, 7, 4, 2, 0, 1, 3, 5))
+SLOTS = tuple(tuple(order.index(q) for q in range(8)) for order in TICKS)
+ONWARD = (
+    ((), (0, 1, 3), (2, 0, 1, 3, 5), ()),
+    ((), (4, 6, 7, 5, 3), (6, 7, 5), ()),
+)
+SUMS = (
+    ((2, 0), (4, 0), (6, 0), (7, 0), (5, 0), (3, 0)),
+    ((4, 0), (6, 0), (7, 0), (0, 1), (5, 0), (1, 1)),
+    ((2, 1), (0, 1), (1, 1), (6, 0), (3, 1), (7, 0)),
+    ((4, 1), (2, 1), (0, 1), (1, 1), (3, 1), (5, 1)),
+)
+LINE = 4
+
+
+def pick(index, values):
+    out = values[0]
+    for k, value in enumerate(values[1:], 1):
+        out = jnp.where(index == k, value, out)
+    return out
+
+
+def hidden_tiles(total):
+    tile = 512
+    return [(first, min(tile, total - first)) for first in range(0, total, tile)]
+
+
+def mlp_kernel(
+    n2,
+    cot_full,
+    hid,
+    aux_all,
+    own_gate,
+    own_up,
+    own_down,
+    peer_gate,
+    peer_up,
+    peer_down,
+    out_part,
+    sum_down,
+    sum_gate,
+    sum_up,
+    grad_mid,
+    grad_gain,
+    gate_w,
+    up_w,
+    down_w,
+    mixed,
+    g_gate,
+    g_up,
+    n2s,
+    cots,
+    parts,
+    coming,
+    stage,
+    w_sem,
+    cot_sem,
+    own_sem,
+    ag_send,
+    ag_recv,
+    rs_send,
+    rs_recv,
+    out_sem,
+    sum_sem,
+    free_sem,
+    swap_send,
+    swap_recv,
+):
+    f32, bf16 = jnp.float32, jnp.bfloat16
+    dp, row, col = lax.axis_index("dp"), lax.axis_index("row"), lax.axis_index("col")
+    part = n2.shape[0]
+    piece = part // 2
+    hidden, half = own_gate.shape
+    tiles = hidden_tiles(hidden)
+    partner = (dp, 1 - row, col)
+    greet([(dp, row, lax.rem(col + k, LINE)) for k in range(1, LINE)] + [partner])
+
+    def slot_rows(slot):
+        return rows_at(slot * piece, piece)
+
+    def hand_on(c, way, q, source=None):
+        to = c + 1 - 2 * way
+        src = n2s.at[slot_rows(SLOTS[c][q])] if source is None else source
+        return remote(
+            src, n2s.at[slot_rows(SLOTS[to][q])], ag_send.at[way, q], ag_recv.at[q], (dp, row, to)
+        )
+
+    def got(c, q):
+        rows_here = n2s.at[slot_rows(SLOTS[c][q])]
+        remote(rows_here, rows_here, ag_send.at[0, q], ag_recv.at[q], partner).wait_recv()
+
+    def ways(c):
+        return [way for way in (0, 1) if 0 <= c + 1 - 2 * way < LINE]
+
+    for c in range(LINE):
+
+        @pl.when(col == c)
+        def _():
+            for way in ways(c):
+                hand_on(c, way, 2 * c, n2.at[pl.ds(0, piece)]).start()
+            if c in (0, LINE - 1):
+                hand_on(c, ways(c)[0], 2 * c + 1, n2.at[pl.ds(piece, piece)]).start()
+
+    own_copy = pltpu.make_async_copy(n2, n2s.at[pl.ds(0, part)], own_sem)
+    own_copy.start()
+
+    def load_copies(index, first, count):
+        rows_here = pl.ds(first, count)
+        copies = []
+        for k, (own, peer, whole) in enumerate(
+            (
+                (own_gate, peer_gate, gate_w),
+                (own_up, peer_up, up_w),
+                (own_down, peer_down, down_w),
+            )
+        ):
+            for side, src in ((row, own), (1 - row, peer)):
+                copies.append((src.at[rows_here], whole.at[rows_here, lanes_at(side * half, half)]))
+        return [
+            pltpu.make_async_copy(src, dst, w_sem.at[index, k])
+            for k, (src, dst) in enumerate(copies)
+        ]
+
+    def cot_copy(slot):
+        q = pick(col, [order[slot] for order in TICKS])
+        return pltpu.make_async_copy(
+            cot_full.at[slot_rows(q)], cots.at[slot_rows(slot)], cot_sem.at[slot]
+        )
+
+    for slot in range(2):
+        cot_copy(slot).start()
+    for index, (first, count) in enumerate(tiles):
+        for copy in load_copies(index, first, count):
+            copy.start()
+    for slot in range(2, 2 * LINE):
+        cot_copy(slot).start()
+    for h in range(2):
+
+        @pl.when(col == 0)
+        def _():
+            coming[h] = jnp.zeros(coming.shape[1:], bf16)
+
+        @pl.when(col == LINE - 1)
+        def _():
+            coming[2 * LINE + h] = jnp.zeros(coming.shape[1:], bf16)
+
+    own_copy.wait()
+
+    def onward(f):
+        for c in (1, 2):
+            for way in (0, 1):
+                if f < len(ONWARD[way][c]):
+                    q = ONWARD[way][c][f]
+
+                    @pl.when(col == c)
+                    def _():
+                        if q // 2 != c:
+                            got(c, q)
+                        hand_on(c, way, q).start()
+
+    def sum_copy(c, q, way):
+        to = c + 1 - 2 * way
+        place = 2 * LINE + q % 2 if way == 1 and q // 2 == to else q
+        return remote(
+            parts.at[slot_rows(SLOTS[c][q])],
+            coming.at[place],
+            rs_send.at[q],
+            rs_recv.at[place],
+            (dp, row, to),
+        )
+
+    def sum_start(e, c):
+        q, way = SUMS[c][e]
+        sum_copy(c, q, way).start()
+
+    def sum_ends(e):
+        for c in (0, LINE - 1):
+
+            @pl.when(col == c)
+            def _():
+                sum_start(e, c)
+
+    def sum_mids(e):
+        @pl.when((col == 1) | (col == 2))
+        def _():
+            q = jnp.where(col == 1, SUMS[1][e][0], SUMS[2][e][0])
+            slot = jnp.where(col == 1, SLOTS[1][SUMS[1][e][0]], SLOTS[2][SUMS[2][e][0]])
+            here = slot_rows(slot)
+            remote(parts.at[here], coming.at[q], rs_send.at[q], rs_recv.at[q], partner).wait_recv()
+            parts[here, :] = (parts[here, :].astype(f32) + coming[q].astype(f32)).astype(bf16)
+            for c in (1, 2):
+
+                @pl.when(col == c)
+                def _():
+                    sum_start(e, c)
+
+    def out_copies(tick):
+        copies = []
+        for h in range(2):
+            q = pick(
+                tick, [pick(col, [order[2 * t + h] for order in TICKS]) for t in range(LINE)]
+            )
+            copies.append(
+                pltpu.make_async_copy(
+                    stage.at[lax.rem(tick, 2), pl.ds(h * piece, piece)],
+                    out_part.at[slot_rows(q)],
+                    out_sem.at[lax.rem(tick, 2), h],
+                )
+            )
+        return copies
+
+    lane_tiles = [(k * 512, 512) for k in range(D // 512)]
+
+    @pl.loop(0, LINE)
+    def _(tick):
+        here = rows_at(tick * part, part)
+        for c in (0, LINE - 1):
+            for t in range(1, LINE):
+
+                @pl.when((col == c) & (tick == t))
+                def _():
+                    for h in range(2):
+                        got(c, TICKS[c][2 * t + h])
+
+        for h in range(2):
+            pltpu.make_async_copy(
+                cot_full.at[pl.ds(0, piece)],
+                cots.at[slot_rows(2 * tick + h)],
+                cot_sem.at[2 * tick + h],
+            ).wait()
+
+        for index, (first, count) in enumerate(tiles):
+
+            @pl.when(tick == 0)
+            def _():
+                for copy in load_copies(index, first, count):
+                    copy.wait()
+
+            rows_here, lanes = slice(first, first + count), slice(first, first + count)
+            gate = matmul_nt(n2s[here, :], gate_w[rows_here, :])
+            up = matmul_nt(n2s[here, :], up_w[rows_here, :])
+            grad = matmul_nt(cots[here, :], down_w[rows_here, :])
+            sigmoid = jax.nn.sigmoid(gate)
+            silu = gate * sigmoid
+            mixed[here, lanes] = (silu * up).astype(bf16)
+            g_gate[here, lanes] = (grad * up * sigmoid * (1.0 + gate * (1.0 - sigmoid))).astype(
+                bf16
+            )
+            g_up[here, lanes] = (grad * silu).astype(bf16)
+            if index == 2:
+
+                @pl.when(tick == 0)
+                def _():
+                    onward(0)
+
+                @pl.when(tick == 1)
+                def _():
+                    onward(2)
+
+                @pl.when(tick == 3)
+                def _():
+                    sum_mids(1)
+
+        for first, count in lane_tiles:
+            lanes = slice(first, first + count)
+            total = matmul(g_gate[here, :], gate_w[:, lanes])
+            total = total + matmul(g_up[here, :], up_w[:, lanes])
+            parts[here, lanes] = total.astype(bf16)
+
+        @pl.when(tick == 0)
+        def _():
+            onward(1)
+
+        @pl.when(tick == 1)
+        def _():
+            onward(3)
+            onward(4)
+            sum_ends(0)
+            sum_ends(1)
+
+        @pl.when(tick == 2)
+        def _():
+            sum_ends(2)
+            sum_ends(3)
+            sum_mids(0)
+
+        @pl.when(tick == 3)
+        def _():
+            sum_ends(4)
+            sum_ends(5)
+            sum_mids(2)
+            sum_mids(3)
+
+        @pl.when(tick >= 2)
+        def _():
+            for copy in out_copies(tick - 2):
+                copy.wait()
+
+        own = jnp.where(tick == 0, 1.0, 0.0)
+        for first, count in lane_tiles:
+            lanes = slice(first, first + count)
+            total = matmul(mixed[here, :], down_w[:, lanes]) + hid[:, lanes] * own
+            stage[lax.rem(tick, 2), :, lanes] = total.astype(bf16)
+        for copy in out_copies(tick):
+            copy.start()
+
+    pl.semaphore_signal(free_sem, inc=1, device_id=partner, device_id_type=MESH)
+    pl.semaphore_wait(free_sem, 1)
+    theirs, ours = lanes_at((1 - row) * half, half), lanes_at(row * half, half)
+    jobs = ((mixed, cots, down_w, sum_down), (g_gate, n2s, gate_w, sum_gate), (g_up, n2s, up_w, sum_up))
+    whole_tiles, tail = tiles[:-1], tiles[-1]
+    tile = tiles[0][1]
+
+    def swap_copy(k, index, rows_here):
+        buffer = jobs[k][2]
+        return remote(
+            buffer.at[rows_here, pl.ds(0, half)],
+            buffer.at[rows_here, pl.ds(half, half)],
+            swap_send.at[k, index],
+            swap_recv.at[k, index],
+            partner,
+        )
+
+    for k, (left, right, buffer, result) in enumerate(jobs):
+
+        def give(index, rows_here, lanes):
+            buffer[rows_here, :half] = matmul_tn(left[:, lanes], right[:, theirs]).astype(bf16)
+            swap_copy(k, index, rows_here).start()
+
+        def keep(index, rows_here, lanes):
+            total = matmul_tn(left[:, lanes], right[:, ours])
+            swap_copy(k, index, rows_here).wait_recv()
+            total = total + buffer[rows_here, half:].astype(f32)
+            buffer[rows_here, half:] = total.astype(bf16)
+
+        for act in (give, keep):
+
+            @pl.loop(0, len(whole_tiles))
+            def _(index):
+                first = index * tile
+                act(index, rows_at(first, tile), lanes_at(first, tile))
+
+            act(len(whole_tiles), pl.ds(*tail), pl.ds(*tail))
+        pltpu.make_async_copy(buffer.at[:, pl.ds(half, half)], result, sum_sem.at[k]).start()
+        if k == 0:
+            sum_mids(4)
+            sum_mids(5)
+        if k == 1:
+            for h in range(2):
+                for c in range(LINE):
+
+                    @pl.when(col == c)
+                    def _():
+                        for way in ways(c):
+                            place = 2 * c + h if way == 1 else 2 * LINE + h
+                            remote(
+                                coming.at[place],
+                                coming.at[place],
+                                rs_send.at[0],
+                                rs_recv.at[place],
+                                partner,
+                            ).wait_recv()
+
+            width = aux_all.shape[2]
+            squares = jnp.zeros((part, 1), f32)
+            inner = jnp.zeros((part, 1), f32)
+            for shard in range(LINE):
+                lanes = slice(shard * width, (shard + 1) * width)
+                middle = hid[:, lanes]
+                from_left = jnp.concatenate([coming[2 * col + h, :, lanes] for h in range(2)])
+                from_right = jnp.concatenate([coming[2 * LINE + h, :, lanes] for h in range(2)])
+                total = parts[:part, lanes].astype(f32) + from_left.astype(f32)
+                total = total + from_right.astype(f32)
+                grad_mid[:, lanes] = total
+                squares = squares + jnp.sum(middle * middle, axis=1, keepdims=True)
+                scaled = total * aux_all[shard, 1:2, :]
+                inner = inner + jnp.sum(scaled * middle, axis=1, keepdims=True)
+            inverse = lax.rsqrt(squares / D + eps)
+            factor = inverse * inverse * inverse * inner / D
+            for shard in range(LINE):
+                lanes = slice(shard * width, (shard + 1) * width)
+                middle, total = hid[:, lanes], grad_mid[:, lanes]
+                gain = jnp.sum(total * middle * inverse, axis=0, keepdims=True)
+                grad_gain[:, lanes] = jnp.broadcast_to(gain, (8, width))
+                grad_mid[:, lanes] = (
+                    cots[:part, lanes].astype(f32)
+                    + inverse * total * aux_all[shard, 1:2, :]
+                    - middle * factor
+                )
+
+    for k, (left, right, buffer, result) in enumerate(jobs):
+        for index, place in enumerate(tiles):
+            swap_copy(k, index, pl.ds(*place)).wait_send()
+        pltpu.make_async_copy(buffer.at[:, pl.ds(half, half)], result, sum_sem.at[k]).wait()
+    for tick in (LINE - 2, LINE - 1):
+        for copy in out_copies(tick):
+            copy.wait()
+    for c in range(LINE):
+
+        @pl.when(col == c)
+        def _():
+            for way in ways(c):
+                hand_on(c, way, 2 * c, n2.at[pl.ds(0, piece)]).wait_send()
+                if c in (0, LINE - 1):
+                    hand_on(c, way, 2 * c + 1, n2.at[pl.ds(piece, piece)]).wait_send()
+                for q in ONWARD[way][c]:
+                    hand_on(c, way, q).wait_send()
+            for q, way in SUMS[c]:
+                sum_copy(c, q, way).wait_send()
+
+
+def mlp(n2, cot_full, hid, aux_all, own, peer):
+    f32, bf16 = jnp.float32, jnp.bfloat16
+    rows = cot_full.shape[0]
+    part = n2.shape[0]
+    hidden, half = own[0].shape
+    shape = jax.ShapeDtypeStruct
+    dma = pltpu.SemaphoreType.DMA
+    outs = [(shape((rows, D), bf16), any_spec())]
+    outs += [(shape((hidden, half), bf16), any_spec())] * 3
+    outs += [(shape((part, D), f32), vmem_spec()), (shape((8, D), f32), vmem_spec())]
+    wide = pltpu.VMEM((hidden, D), bf16)
+    tall = pltpu.VMEM((rows, hidden), bf16)
+    full = pltpu.VMEM((rows, D), bf16)
+    return pl.pallas_call(
+        mlp_kernel,
+        out_shape=[o[0] for o in outs],
+        in_specs=[any_spec(), any_spec(), vmem_spec(), vmem_spec()] + [any_spec()] * 6,
+        out_specs=[o[1] for o in outs],
+        scratch_shapes=[
+            wide,
+            wide,
+            wide,
+            tall,
+            tall,
+            tall,
+            full,
+            full,
+            full,
+            pltpu.VMEM((2 * LINE + 2, part // 2, D), bf16),
+            pltpu.VMEM((2, part, D), bf16),
+            dma((len(hidden_tiles(hidden)), 6)),
+            dma((2 * LINE,)),
+            dma,
+            dma((2, 2 * LINE)),
+            dma((2 * LINE,)),
+            dma((2 * LINE,)),
+            dma((2 * LINE + 2,)),
+            dma((2, 2)),
+            dma((3,)),
+            pltpu.SemaphoreType.REGULAR,
+            dma((3, len(hidden_tiles(hidden)))),
+            dma((3, len(hidden_tiles(hidden)))),
+        ],
+        compiler_params=pltpu.CompilerParams(
+            collective_id=2, has_side_effects=True, vmem_limit_bytes=62 * 2**20
+        ),
+        cost_estimate=pl.CostEstimate(
+            flops=64 * 10**9, bytes_accessed=60 * 10**6, transcendentals=10**7
+        ),
+        name="mlp",
+    )(n2, cot_full, hid, aux_all, *own, *peer)
+
 
 def norm_rows(hidden, gain):
     inverse = lax.rsqrt(jnp.mean(hidden * hidden, axis=1, keepdims=True) + eps)
@@ -1023,19 +1486,13 @@
     (
         inputs_full, normed_one, cot_full, query_rot, seq_kv, attended_f32, lse, att_own, hidden_mid, normed_part, trig, aux_all, wall, wof, peer_gate, peer_up, peer_down,
     ) = front(
-        (col_count, lax.axis_size("dp")), aux, inputs, cotangent, w_query, own_kv, w_out, w_gate, w_up, w_down, seq_lengths, freq
+        (col_count, lax.axis_size("dp")), aux, inputs, cotangent, w_query, own_kv, w_out, w_gate.T, w_up.T, w_down, seq_lengths, freq
     )
     gain_one_full = aux_all[:, 0].reshape(D)
     gain_two_full = aux_all[:, 1].reshape(D)
     full_query = wall[:, : heads * HEAD_WIDTH]
     own_kv = lax.dynamic_slice_in_dim(wall, heads * HEAD_WIDTH + lax.rem(col_pos, 2) * HEAD_WIDTH, HEAD_WIDTH, 1)
 
-    def both(own, peer, axis):
-        return lax.cond(row_pos == 0, lambda: jnp.concatenate([own, peer], axis), lambda: jnp.concatenate([peer, own], axis))
-
-    full_gate = both(w_gate, peer_gate, 0)
-    full_up = both(w_up, peer_up, 0)
-    full_down = both(w_down, peer_down, 1)
     full_out = wof[col_pos]
     lengths = seq_lengths[0]
     place_local = row_pos * rows + jnp.arange(rows, dtype=jnp.int32)
@@ -1050,52 +1507,21 @@
     log_total = lse[:, :, 0].transpose(1, 0)[:, None]
     attended_cols = attended.reshape(rows, heads * HEAD_WIDTH).astype(bf16)
     start = col_pos * part
-    inverse_two = norm_rows(hidden_mid, gain_two_full)[1]
-    normed_two = lax.all_gather(normed_part, "col", axis=0, tiled=True)
-
-    gate = matmul(normed_two, full_gate)
-    up_proj = matmul(normed_two, full_up)
-    sigmoid_gate = jax.nn.sigmoid(gate)
-    silu_gate = gate * sigmoid_gate
-    mixed = (silu_gate * up_proj).astype(bf16)
-    grad_mixed = matmul_nt(cot_full, full_down)
-    grad_gate = (grad_mixed * up_proj * sigmoid_gate * (1.0 + gate * (1.0 - sigmoid_gate))).astype(
-        bf16
-    )
-    grad_up = (grad_mixed * silu_gate).astype(bf16)
-    grad_normed_two = lax.psum_scatter(
-        (matmul_nt(grad_gate, full_gate) + matmul_nt(grad_up, full_up)).astype(bf16),
-        "col",
-        scatter_dimension=0,
-        tiled=True,
-    ).astype(f32)
+    out_part, sum_down, sum_gate, sum_up, grad_mid, grad_gain_two = mlp(
+        normed_part,
+        cot_full,
+        hidden_mid,
+        aux_all,
+        (w_gate.T, w_up.T, w_down),
+        (peer_gate, peer_up, peer_down),
+    )
+    grad_gain_two = grad_gain_two[0]
+    result = lax.psum_scatter(out_part, "col", scatter_dimension=1, tiled=True)
+    wide_sums = lax.psum((sum_down, sum_gate, sum_up), "dp")
 
     def row_sum(grad, dim):
         return lax.psum_scatter(grad.astype(bf16), "row", scatter_dimension=dim, tiled=True)
 
-    out_partial = matmul(mixed, full_down)
-    out_partial = lax.dynamic_update_slice_in_dim(
-        out_partial, lax.dynamic_slice_in_dim(out_partial, start, part, 0) + hidden_mid, start, 0
-    )
-    result = lax.psum_scatter(out_partial.astype(bf16), "col", scatter_dimension=1, tiled=True)
-
-    wide_sums = lax.psum(
-        (
-            row_sum(matmul_tn(mixed, cot_full), 1),
-            row_sum(matmul_tn(normed_two, grad_gate), 0),
-            row_sum(matmul_tn(normed_two, grad_up), 0),
-        ),
-        "dp",
-    )
-
-    scaled = grad_normed_two * gain_two_full[None, :]
-    inner = jnp.sum(scaled * hidden_mid, axis=1, keepdims=True)
-    grad_gain_two = jnp.sum(grad_normed_two * hidden_mid * inverse_two, axis=0)
-    grad_mid = (
-        lax.dynamic_slice_in_dim(cot_full, start, part, 0).astype(f32)
-        + inverse_two * scaled
-        - hidden_mid * (inverse_two * inverse_two * inverse_two * inner / D)
-    )
     grad_mid_full = lax.all_gather(grad_mid.astype(bf16), "col", axis=0, tiled=True)
     grad_attended = matmul_nt(grad_mid_full, full_out).astype(bf16)
     grad_query_rot, key_grads, value_grads = attention_backward(
@@ -1138,6 +1564,7 @@
         g.astype(f32) for g in lax.psum((grad_w_out, grad_w_query, grad_w_kv), "dp")
     )
     grad_w_down, grad_w_gate, grad_w_up = (g.astype(f32) for g in wide_sums)
+    grad_w_gate, grad_w_up = grad_w_gate.T, grad_w_up.T
     grad_b_query = jnp.sum(query_grad_cols.astype(f32), axis=0)
     grad_b_kv = jnp.sum(kv_grad_cols.astype(f32), axis=0)
     grad_normed_one = matmul_nt(query_grad_cols, full_query) + matmul_nt(kv_grad_cols, own_kv)

time: 1070 us -> 742 us (0.69)
  waiting for transfers between devices: 561 us -> 288 us
  matrix products: 185 us -> 69.2 us
  Pallas kernels: 148 us -> 261 us
  other arithmetic: 67.3 us -> 33.9 us
  local copies, waits for them, and re-layouts: 71.6 us -> 51.1 us
    unnamed x19 -> x14, waiting for transfers between devices: 133 us -> 1.26 us
    pallas_call x0 -> x1, Pallas kernels: none -> 114 us  [mlp(): pl.pallas_call(mlp_kernel, out_shape=[o[0] for o in outs], in_specs=[any_...]
    reduce_scatter x1 -> x0, waiting for transfers between devices: 58.7 us -> none  [per_device(): lax.psum_scatter((matmul_nt(grad_gate, full_gate) + matmul_nt(grad_up, fu...]
    dot_general x6 -> x3, matrix products: 53.9 us -> 9.65 us  [matmul_nt(): lax.dot_general(left, right, (((1,), (1,)), ((), ())), preferred_element_...]
    dot_general x3 -> x0, matrix products: 38.7 us -> none  [matmul(): return jnp.dot(left, right, preferred_element_type=jnp.float32)]
    dot_general x6 -> x3, matrix products: 45.2 us -> 10.3 us  [matmul_tn(): lax.dot_general(left, right, (((0,), (0,)), ((), ())), preferred_element_...]
    all_gather x1 -> x0, waiting for transfers between devices: 31.9 us -> none  [per_device(): normed_two = lax.all_gather(normed_part, 'col', axis=0, tiled=True)]
    psum x1, waiting for transfers between devices: 48.4 us -> 22.5 us  [per_device(): lax.psum((grad_w_out, grad_w_query, grad_w_kv), 'dp')]
  transfers between devices with their start and end apart: 16 -> 11, of which waited for: 11 -> 8; matrix products, arithmetic and copies ran while one was open for 14% -> 8% of each run, Pallas kernels for 0% -> 0%
where the time goes in v3:
time: 742 us; the launch traced here: 735 us
  waiting for transfers between devices  288 us (39%)
  Pallas kernels  261 us (35%)
  matrix products  69.2 us (9%)
  local copies, waits for them, and re-layouts  51.1 us (7%)
  other arithmetic  33.9 us (5%)
  between operations  16.2 us (2%)
  blocking collectives  13.6 us (2%)
    psum x1, waiting for transfers between devices, per_device(): wide_sums = lax.psum((sum_down, sum_gate, sum_up), 'dp')  176 us
    pallas_call x1, Pallas kernels, front(): pl.pallas_call(functools.partial(front_kernel, heads, dims), out_shape=[o...  147 us
    pallas_call x1, Pallas kernels, mlp(): pl.pallas_call(mlp_kernel, out_shape=[o[0] for o in outs], in_specs=[any_...  114 us
    all_gather x1, waiting for transfers between devices, per_device(): lax.all_gather(grad_mid.astype(bf16), 'col', axis=0, tiled=True)  60.4 us
    unnamed x53, local copies, waits for them, and re-layouts  26 us
    psum x1, waiting for transfers between devices, per_device(): lax.psum((grad_w_out, grad_w_query, grad_w_kv), 'dp')  22.5 us
    reduce_scatter x3, waiting for transfers between devices, row_sum(): lax.psum_scatter(grad.astype(bf16), 'row', scatter_dimension=dim, tiled=T...  16.7 us
  transfers between devices with their start and end apart: 11, of which 8 were waited for; matrix products, arithmetic and copies ran while one was open for 8% of the time, Pallas kernels for 0%

profile of v3, /device:TPU:0, one launch (start us, length us, event | category | flops | bytes accessed | tf_op | source)
XLA Modules:
  0.0 734.8 jit_solution(754438150129879945)
XLA Ops:
  16.0 147.5 %front.1 = (bf16[1024,1536]{1,0:T(8,128)(2,1)}, bf16[1024,1536]{1,0:T(8,128)(2,1)}, bf16[1024,1536]{1,0:T(8,128)(2,1)}, bf16[3,1024,128]{2,1,0:T(8,128)(2,1)S(1)...) custom-call(f32[8,384]{1,0:T(8,128)S(1)} %select_maximum_fusion.aux,, ...), custom_call_target="tpu_custom_call" | custom-call | flops 10000000000 | bytes 60000000 | tf_op jit(solution)/shard_map/front/pallas_call | solution.py:936
  164.1 113.8 %mlp.1 = (bf16[1024,1536]{1,0:T(8,128)(2,1)}, bf16[2240,768]{1,0:T(8,128)(2,1)}, bf16[2240,768]{1,0:T(8,128)(2,1)}, bf16[2240,768]{1,0:T(8,128)(2,1)}, f32[256,1536]{1,0:T(8,128)}, /*index=5*/f32[8,1536]{1,0:T(8,128)}) custom-call(bf16[256,1536]{1,0:T(8,128)(2,1)} %get-tuple-element.115.n2, bf16[1024,1536]{1,0:T(8,128)(2,1)} %get-tuple-element.116.cot_full, ...), custom_call_target="tpu_custom_call" | custom-call | flops 64000000000 | bytes 60000000 | tf_op jit(solution)/shard_map/mlp/pallas_call | solution.py:1402
  283.7 60.4 %all-gather.2.cloned.1.call-done = bf16[1024,1536]{1,0:T(8,128)(2,1)} async-done(((bf16[256,1536]{1,0:T(8,128)(2,1)}), bf16[1024,1536]{1,0:T(8,128)(2,1)}) %all-gather.2.cloned.1.call-update) | async-done | bytes 3145744 | tf_op jit(solution)/shard_map/all_gather | solution.py:1525
  344.1 3.6 convolution_convert_fusion.3
  352.7 62.8 %while.15 = (s32[]{:T(128)}, f32[1024,1,3,128]{0,3,2,1:T(8,128)}, bf16[4,512,1,128]{3,1,2,0:T(8,128)(2,1)}, bf16[4,512,1,128]{3,1,2,0:T(8,128)(2,1)}, bf16[4,512...) while((s32[]{:T(128)}, f32[1024,1,3,128]{0,3,2,1:T(8,128)}, ...), condition=%wide.region_7.8_spmd.clone, body=%wide.region_6.7_spmd.clone.sunk | while | flops 2031813632 | bytes 108460496 | solution.py:190
  357.2 3.1 fusion.106
  360.3 2.9 bitcast_add_fusion.2
  363.2 2.9 fusion.107
  372.4 3.1 fusion.106
  375.6 3.4 bitcast_add_fusion.2
  379.0 2.9 fusion.107
  388.2 3.1 fusion.106
  391.4 3.4 bitcast_add_fusion.2
  394.8 2.9 fusion.107
  404.0 3.1 fusion.106
  407.1 3.4 bitcast_add_fusion.2
  410.6 2.9 fusion.107
  419.3 7.2 reduce-scatter.15.cloned.1.call-done
  432.1 2.9 convolution_convert_fusion
  436.6 4.7 convolution_convert_fusion.1
  441.4 4.2 reduce-scatter.17.cloned.1.call-done
  450.3 2.8 copy.85
  459.1 4.2 fusion.39
  464.6 5.0 reduce-scatter.19.cloned.1.call-done
  469.5 11.7 %reduce-scatter.23.cloned.1.call-done = bf16[768,128]{1,0:T(8,128)(2,1)} async-done(((bf16[1536,128]{1,0:T(8,128)(2,1)}), bf16[768,128]{1,0:T(8,128)(2,1)}) %reduce-scatter.23.cloned.1.call-update) | async-done | bytes 196624 | tf_op jit(solution)/shard_map/reduce_scatter | solution.py:1523
  481.2 175.9 %all-reduce.9.cloned.1.call-done = (bf16[2240,768]{1,0:T(8,128)(2,1)}, bf16[2240,768]{1,0:T(8,128)(2,1)}, bf16[2240,768]{1,0:T(8,128)(2,1)}) async-done(((bf16[2240,768]{1,0:T(8,128)(2,1)}, bf16[2240,768]{1,0:T(8,128)(2,1)}, bf16[2240,768]{1,0:T(8,128)(2,1)}), (bf16[2240,768]{1,0:T(8,128)(2,1)}, bf16[2240,768]{1,0:T(8,128)(2,1)}, bf16[2240,768]{1,0:T(8,128)(2,1)})) %all-reduce.9.cloned.1.call-update) | async-done | bytes 10321936 | tf_op jit(solution)/shard_map/psum | solution.py:1520
  657.2 3.6 fusion.37
  661.6 2.9 copy.87
  669.1 13.6 %psum.49 = f32[1280]{0:T(1024)S(1)} all-reduce(f32[1280]{0:T(1024)S(1)} %pad_maximum_fusion.5), channel_id=1, replica_groups=mesh['dp'=4,'row'=2,'col'=4] {'dp','row'}, use_global_device_ids=true, to_apply=%region_17.18 | all-reduce | flops 1280 | bytes 10240 | tf_op jit(solution)/shard_map/psum | solution.py:1586
  683.9 4.1 convert_element_type.116
  689.5 6.2 convert_bitcast_fusion
  695.7 22.5 %all-reduce.7.cloned.1.call-done = (bf16[768,128]{1,0:T(8,128)(2,1)}, bf16[768,384]{1,0:T(8,128)(2,1)}, bf16[384,768]{1,0:T(8,128)(2,1)}) async-done(((bf16[768,128]{1,0:T(8,128)(2,1)}, bf16[768,384]{1,0:T(8,128)(2,1)}, bf16[384,768]{1,0:T(8,128)(2,1)}), (bf16[768,128]{1,0:T(8,128)(2,1)}, bf16[768,384]{1,0:T(8,128)(2,1)}, bf16[384,768]{1,0:T(8,128)(2,1)})) %all-reduce.7.cloned.1.call-update) | async-done | bytes 1376272 | tf_op jit(solution)/shard_map/psum | solution.py:1564
  (236 shorter events, 84.0 us)
Async XLA Ops:
  8.0 336.1 %all-gather.2.cloned.1.call-start = ((), (), s32[]{:S(2)}) async-start(), calls=%async_computation.8 | async-start | bytes 3932160 | tf_op jit(solution)/shard_map/all_gather | solution.py:1525
  278.0 4.9 copy-start.28
  280.5 146.0 %reduce-scatter.15.cloned.1.call-start = ((), (), s32[]{:S(2)}) async-start(), calls=%async_computation.9 | async-start | bytes 1572864 | tf_op jit(solution)/shard_map/reduce_scatter | solution.py:1537
  353.5 3.7 copy-start.29
  360.3 5.8 copy-start.6
  363.2 2.9 copy-start.30
  368.7 3.7 copy-start.29
  375.6 6.3 copy-start.6
  379.0 2.9 copy-start.30
  384.5 3.7 copy-start.29
  391.3 6.3 copy-start.6
  394.8 2.9 copy-start.30
  400.3 3.7 copy-start.29
  407.1 6.3 copy-start.6
  410.6 2.9 copy-start.30
  419.1 11.6 %copy-start.9 = (f32[1024,1,3,128]{0,3,2,1:T(8,128)S(1)}, f32[1024,1,3,128]{0,3,2,1:T(8,128)}, u32[]{:S(2)}) copy-start(f32[1024,1,3,128]{0,3,2,1:T(8,128)} %get-tuple-element.130) | copy-start | bytes 4718596
  419.1 26.4 %reduce-scatter.17.cloned.1.call-start = ((), (), s32[]{:S(2)}) async-start(), calls=%async_computation.10 | async-start | bytes 786432 | tf_op jit(solution)/shard_map/reduce_scatter | solution.py:1548
  429.7 34.9 %reduce-scatter.21.cloned.1.call-start = ((), (), s32[]{:S(2)}) async-start(), calls=%async_computation.12 | async-start | bytes 1769472 | tf_op jit(solution)/shard_map/reduce_scatter | solution.py:1523
  432.1 3.2 copy-start.16
  435.0 34.6 %reduce-scatter.19.cloned.1.call-start = ((), (), s32[]{:S(2)}) async-start(), calls=%async_computation.11 | async-start | bytes 1769472 | tf_op jit(solution)/shard_map/reduce_scatter | solution.py:1523
  436.6 9.0 %copy-start.18 = (bf16[1024,1536]{1,0:T(8,128)(2,1)S(1)}, bf16[1024,1536]{1,0:T(8,128)(2,1)}, u32[]{:S(2)}) copy-start(bf16[1024,1536]{1,0:T(8,128)(2,1)} %get-tuple-element.135) | copy-start | bytes 9437188
  441.3 39.9 %reduce-scatter.23.cloned.1.call-start = ((), (), s32[]{:S(2)}) async-start(), calls=%async_computation.13 | async-start | bytes 589824 | tf_op jit(solution)/shard_map/reduce_scatter | solution.py:1523
  448.3 208.8 %all-reduce.9.cloned.1.call-start = ((), (), s32[]{:S(2)}) async-start(), calls=%async_computation.18 | async-start | bytes 20643840 | tf_op jit(solution)/shard_map/psum | solution.py:1520
  448.9 215.6 %reduce-scatter.25.cloned.1.call-start = ((), (), s32[]{:S(2)}) async-start(), calls=%async_computation.14 | async-start | bytes 3932160
  453.1 214.9 %reduce-scatter.29.cloned.1.call-start = ((), (), s32[]{:S(2)}) async-start(), calls=%async_computation.16 | async-start | bytes 983040
  464.5 253.7 %all-reduce.7.cloned.1.call-start = ((), (), s32[]{:S(2)}) async-start(), calls=%async_computation.17 | async-start | bytes 2752512 | tf_op jit(solution)/shard_map/psum | solution.py:1564
  657.2 67.7 %reduce-scatter.27.cloned.1.call-start = ((), (), s32[]{:S(2)}) async-start(), calls=%async_computation.15 | async-start | bytes 3932160
  657.2 3.6 copy-start.15
  664.5 19.4 %copy-start.23 = (bf16[2240,768]{1,0:T(8,128)(2,1)S(1)}, bf16[2240,768]{1,0:T(8,128)(2,1)}, u32[]{:S(2)}) copy-start(bf16[2240,768]{1,0:T(8,128)(2,1)} %get-tuple-element.144) | copy-start | bytes 10321924
  683.9 4.1 copy-start.21
  683.9 5.6 copy-start.22
  718.2 4.4 copy-start.25
  (40 other events, 74.0 us)
Sparse Core Ops, SparseCore 0:
  280.6 63.5 all-gather.1
  419.2 7.1 reduce-scatter.14
  429.8 15.7 reduce-scatter.16
  448.2 8.6 reduce-scatter.20
  459.7 9.8 reduce-scatter.18
  472.2 8.9 reduce-scatter.22
  484.2 61.3 reduce-scatter.24
  548.6 23.3 reduce-scatter.28
  664.6 60.2 reduce-scatter.26
Sparse Core Ops, SparseCore 1:
  453.2 203.9 all-reduce.8
  660.4 57.8 all-reduce.6

commit v4 on v3

--- a/solution.py
+++ b/solution.py
@@ -545,6 +545,7 @@
     hid_out,
     n2_out,
     trig_out,
+    att_low,
     aux_out,
     wall_out,
     wof_out,
@@ -554,7 +555,6 @@
     x_full,
     n1,
     cot_full,
-    att_low,
     x_send,
     x_recv,
     c_send,
@@ -820,7 +820,10 @@
         attended = (acc / total).reshape(heads, part, HEAD_WIDTH)
         att_out[:, here, :] = attended
         log_total = (largest + jnp.log(total)).reshape(heads, part, 1)
-        lse_out[:, here, :] = jnp.broadcast_to(log_total, (heads, part, HEAD_WIDTH))
+        spread = jnp.zeros((part, HEAD_WIDTH), f32)
+        for head in range(heads):
+            spread = jnp.where(lane == head, log_total[head], spread)
+        lse_out[here, :] = spread
         for head in range(heads):
             lanes = slice(head * HEAD_WIDTH, (head + 1) * HEAD_WIDTH)
             att_low[block, :, lanes] = attended[head].astype(bf16)
@@ -920,11 +923,12 @@
         (shape((heads, rows, HEAD_WIDTH), bf16), vmem_spec()),
         (shape((2 * rows, 2 * HEAD_WIDTH), bf16), vmem_spec()),
         (shape((heads, rows, HEAD_WIDTH), f32), vmem_spec()),
-        (shape((heads, rows, HEAD_WIDTH), f32), vmem_spec()),
+        (shape((rows, HEAD_WIDTH), f32), vmem_spec()),
         (shape((part, D), bf16), vmem_spec()),
         (shape((part, D), f32), vmem_spec()),
         (shape((part, D), bf16), vmem_spec()),
         (shape((2, rows, HEAD_WIDTH), f32), vmem_spec()),
+        (shape((count, part, width), bf16), vmem_spec()),
         (shape((count,) + aux.shape, f32), vmem_spec()),
         (shape((D, wall), bf16), vmem_spec()),
         (shape((count, wout.shape[0], D), bf16), vmem_spec()),
@@ -944,7 +948,6 @@
             pltpu.VMEM((rows, D), bf16),
             pltpu.VMEM((rows, D), bf16),
             pltpu.VMEM((rows, D), bf16),
-            pltpu.VMEM((count, part, width), bf16),
             dma((2, count - 1, count)),
             dma((count, count)),
             dma((2, count - 1, count)),
@@ -975,6 +978,8 @@
         ),
         name="front",
     )(aux, x, cot, wq, wkv, wout, w_gate, w_up, w_down, lengths, freq)
+
+
 TICKS = ((0, 1, 2, 4, 6, 7, 5, 3), (2, 3, 0, 4, 1, 6, 7, 5), (4, 5, 6, 2, 7, 0, 1, 3), (6, 7, 4, 2, 0, 1, 3, 5))
 SLOTS = tuple(tuple(order.index(q) for q in range(8)) for order in TICKS)
 ONWARD = (
@@ -988,6 +993,7 @@
     ((4, 1), (2, 1), (0, 1), (1, 1), (3, 1), (5, 1)),
 )
 LINE = 4
+TILE = 768
 
 
 def pick(index, values):
@@ -1014,9 +1020,8 @@
     peer_up,
     peer_down,
     out_part,
-    sum_down,
-    sum_gate,
-    sum_up,
+    left_out,
+    right_out,
     grad_mid,
     grad_gain,
     gate_w,
@@ -1038,10 +1043,8 @@
     rs_send,
     rs_recv,
     out_sem,
-    sum_sem,
-    free_sem,
-    swap_send,
-    swap_recv,
+    left_sem,
+    right_sem,
 ):
     f32, bf16 = jnp.float32, jnp.bfloat16
     dp, row, col = lax.axis_index("dp"), lax.axis_index("row"), lax.axis_index("col")
@@ -1122,6 +1125,8 @@
             coming[2 * LINE + h] = jnp.zeros(coming.shape[1:], bf16)
 
     own_copy.wait()
+    for ref in (mixed, g_gate, g_up):
+        ref[:, hidden:] = jnp.zeros((ref.shape[0], ref.shape[1] - hidden), bf16)
 
     def onward(f):
         for c in (1, 2):
@@ -1186,6 +1191,16 @@
             )
         return copies
 
+    def left_copies(tick):
+        here = rows_at(tick * part, part)
+        return [
+            pltpu.make_async_copy(ref.at[here], left_out.at[k, here], left_sem.at[tick, k])
+            for k, ref in enumerate((mixed, g_gate, g_up))
+        ]
+
+    def right_copy(slot):
+        return pltpu.make_async_copy((cots, n2s)[slot], right_out.at[slot], right_sem.at[slot])
+
     lane_tiles = [(k * 512, 512) for k in range(D // 512)]
 
     @pl.loop(0, LINE)
@@ -1238,10 +1253,12 @@
                 def _():
                     sum_mids(1)
 
+        for copy in left_copies(tick):
+            copy.start()
         for first, count in lane_tiles:
             lanes = slice(first, first + count)
-            total = matmul(g_gate[here, :], gate_w[:, lanes])
-            total = total + matmul(g_up[here, :], up_w[:, lanes])
+            total = matmul(g_gate[here, :hidden], gate_w[:, lanes])
+            total = total + matmul(g_up[here, :hidden], up_w[:, lanes])
             parts[here, lanes] = total.astype(bf16)
 
         @pl.when(tick == 0)
@@ -1276,99 +1293,66 @@
         own = jnp.where(tick == 0, 1.0, 0.0)
         for first, count in lane_tiles:
             lanes = slice(first, first + count)
-            total = matmul(mixed[here, :], down_w[:, lanes]) + hid[:, lanes] * own
+            total = matmul(mixed[here, :hidden], down_w[:, lanes]) + hid[:, lanes] * own
             stage[lax.rem(tick, 2), :, lanes] = total.astype(bf16)
         for copy in out_copies(tick):
             copy.start()
 
-    pl.semaphore_signal(free_sem, inc=1, device_id=partner, device_id_type=MESH)
-    pl.semaphore_wait(free_sem, 1)
-    theirs, ours = lanes_at((1 - row) * half, half), lanes_at(row * half, half)
-    jobs = ((mixed, cots, down_w, sum_down), (g_gate, n2s, gate_w, sum_gate), (g_up, n2s, up_w, sum_up))
-    whole_tiles, tail = tiles[:-1], tiles[-1]
-    tile = tiles[0][1]
-
-    def swap_copy(k, index, rows_here):
-        buffer = jobs[k][2]
-        return remote(
-            buffer.at[rows_here, pl.ds(0, half)],
-            buffer.at[rows_here, pl.ds(half, half)],
-            swap_send.at[k, index],
-            swap_recv.at[k, index],
-            partner,
-        )
-
-    for k, (left, right, buffer, result) in enumerate(jobs):
-
-        def give(index, rows_here, lanes):
-            buffer[rows_here, :half] = matmul_tn(left[:, lanes], right[:, theirs]).astype(bf16)
-            swap_copy(k, index, rows_here).start()
-
-        def keep(index, rows_here, lanes):
-            total = matmul_tn(left[:, lanes], right[:, ours])
-            swap_copy(k, index, rows_here).wait_recv()
-            total = total + buffer[rows_here, half:].astype(f32)
-            buffer[rows_here, half:] = total.astype(bf16)
-
-        for act in (give, keep):
-
-            @pl.loop(0, len(whole_tiles))
-            def _(index):
-                first = index * tile
-                act(index, rows_at(first, tile), lanes_at(first, tile))
-
-            act(len(whole_tiles), pl.ds(*tail), pl.ds(*tail))
-        pltpu.make_async_copy(buffer.at[:, pl.ds(half, half)], result, sum_sem.at[k]).start()
-        if k == 0:
-            sum_mids(4)
-            sum_mids(5)
-        if k == 1:
-            for h in range(2):
-                for c in range(LINE):
-
-                    @pl.when(col == c)
-                    def _():
-                        for way in ways(c):
-                            place = 2 * c + h if way == 1 else 2 * LINE + h
-                            remote(
-                                coming.at[place],
-                                coming.at[place],
-                                rs_send.at[0],
-                                rs_recv.at[place],
-                                partner,
-                            ).wait_recv()
-
-            width = aux_all.shape[2]
-            squares = jnp.zeros((part, 1), f32)
-            inner = jnp.zeros((part, 1), f32)
-            for shard in range(LINE):
-                lanes = slice(shard * width, (shard + 1) * width)
-                middle = hid[:, lanes]
-                from_left = jnp.concatenate([coming[2 * col + h, :, lanes] for h in range(2)])
-                from_right = jnp.concatenate([coming[2 * LINE + h, :, lanes] for h in range(2)])
-                total = parts[:part, lanes].astype(f32) + from_left.astype(f32)
-                total = total + from_right.astype(f32)
-                grad_mid[:, lanes] = total
-                squares = squares + jnp.sum(middle * middle, axis=1, keepdims=True)
-                scaled = total * aux_all[shard, 1:2, :]
-                inner = inner + jnp.sum(scaled * middle, axis=1, keepdims=True)
-            inverse = lax.rsqrt(squares / D + eps)
-            factor = inverse * inverse * inverse * inner / D
-            for shard in range(LINE):
-                lanes = slice(shard * width, (shard + 1) * width)
-                middle, total = hid[:, lanes], grad_mid[:, lanes]
-                gain = jnp.sum(total * middle * inverse, axis=0, keepdims=True)
-                grad_gain[:, lanes] = jnp.broadcast_to(gain, (8, width))
-                grad_mid[:, lanes] = (
-                    cots[:part, lanes].astype(f32)
-                    + inverse * total * aux_all[shard, 1:2, :]
-                    - middle * factor
-                )
-
-    for k, (left, right, buffer, result) in enumerate(jobs):
-        for index, place in enumerate(tiles):
-            swap_copy(k, index, pl.ds(*place)).wait_send()
-        pltpu.make_async_copy(buffer.at[:, pl.ds(half, half)], result, sum_sem.at[k]).wait()
+    for slot in range(2):
+        right_copy(slot).start()
+    sum_mids(4)
+    sum_mids(5)
+
+    for h in range(2):
+        for c in range(LINE):
+
+            @pl.when(col == c)
+            def _():
+                for way in ways(c):
+                    place = 2 * c + h if way == 1 else 2 * LINE + h
+                    remote(
+                        coming.at[place],
+                        coming.at[place],
+                        rs_send.at[0],
+                        rs_recv.at[place],
+                        partner,
+                    ).wait_recv()
+
+    width = aux_all.shape[2]
+    squares = jnp.zeros((part, 1), f32)
+    inner = jnp.zeros((part, 1), f32)
+    for shard in range(LINE):
+        lanes = slice(shard * width, (shard + 1) * width)
+        middle = hid[:, lanes]
+        from_left = jnp.concatenate([coming[2 * col + h, :, lanes] for h in range(2)])
+        from_right = jnp.concatenate([coming[2 * LINE + h, :, lanes] for h in range(2)])
+        total = parts[:part, lanes].astype(f32) + from_left.astype(f32)
+        total = total + from_right.astype(f32)
+        grad_mid[:, lanes] = total
+        squares = squares + jnp.sum(middle * middle, axis=1, keepdims=True)
+        scaled = total * aux_all[shard, 1:2, :]
+        inner = inner + jnp.sum(scaled * middle, axis=1, keepdims=True)
+    inverse = lax.rsqrt(squares / D + eps)
+    factor = inverse * inverse * inverse * inner / D
+    for shard in range(LINE):
+        lanes = slice(shard * width, (shard + 1) * width)
+        middle, total = hid[:, lanes], grad_mid[:, lanes]
+        gain = jnp.sum(total * middle * inverse, axis=0, keepdims=True)
+        grad_gain[:, lanes] = jnp.broadcast_to(gain, (8, width))
+        grad_mid[:, lanes] = (
+            cots[:part, lanes].astype(f32)
+            + inverse * total * aux_all[shard, 1:2, :]
+            - middle * factor
+        )
+
+    for slot in range(2):
+        right_copy(slot).wait()
+
+    @pl.loop(0, LINE)
+    def _(tick):
+        for copy in left_copies(tick):
+            copy.wait()
+
     for tick in (LINE - 2, LINE - 1):
         for copy in out_copies(tick):
             copy.wait()
@@ -1394,10 +1378,12 @@
     shape = jax.ShapeDtypeStruct
     dma = pltpu.SemaphoreType.DMA
     outs = [(shape((rows, D), bf16), any_spec())]
-    outs += [(shape((hidden, half), bf16), any_spec())] * 3
+    padded = -(-hidden // TILE) * TILE
+    outs += [(shape((3, rows, padded), bf16), any_spec())]
+    outs += [(shape((2, rows, D), bf16), any_spec())]
     outs += [(shape((part, D), f32), vmem_spec()), (shape((8, D), f32), vmem_spec())]
     wide = pltpu.VMEM((hidden, D), bf16)
-    tall = pltpu.VMEM((rows, hidden), bf16)
+    tall = pltpu.VMEM((rows, padded), bf16)
     full = pltpu.VMEM((rows, D), bf16)
     return pl.pallas_call(
         mlp_kernel,
@@ -1424,10 +1410,8 @@
             dma((2 * LINE,)),
             dma((2 * LINE + 2,)),
             dma((2, 2)),
-            dma((3,)),
-            pltpu.SemaphoreType.REGULAR,
-            dma((3, len(hidden_tiles(hidden)))),
-            dma((3, len(hidden_tiles(hidden)))),
+            dma((LINE, 3)),
+            dma((2,)),
         ],
         compiler_params=pltpu.CompilerParams(
             collective_id=2, has_side_effects=True, vmem_limit_bytes=62 * 2**20
@@ -1439,9 +1423,763 @@
     )(n2, cot_full, hid, aux_all, *own, *peer)
 
 
-def norm_rows(hidden, gain):
-    inverse = lax.rsqrt(jnp.mean(hidden * hidden, axis=1, keepdims=True) + eps)
-    return ((hidden * inverse * gain[None, :]).astype(jnp.bfloat16), inverse)
+CHUNK = 320
+TAIL = 960
+LAG = 2
+RING = 12
+
+
+class AllReduce:
+    def __init__(self, place, total, inbox, sends, recvs, result, own_sems, chunks):
+        self.dp, self.row, self.col = place
+        self.total, self.inbox, self.sends, self.recvs = total, inbox, sends, recvs
+        self.result, self.own_sems, self.chunks = result, own_sems, chunks
+        x, y = lax.rem(self.dp, 2), self.dp // 2
+        over_x = (self.dp + 1 - 2 * x, self.row, self.col)
+        over_y = (self.dp + 2 - 4 * y, self.row, self.col)
+        lanes = total.shape[1] // 2
+        self.kinds = (
+            (pl.ds(0, lanes), x, over_x, y, over_y),
+            (pl.ds(lanes, lanes), y, over_y, x, over_x),
+        )
+
+    def part(self, ref, first, count, kind):
+        return ref.at[rows_at(first, count), self.kinds[kind][0]]
+
+    def places(self, chunk, kind):
+        half, quarter = CHUNK // 2, CHUNK // 4
+        _, bit1, peer1, bit2, peer2 = self.kinds[kind]
+        own_half, far_half = chunk * CHUNK + half * bit1, chunk * CHUNK + half * (1 - bit1)
+        box = lax.rem(chunk, RING) * (half + quarter)
+        return (
+            (own_half, far_half, box, box + half)
+            + (own_half + quarter * bit2, own_half + quarter * (1 - bit2))
+            + (far_half + quarter * bit2, far_half + quarter * (1 - bit2))
+            + (peer1, peer2)
+        )
+
+    def copy(self, chunk, kind, stage, leaving):
+        half, quarter = CHUNK // 2, CHUNK // 4
+        _, far_half, box1, box2, own, mate, far, far_mate, peer1, peer2 = self.places(chunk, kind)
+        count = quarter if stage else half
+        if stage < 2:
+            src = self.part(self.total, (far_half, mate)[stage], count, kind)
+            dst = self.part(self.inbox, (box1, box2)[stage], count, kind)
+        else:
+            held = self.total if stage < 4 else self.result
+            src = self.part(held, mate if stage == 4 else own, count, kind)
+            if leaving:
+                dst = self.part(self.result, mate if stage == 4 else own, count, kind)
+            else:
+                dst = self.part(self.result, (mate, far, far_mate)[stage - 2], count, kind)
+        slot = lax.rem(chunk, RING)
+        return remote(
+            src,
+            dst,
+            self.sends.at[slot, kind, stage],
+            self.recvs.at[slot, kind, stage],
+            peer2 if stage in (1, 2) else peer1,
+        )
+
+    def own_copy(self, chunk, kind):
+        own = self.places(chunk, kind)[4]
+        return pltpu.make_async_copy(
+            self.part(self.total, own, CHUNK // 4, kind),
+            self.part(self.result, own, CHUNK // 4, kind),
+            self.own_sems.at[lax.rem(chunk, RING), kind],
+        )
+
+    def add(self, chunk, kind, stage):
+        self.copy(chunk, kind, stage, False).wait_recv()
+        own_half, _, box1, box2, own, *_ = self.places(chunk, kind)
+        count = CHUNK // 4 if stage else CHUNK // 2
+        lanes = self.kinds[kind][0]
+        mine = rows_at(own if stage else own_half, count)
+        coming = self.inbox[rows_at(box2 if stage else box1, count), lanes].astype(jnp.float32)
+        self.total[mine, lanes] = (
+            self.total[mine, lanes].astype(jnp.float32) + coming
+        ).astype(jnp.bfloat16)
+
+    def step(self, number):
+        for stage in range(5):
+
+            @pl.when((number - stage * LAG >= 0) & (number - stage * LAG < self.chunks))
+            def _():
+                chunk = number - stage * LAG
+                for kind in range(2):
+                    if stage == 0:
+                        self.copy(chunk, kind, 0, True).start()
+                    elif stage == 1:
+                        self.add(chunk, kind, 0)
+                        self.copy(chunk, kind, 1, True).start()
+                    elif stage == 2:
+                        self.add(chunk, kind, 1)
+                        self.copy(chunk, kind, 2, True).start()
+                        self.copy(chunk, kind, 3, True).start()
+                        self.own_copy(chunk, kind).start()
+                    elif stage == 3:
+                        self.copy(chunk, kind, 2, False).wait_recv()
+                        self.copy(chunk, kind, 4, True).start()
+                    else:
+                        self.copy(chunk, kind, 3, False).wait_recv()
+                        self.copy(chunk, kind, 4, False).wait_recv()
+                        self.own_copy(chunk, kind).wait()
+                        for sent in range(5):
+                            self.copy(chunk, kind, sent, True).wait_send()
+
+
+class RowChain(Chain):
+    def block(self, shard, chunk):
+        shard_rows = self.full.shape[0] // self.count
+        count = shard_rows // self.chunks
+        return self.full.at[rows_at(shard * shard_rows + chunk * count, count)]
+
+    def copy(self, way, step, shard, chunk):
+        self.rows = self.full.shape[0] // self.count // self.chunks
+        return super().copy(way, step, shard, chunk)
+
+
+def back_kernel(
+    heads,
+    lefts,
+    rights,
+    grad_mid,
+    aux_all,
+    gain_in,
+    wof_in,
+    wall_in,
+    n1_in,
+    x_in,
+    kv_in,
+    q_in,
+    att_in,
+    lse_in,
+    trig_in,
+    attl_in,
+    lengths,
+    grad_x,
+    sums_out,
+    gq_out,
+    gkv_out,
+    small_out,
+    total,
+    inbox,
+    give_buf,
+    got_buf,
+    tiles,
+    y,
+    big,
+    wall,
+    x,
+    kv,
+    q,
+    att,
+    lse,
+    trig,
+    att_low,
+    low,
+    ga_send,
+    ga,
+    dkv,
+    kv_give,
+    kv_got,
+    mate_give,
+    mate_got,
+    gqk,
+    gn1,
+    gain_sum,
+    gains,
+    gains_got,
+    load_sem,
+    y_sem,
+    tile_sem,
+    credit,
+    swap_send,
+    swap_recv,
+    ar_send,
+    ar_recv,
+    result_sem,
+    ga_ssem,
+    ga_rsem,
+    gm_send,
+    gm_recv,
+    kv_sem,
+    mate_sem,
+    fin_send,
+    fin_recv,
+    gain_ssem,
+    gain_rsem,
+    end_sem,
+):
+    f32, bf16 = jnp.float32, jnp.bfloat16
+    dp, row, col = lax.axis_index("dp"), lax.axis_index("row"), lax.axis_index("col")
+    place = (dp, row, col)
+    part = grad_mid.shape[0]
+    rows = LINE * part
+    width = heads * HEAD_WIDTH
+    half = TILE
+    hidden = (total.shape[0] - TAIL) // 3
+    member = lax.rem(col, 2)
+    mate = (dp, row, col + 1 - 2 * member)
+    partner = (dp, 1 - row, col)
+    col_peers = [(dp, row, lax.rem(col + k, LINE)) for k in range(1, LINE)]
+    bit_x, bit_y = lax.rem(dp, 2), dp // 2
+    greet(
+        col_peers
+        + [partner, (dp + 1 - 2 * bit_x, row, col), (dp + 2 - 4 * bit_y, row, col)]
+    )
+    chunks = total.shape[0] // CHUNK
+    reduce = AllReduce(place, total, inbox, ar_send, ar_recv, sums_out, result_sem, chunks)
+
+    y_copies = [pltpu.make_async_copy(rights.at[k], y.at[k], y_sem.at[k]) for k in range(2)]
+
+    def tile_copy(index):
+        return pltpu.make_async_copy(
+            lefts.at[index // 3, :, lanes_at(lax.rem(index, 3) * TILE, TILE)],
+            tiles.at[lax.rem(index, 3)],
+            tile_sem.at[lax.rem(index, 3)],
+        )
+
+    y_copies[0].start()
+    for index in range(3):
+        tile_copy(index).start()
+    y_copies[1].start()
+    loads = [
+        pltpu.make_async_copy(src, dst, load_sem.at[k])
+        for k, (src, dst) in enumerate(
+            (
+                (wof_in, big),
+                (wall_in, wall),
+                (x_in, x),
+                (kv_in, kv),
+                (q_in, q),
+                (att_in, att),
+                (lse_in, lse),
+                (trig_in, trig),
+                (attl_in, att_low),
+            )
+        )
+    ]
+    for copy in loads:
+        copy.start()
+
+    theirs, ours = lanes_at((1 - row) * half, half), lanes_at(row * half, half)
+
+    def swap_copy(index):
+        ring = rows_at(lax.rem(index, 2) * TILE, TILE)
+        return remote(
+            give_buf.at[ring],
+            got_buf.at[ring],
+            swap_send.at[lax.rem(index, 2)],
+            swap_recv.at[lax.rem(index, 2)],
+            partner,
+        )
+
+    jobs = 9
+    y_copies[0].wait()
+
+    @pl.loop(0, jobs + 1)
+    def _(index):
+        @pl.when(index == 3)
+        def _():
+            y_copies[1].wait()
+
+        @pl.when(index < jobs)
+        def _():
+            tile_copy(index).wait()
+
+            @pl.when(index >= 2)
+            def _():
+                pl.semaphore_wait(credit, 1)
+                swap_copy(index - 2).wait_send()
+
+            side = jnp.minimum(index // 3, 1)
+            product = matmul_tn(tiles[lax.rem(index, 3)], y[side, :, theirs])
+            give_buf[rows_at(lax.rem(index, 2) * TILE, TILE), :] = product.astype(bf16)
+            swap_copy(index).start()
+
+        @pl.when(index >= 1)
+        def _():
+            last = index - 1
+            side = jnp.minimum(last // 3, 1)
+            product = matmul_tn(tiles[lax.rem(last, 3)], y[side, :, ours])
+            swap_copy(last).wait_recv()
+            product = product + got_buf[rows_at(lax.rem(last, 2) * TILE, TILE), :].astype(f32)
+            first = (last // 3) * hidden + lax.rem(last, 3) * TILE
+            total[rows_at(first, TILE), :] = product.astype(bf16)
+            pl.semaphore_signal(credit, inc=1, device_id=partner, device_id_type=MESH)
+
+            @pl.when(last + 3 < jobs)
+            def _():
+                tile_copy(last + 3).start()
+
+        @pl.when(lax.rem(index, 2) == 1)
+        def _():
+            reduce.step(index // 2)
+
+    for copy in loads:
+        copy.wait()
+    for piece in range(LINE):
+        lanes = slice(piece * width, (piece + 1) * width)
+        low[:, lanes] = grad_mid[:, lanes].astype(bf16)
+
+    def ga_copy(k):
+        to = lax.rem(col + k, LINE)
+        return remote(
+            ga_send.at[k - 1],
+            ga.at[rows_at(col * part, part)],
+            ga_ssem.at[k - 1],
+            ga_rsem.at[k - 1],
+            (dp, row, to),
+        )
+
+    for k in (1, 2, 3, 0):
+        shard = lax.rem(col + k, LINE)
+        block = matmul_nt(low[...], big[shard]).astype(bf16)
+        if k:
+            ga_send[k - 1] = block
+            ga_copy(k).start()
+        else:
+            ga[rows_at(col * part, part), :] = block
+    n1_copy = pltpu.make_async_copy(n1_in, y.at[1], y_sem.at[1])
+    reduce.step(5)
+
+    span = min(512, rows)
+    dkv[...] = jnp.zeros_like(dkv)
+    chain = RowChain(place, low, y.at[0], gm_send, gm_recv, LINE, 2)
+
+    @pl.loop(0, LINE)
+    def _(turn):
+        block = lax.rem(col + LINE - turn, LINE)
+        here = rows_at(block * part, part)
+        for k in range(1, LINE):
+
+            @pl.when(turn == k)
+            def _():
+                ga_copy(k).wait_recv()
+
+        first_query = row * rows + block * part
+        query = q[:, here, :].reshape(heads * part, HEAD_WIDTH)
+        back = jnp.concatenate(
+            [ga[here, h * HEAD_WIDTH : (h + 1) * HEAD_WIDTH] for h in range(heads)], axis=0
+        )
+        attended = att[:, here, :].reshape(heads * part, HEAD_WIDTH)
+        log_total = jnp.concatenate([lse[here, h : h + 1] for h in range(heads)], axis=0)
+        delta = jnp.sum(back.astype(f32) * attended, axis=1, keepdims=True)
+
+        def body(index, acc):
+            keys = rows_at(index * span, span)
+            key, value = kv[keys, :HEAD_WIDTH], kv[keys, HEAD_WIDTH:]
+            scores = matmul_nt(query, key) * SCALE
+            allowed = allowed_keys(lengths, first_query, part, index * span, span)
+            probs = jnp.exp(scores - log_total).reshape(heads, part, span)
+            probs = jnp.where(allowed[None], probs, 0.0).reshape(heads * part, span)
+            grads = matmul_nt(back, value)
+            grad_scores = (probs * (grads - delta)).astype(bf16)
+            dkv[keys, :HEAD_WIDTH] += matmul_tn(grad_scores, query)
+            dkv[keys, HEAD_WIDTH:] += matmul_tn(probs.astype(bf16), back)
+            return acc + matmul(grad_scores, key)
+
+        blocks = (first_query + part + span - 1) // span
+        acc = lax.fori_loop(0, blocks, body, jnp.zeros((heads * part, HEAD_WIDTH), f32))
+        cosine, sine = trig[0, here, :], -trig[1, here, :]
+        for h in range(heads):
+            grad = acc[h * part : (h + 1) * part] * SCALE
+            lanes = slice(h * HEAD_WIDTH, (h + 1) * HEAD_WIDTH)
+            gqk[here, lanes] = rotate(grad, cosine, sine).astype(bf16)
+        reduce.step(6 + turn)
+
+    y[0, rows_at(col * part, part), :] = low[...]
+    for chunk in range(2):
+        chain.start_own(chunk)
+    n1_copy.start()
+
+    other = rows_at((1 - row) * rows, rows)
+    kv_give[...] = dkv[other, :].astype(bf16)
+    kv_copy = remote(kv_give, kv_got, kv_sem.at[0], kv_sem.at[1], partner)
+    kv_copy.start()
+    reduce.step(10)
+    kv_copy.wait_recv()
+    lane = lax.broadcasted_iota(jnp.int32, (1, HEAD_WIDTH), 1)
+    low_lanes = lane < HEAD_WIDTH // 2
+    turn_by = HEAD_WIDTH // 2
+    mate_copy = remote(mate_give, mate_got, mate_sem.at[0], mate_sem.at[1], mate)
+
+    @pl.loop(0, LINE)
+    def _(chunk):
+        here = rows_at(chunk * part, part)
+        there = rows_at(row * rows + chunk * part, part)
+        both = dkv[there, :] + kv_got[here, :].astype(f32)
+        key = rotate(both[:, :HEAD_WIDTH] * SCALE, trig[0, here, :], -trig[1, here, :])
+        value = both[:, HEAD_WIDTH:]
+        first = jnp.where(low_lanes, key, pltpu.roll(value, turn_by, 1))
+        second = jnp.where(low_lanes, pltpu.roll(key, turn_by, 1), value)
+        is_first = jnp.where(member == 0, 1.0, 0.0)
+        kept = first * is_first + second * (1.0 - is_first)
+        given = second * is_first + first * (1.0 - is_first)
+        dkv[there, :HEAD_WIDTH] = kept
+        mate_give[here, :] = given.astype(bf16)
+
+    mate_copy.start()
+    for chunk in range(2):
+        chain.step(1, chunk)
+    reduce.step(11)
+    mate_copy.wait_recv()
+
+    @pl.loop(0, LINE)
+    def _(chunk):
+        here = rows_at(chunk * part, part)
+        there = rows_at(row * rows + chunk * part, part)
+        kept = dkv[there, :HEAD_WIDTH] + mate_got[here, :].astype(f32)
+        gqk[here, width:] = kept.astype(bf16)
+
+    def share_at(chunk, shard):
+        return big.at[chunk, pl.ds(0, part), lanes_at(shard * width, width)]
+
+    def box_rows(slot, chunk):
+        return tiles.at[
+            slot // 2, rows_at(chunk * part, part), lanes_at(lax.rem(slot, 2) * width, width)
+        ]
+
+    def fin_copy(chunk, shard, way):
+        to = col + 1 - 2 * way
+        slot = jnp.where((way == 1) & (shard == to), LINE, shard)
+        return remote(
+            share_at(chunk, shard),
+            box_rows(slot, chunk),
+            fin_send.at[shard, chunk],
+            fin_recv.at[slot, chunk],
+            (dp, row, to),
+        )
+
+    def fin_got(chunk, slot):
+        remote(
+            box_rows(slot, chunk),
+            box_rows(slot, chunk),
+            fin_send.at[0, chunk],
+            fin_recv.at[slot, chunk],
+            partner,
+        ).wait_recv()
+
+    def fin_add(chunk, shard):
+        fin_got(chunk, shard)
+        share = share_at(chunk, shard)
+        share[...] = (share[...].astype(f32) + box_rows(shard, chunk)[...].astype(f32)).astype(bf16)
+
+    def fin_ends(chunk):
+        @pl.when(col == 0)
+        def _():
+            for shard in (3, 2, 1):
+                fin_copy(chunk, shard, 0).start()
+
+        @pl.when(col == LINE - 1)
+        def _():
+            for shard in (0, 1, 2):
+                fin_copy(chunk, shard, 1).start()
+
+    def fin_near(chunk):
+        for k in range(2):
+
+            @pl.when(col == 1)
+            def _():
+                fin_add(chunk, 3 - k)
+                fin_copy(chunk, 3 - k, 0).start()
+
+            @pl.when(col == 2)
+            def _():
+                fin_add(chunk, k)
+                fin_copy(chunk, k, 1).start()
+
+    def fin_far(chunk):
+        @pl.when(col == 1)
+        def _():
+            fin_add(chunk, 0)
+            fin_copy(chunk, 0, 1).start()
+
+        @pl.when(col == 2)
+        def _():
+            fin_add(chunk, 3)
+            fin_copy(chunk, 3, 0).start()
+
+    gain_sum[...] = jnp.zeros_like(gain_sum)
+    kv_lanes = lanes_at(width + member * HEAD_WIDTH, HEAD_WIDTH)
+
+    @pl.loop(0, LINE + 2)
+    def _(chunk):
+        @pl.when(chunk < LINE)
+        def _():
+            here = rows_at(chunk * part, part)
+            squares = jnp.zeros((part, 1), f32)
+            inner = jnp.zeros((part, 1), f32)
+            for shard in range(LINE):
+                lanes = slice(shard * width, (shard + 1) * width)
+                grad = matmul_nt(gqk[here, :width], wall[lanes, :width])
+                grad = grad + matmul_nt(gqk[here, width:], wall[lanes, kv_lanes])
+                gn1[:, lanes] = grad
+                value = x[here, lanes].astype(f32)
+                squares = squares + jnp.sum(value * value, axis=1, keepdims=True)
+                scaled = grad * aux_all[shard, 0:1, :]
+                inner = inner + jnp.sum(scaled * value, axis=1, keepdims=True)
+            inverse = lax.rsqrt(squares / D + eps)
+            factor = inverse * inverse * inverse * inner / D
+            own = jnp.where(chunk == col, 1.0, 0.0)
+            for shard in range(LINE):
+                lanes = slice(shard * width, (shard + 1) * width)
+                grad, value = gn1[:, lanes], x[here, lanes].astype(f32)
+                gain_sum[:, lanes] += jnp.sum(grad * value * inverse, axis=0, keepdims=True)
+                result = inverse * grad * aux_all[shard, 0:1, :] - value * factor
+                result = result + grad_mid[:, lanes] * own
+                big[chunk, :part, lanes] = result.astype(bf16)
+            fin_ends(chunk)
+
+        @pl.when((chunk >= 1) & (chunk <= LINE))
+        def _():
+            fin_near(chunk - 1)
+
+        @pl.when(chunk >= 2)
+        def _():
+            fin_far(chunk - 2)
+
+        reduce.step(12 + chunk)
+
+    gains[...] = gain_in[...]
+    gains[0:1, :] = gain_sum[...]
+
+    def gain_copy(k):
+        to = lax.rem(col + k, LINE)
+        return remote(
+            gains.at[:, lanes_at(to * width, width)],
+            gains_got.at[k - 1],
+            gain_ssem.at[k - 1],
+            gain_rsem.at[k - 1],
+            (dp, row, to),
+        )
+
+    for k in range(1, LINE):
+        gain_copy(k).start()
+
+    for step in (2, 3):
+        for chunk in range(2):
+            chain.step(step, chunk)
+    n1_copy.wait()
+    reduce.step(18)
+    for k in range(1, LINE):
+        gain_copy(k).wait_recv()
+    gain_total = gains[:, lanes_at(col * width, width)]
+    for k in range(1, LINE):
+        gain_total = gain_total + gains_got[k - 1]
+    bias = jnp.zeros((1, width + HEAD_WIDTH), f32)
+    for chunk in range(LINE):
+        piece = gqk[chunk * part : (chunk + 1) * part, :].astype(f32)
+        bias = bias + jnp.sum(piece, axis=0, keepdims=True)
+    small = jnp.concatenate(
+        [
+            jnp.concatenate([gain_total, jnp.zeros((8, half - width), f32)], axis=1),
+            jnp.concatenate(
+                [
+                    jnp.broadcast_to(bias, (8, width + HEAD_WIDTH)),
+                    jnp.zeros((8, half - width - HEAD_WIDTH), f32),
+                ],
+                axis=1,
+            ),
+        ],
+        axis=0,
+    )
+    base = 3 * hidden
+    first_q, first_kv, first_small = width, width + half // 2, width + half // 2 + HEAD_WIDTH
+
+    def projections(side_lanes, store):
+        store(0, width, slice(0, half), matmul_tn(att_low[...], y[0, :, side_lanes]))
+        product = matmul_tn(y[1, :, side_lanes], gqk[...])
+        for k in range(2):
+            store(
+                first_q,
+                half // 2,
+                slice(k * width, (k + 1) * width),
+                product[k * half // 2 : (k + 1) * half // 2, :width],
+            )
+        for k in range(half // HEAD_WIDTH):
+            store(
+                first_kv,
+                HEAD_WIDTH,
+                slice(k * HEAD_WIDTH, (k + 1) * HEAD_WIDTH),
+                product[k * HEAD_WIDTH : (k + 1) * HEAD_WIDTH, width:],
+            )
+        store(first_small, 16, slice(0, half), small)
+        store(first_small + 16, TAIL - first_small - 16, slice(0, half), None)
+
+    for k in range(2):
+        swap_copy(jobs - 2 + k).wait_send()
+    pl.semaphore_wait(credit, 2)
+
+    def store_give(first, count, lanes, value):
+        if value is None:
+            value = jnp.zeros((count, half), f32)
+        give_buf[first : first + count, lanes] = value.astype(bf16)
+
+    def store_keep(first, count, lanes, value):
+        got = got_buf[first : first + count, lanes].astype(f32)
+        if value is not None:
+            got = got + value
+        total[base + first : base + first + count, lanes] = got.astype(bf16)
+
+    projections(theirs, store_give)
+    tail = pl.ds(0, TAIL)
+    tail_copy = remote(give_buf.at[tail], got_buf.at[tail], end_sem.at[0], end_sem.at[1], partner)
+    tail_copy.start()
+    reduce.step(19)
+    tail_copy.wait_recv()
+    projections(ours, store_keep)
+    reduce.step(20)
+
+    for c in range(LINE):
+
+        @pl.when(col == c)
+        def _():
+            @pl.loop(0, LINE)
+            def _(chunk):
+                here = rows_at(chunk * part, part)
+                result = big[chunk, :part, c * width : (c + 1) * width].astype(f32)
+                if c > 0:
+                    fin_got(chunk, c)
+                    result = result + box_rows(c, chunk)[...].astype(f32)
+                if c < LINE - 1:
+                    fin_got(chunk, LINE)
+                    result = result + box_rows(LINE, chunk)[...].astype(f32)
+                grad_x[here, :] = result.astype(bf16)
+
+    @pl.loop(21, chunks + 4 * LAG)
+    def _(number):
+        reduce.step(number)
+
+    outs = [
+        pltpu.make_async_copy(
+            sums_out.at[pl.ds(base + first_q, half // 2), pl.ds(k * width, width)],
+            gq_out.at[pl.ds(k * half // 2, half // 2)],
+            load_sem.at[k],
+        )
+        for k in range(2)
+    ]
+    outs += [
+        pltpu.make_async_copy(
+            sums_out.at[pl.ds(base + first_kv, HEAD_WIDTH), pl.ds(k * HEAD_WIDTH, HEAD_WIDTH)],
+            gkv_out.at[pl.ds(k * HEAD_WIDTH, HEAD_WIDTH)],
+            load_sem.at[2 + k],
+        )
+        for k in range(half // HEAD_WIDTH)
+    ]
+    outs.append(
+        pltpu.make_async_copy(
+            sums_out.at[pl.ds(base + first_small, 16)], small_out, load_sem.at[8]
+        )
+    )
+    for copy in outs:
+        copy.start()
+
+    chain.finish()
+    for k in range(1, LINE):
+        ga_copy(k).wait_send()
+        gain_copy(k).wait_send()
+    kv_copy.wait_send()
+    mate_copy.wait_send()
+    tail_copy.wait_send()
+    for c in range(LINE):
+
+        @pl.when(col == c)
+        def _():
+            for shard in range(LINE):
+                if shard != c:
+
+                    @pl.loop(0, LINE)
+                    def _(chunk):
+                        fin_copy(chunk, shard, 0 if shard > c else 1).wait_send()
+
+    for copy in outs:
+        copy.wait()
+
+
+def back(lefts, rights, grad_mid, aux_all, gain_in, wof, wall, n1, x, kv, q, att, lse, trig, att_low, lengths, hidden):
+    f32, bf16 = jnp.float32, jnp.bfloat16
+    shape = jax.ShapeDtypeStruct
+    dma = pltpu.SemaphoreType.DMA
+    heads, rows, _ = q.shape
+    width = heads * HEAD_WIDTH
+    part = grad_mid.shape[0]
+    total_rows = 3 * hidden + TAIL
+    outs = [
+        (shape((rows, width), bf16), vmem_spec()),
+        (shape((total_rows, TILE), bf16), any_spec()),
+        (shape((TILE, width), bf16), any_spec()),
+        (shape((TILE, HEAD_WIDTH), bf16), any_spec()),
+        (shape((16, TILE), bf16), vmem_spec()),
+    ]
+    vmem = pltpu.VMEM
+    return pl.pallas_call(
+        functools.partial(back_kernel, heads),
+        out_shape=[o[0] for o in outs],
+        in_specs=[any_spec()] * 2
+        + [vmem_spec()] * 3
+        + [any_spec()] * 10
+        + [pl.BlockSpec(memory_space=pltpu.SMEM)],
+        out_specs=[o[1] for o in outs],
+        scratch_shapes=[
+            vmem((total_rows, TILE), bf16),
+            vmem((RING * CHUNK * 3 // 4, TILE), bf16),
+            vmem((2 * TILE, TILE), bf16),
+            vmem((2 * TILE, TILE), bf16),
+            vmem((3, rows, TILE), bf16),
+            vmem((2, rows, D), bf16),
+            vmem(wof.shape, bf16),
+            vmem(wall.shape, bf16),
+            vmem(x.shape, bf16),
+            vmem(kv.shape, bf16),
+            vmem(q.shape, bf16),
+            vmem(att.shape, f32),
+            vmem(lse.shape, f32),
+            vmem(trig.shape, f32),
+            vmem(att_low.shape, bf16),
+            vmem((part, D), bf16),
+            vmem((LINE - 1, part, width), bf16),
+            vmem((rows, width), bf16),
+            vmem(kv.shape, f32),
+            vmem((rows, 2 * HEAD_WIDTH), bf16),
+            vmem((rows, 2 * HEAD_WIDTH), bf16),
+            vmem((rows, HEAD_WIDTH), bf16),
+            vmem((rows, HEAD_WIDTH), bf16),
+            vmem((rows, width + HEAD_WIDTH), bf16),
+            vmem((part, D), f32),
+            vmem((1, D), f32),
+            vmem((8, D), f32),
+            vmem((LINE - 1, 8, width), f32),
+            dma((9,)),
+            dma((2,)),
+            dma((3,)),
+            pltpu.SemaphoreType.REGULAR,
+            dma((2,)),
+            dma((2,)),
+            dma((RING, 2, 5)),
+            dma((RING, 2, 5)),
+            dma((RING, 2)),
+            dma((LINE - 1,)),
+            dma((LINE - 1,)),
+            dma((2, LINE - 1, 2)),
+            dma((LINE, 2)),
+            dma((2,)),
+            dma((2,)),
+            dma((LINE, LINE)),
+            dma((LINE + 1, LINE)),
+            dma((LINE - 1,)),
+            dma((LINE - 1,)),
+            dma((2,)),
+        ],
+        compiler_params=pltpu.CompilerParams(
+            collective_id=3, has_side_effects=True, vmem_limit_bytes=63 * 2**20
+        ),
+        cost_estimate=pl.CostEstimate(
+            flops=64 * 10**9, bytes_accessed=60 * 10**6, transcendentals=10**7
+        ),
+        name="back",
+    )(lefts, rights, grad_mid, aux_all, gain_in, wof, wall, n1, x, kv, q, att, lse, trig, att_low, lengths)
 
 
 def per_device(
@@ -1461,150 +2199,99 @@
     w_down,
     cotangent,
 ):
-    row_pos = lax.axis_index("row")
-    col_pos = lax.axis_index("col")
-    row_count = lax.axis_size("row")
-    col_count = lax.axis_size("col")
-    rows = inputs.shape[0]
-    part = rows // col_count
-    seq_len = rows * row_count
-    heads = QUERY_HEADS // col_count
-    share = col_count // KEY_VALUE_HEADS
-    groups = [[g * share + s for s in range(share)] for g in range(KEY_VALUE_HEADS)]
-    f32, bf16 = jnp.float32, jnp.bfloat16
-
+    f32 = jnp.float32
+    planes = lax.axis_size("dp")
+    rows, width = inputs.shape
+    kv_cols = w_key.shape[1]
+    hidden = w_down.shape[0]
     half = HEAD_WIDTH // 2
     freq = theta_base ** (-(jnp.arange(half, dtype=f32) * 2.0) / HEAD_WIDTH)
     freq = jnp.concatenate([freq, freq]).reshape(1, HEAD_WIDTH)
-    kv_cols = w_key.shape[1]
     biases = jnp.concatenate([b_key, b_value]).astype(f32)
-    aux = jnp.stack(
-        [gain_one, gain_two, b_query.astype(f32), jnp.pad(biases, (0, gain_one.shape[0] - 2 * kv_cols))]
-    )
+    biases = jnp.pad(biases, (0, width - 2 * kv_cols))
+    aux = jnp.stack([gain_one, gain_two, b_query.astype(f32), biases])
     aux = jnp.pad(aux, ((0, 4), (0, 0)))
     own_kv = jnp.concatenate([w_key, w_value], axis=1)
+    own = (w_gate.T, w_up.T, w_down)
     (
-        inputs_full, normed_one, cot_full, query_rot, seq_kv, attended_f32, lse, att_own, hidden_mid, normed_part, trig, aux_all, wall, wof, peer_gate, peer_up, peer_down,
+        x_full,
+        normed_one,
+        cot_full,
+        queries,
+        keys_values,
+        attended,
+        log_total,
+        att_own,
+        hidden_mid,
+        normed_two,
+        trig,
+        att_low,
+        aux_all,
+        wall,
+        wof,
+        *peer,
     ) = front(
-        (col_count, lax.axis_size("dp")), aux, inputs, cotangent, w_query, own_kv, w_out, w_gate.T, w_up.T, w_down, seq_lengths, freq
-    )
-    gain_one_full = aux_all[:, 0].reshape(D)
-    gain_two_full = aux_all[:, 1].reshape(D)
-    full_query = wall[:, : heads * HEAD_WIDTH]
-    own_kv = lax.dynamic_slice_in_dim(wall, heads * HEAD_WIDTH + lax.rem(col_pos, 2) * HEAD_WIDTH, HEAD_WIDTH, 1)
-
-    full_out = wof[col_pos]
-    lengths = seq_lengths[0]
-    place_local = row_pos * rows + jnp.arange(rows, dtype=jnp.int32)
-    doc_local, local_position = documents(lengths, place_local)
-    doc_all = documents(lengths, jnp.arange(seq_len, dtype=jnp.int32))[0]
-
-    hidden_in = inputs_full.astype(f32)
-    inverse_one = norm_rows(hidden_in, gain_one_full)[1]
-    blocks = key_layout(seq_kv[:, :HEAD_WIDTH], seq_kv[:, HEAD_WIDTH:], doc_all)
-    heads_of_queries = query_rot.transpose(1, 0, 2)[:, None]
-    attended = attended_f32.transpose(1, 0, 2)[:, None]
-    log_total = lse[:, :, 0].transpose(1, 0)[:, None]
-    attended_cols = attended.reshape(rows, heads * HEAD_WIDTH).astype(bf16)
-    start = col_pos * part
-    out_part, sum_down, sum_gate, sum_up, grad_mid, grad_gain_two = mlp(
-        normed_part,
-        cot_full,
-        hidden_mid,
+        (LINE, planes),
+        aux,
+        inputs,
+        cotangent,
+        w_query,
+        own_kv,
+        w_out,
+        *own,
+        seq_lengths,
+        freq,
+    )
+    out_part, lefts, rights, grad_mid, grad_gain_two = mlp(
+        normed_two, cot_full, hidden_mid, aux_all, own, peer
+    )
+    grad_inputs, sums, grad_w_query, grad_kv, small = back(
+        lefts,
+        rights,
+        grad_mid,
         aux_all,
-        (w_gate.T, w_up.T, w_down),
-        (peer_gate, peer_up, peer_down),
-    )
-    grad_gain_two = grad_gain_two[0]
+        grad_gain_two,
+        wof,
+        wall,
+        normed_one,
+        x_full,
+        keys_values,
+        queries,
+        attended,
+        log_total,
+        trig,
+        att_low.reshape(rows, width),
+        seq_lengths,
+        hidden,
+    )
     result = lax.psum_scatter(out_part, "col", scatter_dimension=1, tiled=True)
-    wide_sums = lax.psum((sum_down, sum_gate, sum_up), "dp")
-
-    def row_sum(grad, dim):
-        return lax.psum_scatter(grad.astype(bf16), "row", scatter_dimension=dim, tiled=True)
-
-    grad_mid_full = lax.all_gather(grad_mid.astype(bf16), "col", axis=0, tiled=True)
-    grad_attended = matmul_nt(grad_mid_full, full_out).astype(bf16)
-    grad_query_rot, key_grads, value_grads = attention_backward(
-        heads_of_queries,
-        blocks,
-        doc_local,
-        place_local,
-        log_total,
-        attended,
-        grad_attended.reshape(rows, 1, heads, HEAD_WIDTH),
-    )
-    grad_w_out = row_sum(matmul_tn(attended_cols, grad_mid_full), 1)
-    kv_grads = lax.psum_scatter(
-        jnp.concatenate([key_grads, value_grads], axis=1).astype(bf16),
-        "row",
-        scatter_dimension=0,
-        tiled=True,
-    ).astype(f32)
-    grad_key_part = rotary_embedding(kv_grads[:, None, :HEAD_WIDTH], local_position, -1.0)
-    kv_part = jnp.stack(
-        [grad_key_part.reshape(rows, share, kv_cols), kv_grads[:, HEAD_WIDTH:].reshape(rows, share, kv_cols)],
-        axis=2,
-    ).reshape(rows, 2 * HEAD_WIDTH)
-    kv_grad_cols = lax.psum_scatter(
-        kv_part.astype(bf16), "col", scatter_dimension=1, tiled=True, axis_index_groups=groups
-    )
-    query_grad_cols = (
-        rotary_embedding(
-            grad_query_rot.reshape(rows, heads, HEAD_WIDTH), local_position, -1.0
-        )
-        .reshape(rows, heads * HEAD_WIDTH)
-        .astype(bf16)
-    )
-    grad_w_query = row_sum(matmul_tn(normed_one, query_grad_cols), 0)
-    grad_w_kv = row_sum(matmul_tn(normed_one, kv_grad_cols), 0)
-    (grad_w_out, grad_w_query, grad_w_kv), wide_sums = lax.optimization_barrier(
-        ((grad_w_out, grad_w_query, grad_w_kv), wide_sums)
-    )
-    grad_w_out, grad_w_query, grad_w_kv = (
-        g.astype(f32) for g in lax.psum((grad_w_out, grad_w_query, grad_w_kv), "dp")
-    )
-    grad_w_down, grad_w_gate, grad_w_up = (g.astype(f32) for g in wide_sums)
-    grad_w_gate, grad_w_up = grad_w_gate.T, grad_w_up.T
-    grad_b_query = jnp.sum(query_grad_cols.astype(f32), axis=0)
-    grad_b_kv = jnp.sum(kv_grad_cols.astype(f32), axis=0)
-    grad_normed_one = matmul_nt(query_grad_cols, full_query) + matmul_nt(kv_grad_cols, own_kv)
-    scaled_one = grad_normed_one * gain_one_full[None, :]
-    inner_one = jnp.sum(scaled_one * hidden_in, axis=1, keepdims=True)
-    grad_gain_one = jnp.sum(grad_normed_one * hidden_in * inverse_one, axis=0)
-    back_one = inverse_one * scaled_one - hidden_in * (
-        inverse_one * inverse_one * inverse_one * inner_one / D
-    )
-    back_one = lax.dynamic_update_slice_in_dim(
-        back_one, lax.dynamic_slice_in_dim(back_one, start, part, 0) + grad_mid, start, 0
-    )
-    grad_inputs = lax.psum_scatter(back_one.astype(bf16), "col", scatter_dimension=1, tiled=True)
-    gains = lax.psum_scatter(
-        jnp.stack([grad_gain_one, grad_gain_two]), "col", scatter_dimension=1, tiled=True
-    )
-    width = gains.shape[1]
-    small = jnp.concatenate([gains.reshape(-1), grad_b_query, grad_b_kv])
-    small = lax.psum(small, ("dp", "row"))
-    biases = small[2 * width :]
+    grad_w_down, grad_w_gate, grad_w_up = (
+        sums[k * hidden : (k + 1) * hidden].astype(f32) for k in range(3)
+    )
+    grad_w_out = sums[3 * hidden : 3 * hidden + width].astype(f32)
+    grad_kv = grad_kv.astype(f32)
+    small = small.astype(f32)
+    bias = small[8]
     return (
         result,
         grad_inputs,
-        small[:width],
-        grad_w_query,
-        biases[:width],
-        grad_w_kv[:, :kv_cols],
-        biases[width : width + kv_cols],
-        grad_w_kv[:, kv_cols:],
-        biases[width + kv_cols :],
+        small[0, :width],
+        grad_w_query.astype(f32),
+        bias[:width],
+        grad_kv[:, :kv_cols],
+        bias[width : width + kv_cols],
+        grad_kv[:, kv_cols:],
+        bias[width + kv_cols : width + 2 * kv_cols],
         grad_w_out,
-        small[width : 2 * width],
-        grad_w_gate,
-        grad_w_up,
+        small[1, :width],
+        grad_w_gate.T,
+        grad_w_up.T,
         grad_w_down,
     )
 
 
 def solution(mesh):
-    whole_heads = dict(mesh.shape) == {"dp": 4, "row": 2, "col": 4}
+    whole_heads = dict(mesh.shape) == {"dp": 4, "row": 2, "col": LINE}
     return jax.shard_map(
         per_device if whole_heads else per_device_any,
         mesh=mesh,

time: 742 us -> 569 us (0.77)
  waiting for transfers between devices: 288 us -> 0.02 us
  Pallas kernels: 261 us -> 509 us
  matrix products: 69.2 us -> 0 us
  local copies, waits for them, and re-layouts: 51.1 us -> 20.2 us
  other arithmetic: 33.9 us -> 16 us
  blocking collectives: 13.6 us -> 0 us
    pallas_call x0 -> x1, Pallas kernels: none -> 268 us  [back(): pl.pallas_call(functools.partial(back_kernel, heads), out_shape=[o[0] for...]
    psum x2 -> x0, waiting for transfers between devices: 198 us -> none  [the longest x1 176 us: per_device(): wide_sums = lax.psum((sum_down, sum_gate, sum_up), 'dp')]
    dot_general x26 -> x0, matrix products: 69.2 us -> none  [the longest x4 13.2 us: back_pass(): jnp.einsum('tkgs,skh->tkgh', grad_scores, packed[0], preferred_element_ty...]
    all_gather x1 -> x0, waiting for transfers between devices: 60.4 us -> none  [per_device(): lax.all_gather(grad_mid.astype(bf16), 'col', axis=0, tiled=True)]
    reduce_scatter x5 -> x0, waiting for transfers between devices: 28 us -> none  [the longest x3 16.7 us: row_sum(): lax.psum_scatter(grad.astype(bf16), 'row', scatter_dimension=dim, tiled=T...]
    pallas_call x1, Pallas kernels: 114 us -> 93.5 us  [mlp(): pl.pallas_call(mlp_kernel, out_shape=[o[0] for o in outs], in_specs=[any_...]
    psum x1 -> x0, blocking collectives: 13.6 us -> none  [per_device(): small = lax.psum(small, ('dp', 'row'))]
    while x80 -> x0, local copies, waits for them, and re-layouts: 10.9 us -> none
  transfers between devices with their start and end apart: 11 -> 1, of which waited for: 8 -> 0; matrix products, arithmetic and copies ran while one was open for 8% -> 3% of each run, Pallas kernels for 0% -> 48%
where the time goes in v4:
time: 569 us; the launch traced here: 560 us
  Pallas kernels  509 us (89%)
  local copies, waits for them, and re-layouts  20.2 us (4%)
  other arithmetic  16 us (3%)
  between operations  14.6 us (3%)
    pallas_call x1, Pallas kernels, back(): pl.pallas_call(functools.partial(back_kernel, heads), out_shape=[o[0] for...  268 us
    pallas_call x1, Pallas kernels, front(): pl.pallas_call(functools.partial(front_kernel, heads, dims), out_shape=[o...  147 us
    pallas_call x1, Pallas kernels, mlp(): pl.pallas_call(mlp_kernel, out_shape=[o[0] for o in outs], in_specs=[any_...  93.5 us
    unnamed x19, local copies, waits for them, and re-layouts  15.8 us
  transfers between devices with their start and end apart: 1, of which 0 were waited for; matrix products, arithmetic and copies ran while one was open for 3% of the time, Pallas kernels for 48%

profile of v4, /device:TPU:0, one launch (start us, length us, event | category | flops | bytes accessed | tf_op | source)
XLA Modules:
  0.0 560.1 jit_solution(16000225990917634382)
XLA Ops:
  7.2 0.0 reduce-scatter.4.cloned.1.call-start
  7.2 0.1 maximum_bitcast_fusion.freq
  7.3 0.7 stack.21
  8.0 0.7 reshape.39
  8.7 0.7 stack.22
  9.4 0.7 fusion.3
  10.1 1.1 copy.33
  11.2 1.1 copy.34
  12.3 0.1 pad_maximum_fusion.wkv
  12.4 0.0 copy-start
  12.4 1.1 copy-done
  13.5 1.1 copy-done.1
  14.6 0.7 copy-done.2
  15.2 147.4 %front.1 = (bf16[1024,1536]{1,0:T(8,128)(2,1)}, bf16[1024,1536]{1,0:T(8,128)(2,1)}, bf16[1024,1536]{1,0:T(8,128)(2,1)}, bf16[3,1024,128]{2,1,0:T(8,128)(2,1)}, b...) custom-call(f32[8,384]{1,0:T(8,128)S(1)} %select_maximum_fusion.aux,, ...), custom_call_target="tpu_custom_call" | custom-call | flops 10000000000 | bytes 60000000 | tf_op jit(solution)/shard_map/front/pallas_call | solution.py:940
  162.6 0.0 copy-start.3
  162.6 0.8 copy-done.3
  163.4 0.6 copy-done.4
  164.0 93.5 %mlp.1 = (bf16[1024,1536]{1,0:T(8,128)(2,1)}, bf16[3,1024,2304]{2,1,0:T(8,128)(2,1)}, bf16[2,1024,1536]{2,1,0:T(8,128)(2,1)}, f32[256,1536]{1,0:T(8,128)}, f32[8,1536]{1,0:T(8,128)}) custom-call(bf16[256,1536]{1,0:T(8,128)(2,1)} %get-tuple-element.41.n2, bf16[1024,1536]{1,0:T(8,128)(2,1)} %get-tuple-element.42.cot_full, f32[256,1536]{1,0:T(8,128)} %get-tuple-element.43.hid, ...), custom_call_target="tpu_custom_call" | custom-call | flops 64000000000 | bytes 60000000 | tf_op jit(solution)/shard_map/mlp/pallas_call | solution.py:1388
  257.5 4.6 copy.37
  262.2 0.0 reduce-scatter.4.cloned.1.call-update
  262.2 268.4 %back.1 = (bf16[1024,384]{1,0:T(8,128)(2,1)}, bf16[7680,768]{1,0:T(8,128)(2,1)}, bf16[768,384]{1,0:T(8,128)(2,1)}, bf16[768,128]{1,0:T(8,128)(2,1)}, bf16[16,768]{1,0:T(8,128)(2,1)}) custom-call(bf16[3,1024,2304]{2,1,0:T(8,128)(2,1)} %get-tuple-element.49.lefts, bf16[2,1024,1536]{2,1,0:T(8,128)(2,1)} %get-tuple-element.50.rights, ...), custom_call_target="tpu_custom_call" | custom-call | flops 64000000000 | bytes 60000000 | tf_op jit(solution)/shard_map/back/pallas_call | solution.py:2117
  530.7 0.7 convert_element_type.23
  531.4 1.1 fusion.4
  532.5 0.8 copy.36
  533.4 0.8 copy.35
  534.2 2.2 convert_element_type.24
  536.4 0.6 slice_reduce_fusion
  537.0 0.6 slice_bitcast_fusion
  537.5 2.2 slice_convert_fusion.1
  539.7 10.0 %slice_convert_fusion = (f32[2240,768]{1,0:T(8,128)}, f32[768,2240]{0,1:T(8,128)}, f32[768,2240]{0,1:T(8,128)}) fusion(bf16[7680,768]{1,0:T(8,128)(2,1)} %get-tuple-element.67), kind=kLoop, calls=%fused_computation.2 | loop fusion | flops 5160960 | bytes 30965760 | tf_op jit(solution)/shard_map/convert_element_type | solution.py:2269
  549.7 2.3 copy.38
  551.9 0.9 copy.40
  (9 shorter events, 0.0 us)
Async XLA Ops:
  7.2 542.5 %reduce-scatter.4.cloned.1.call-start = ((), (), s32[]{:S(2)}) async-start(), calls=%async_computation.1 | async-start | bytes 3932160
  12.4 1.1 copy-start
  13.5 1.1 copy-start.1
  14.6 0.7 copy-start.2
  162.6 0.8 copy-start.3
  163.4 0.6 copy-start.4
  539.7 12.3 %copy-start.5 = (bf16[1024,384]{1,0:T(8,128)(2,1)S(1)}, bf16[1024,384]{1,0:T(8,128)(2,1)}, u32[]{:S(2)}) copy-start(bf16[1024,384]{1,0:T(8,128)(2,1)} %get-tuple-element.121) | copy-start | bytes 2359300
Sparse Core Ops, SparseCore 0:
  262.3 71.8 reduce-scatter.3

commit v5 on v4

--- a/solution.py
+++ b/solution.py
@@ -980,20 +980,9 @@
     )(aux, x, cot, wq, wkv, wout, w_gate, w_up, w_down, lengths, freq)
 
 
-TICKS = ((0, 1, 2, 4, 6, 7, 5, 3), (2, 3, 0, 4, 1, 6, 7, 5), (4, 5, 6, 2, 7, 0, 1, 3), (6, 7, 4, 2, 0, 1, 3, 5))
-SLOTS = tuple(tuple(order.index(q) for q in range(8)) for order in TICKS)
-ONWARD = (
-    ((), (0, 1, 3), (2, 0, 1, 3, 5), ()),
-    ((), (4, 6, 7, 5, 3), (6, 7, 5), ()),
-)
-SUMS = (
-    ((2, 0), (4, 0), (6, 0), (7, 0), (5, 0), (3, 0)),
-    ((4, 0), (6, 0), (7, 0), (0, 1), (5, 0), (1, 1)),
-    ((2, 1), (0, 1), (1, 1), (6, 0), (3, 1), (7, 0)),
-    ((4, 1), (2, 1), (0, 1), (1, 1), (3, 1), (5, 1)),
-)
 LINE = 4
 TILE = 768
+ORDER = ((0, 1, 2, 3), (1, 0, 2, 3), (2, 1, 3, 0), (3, 2, 1, 0))
 
 
 def pick(index, values):
@@ -1008,91 +997,180 @@
     return [(first, min(tile, total - first)) for first in range(0, total, tile)]
 
 
+class RowChain(Chain):
+    def block(self, shard, chunk):
+        shard_rows = self.full.shape[0] // self.count
+        count = shard_rows // self.chunks
+        return self.full.at[rows_at(shard * shard_rows + chunk * count, count)]
+
+    def copy(self, way, step, shard, chunk):
+        self.rows = self.full.shape[0] // self.count // self.chunks
+        return super().copy(way, step, shard, chunk)
+
+
+class LineSum:
+    def __init__(self, place, share, box, sends, recvs, chunks):
+        self.dp, self.row, self.col = place
+        self.share, self.box, self.sends, self.recvs = share, box, sends, recvs
+        self.chunks = chunks
+
+    def copy(self, c, chunk, shard):
+        to = c + 1 if shard > c else c - 1
+        slot = LINE if to < c and shard == to else shard
+        return remote(
+            self.share(chunk, shard),
+            self.box(slot, chunk),
+            self.sends.at[shard, chunk],
+            self.recvs.at[slot, chunk],
+            (self.dp, self.row, to),
+        )
+
+    def got(self, chunk, slot):
+        box = self.box(slot, chunk)
+        partner = (self.dp, 1 - self.row, self.col)
+        remote(box, box, self.sends.at[0, chunk], self.recvs.at[slot, chunk], partner).wait_recv()
+
+    def onward(self, c, chunk, shard):
+        self.got(chunk, shard)
+        share, box = self.share(chunk, shard), self.box(shard, chunk)
+        share[...] = (share[...].astype(jnp.float32) + box[...].astype(jnp.float32)).astype(
+            jnp.bfloat16
+        )
+        self.copy(c, chunk, shard).start()
+
+    def left_end(self, chunk):
+        @pl.when(self.col == 0)
+        def _():
+            for shard in (3, 2, 1):
+                self.copy(0, chunk, shard).start()
+
+    def right_end(self, chunk):
+        @pl.when(self.col == LINE - 1)
+        def _():
+            for shard in (0, 1, 2):
+                self.copy(LINE - 1, chunk, shard).start()
+
+    def ends(self, chunk):
+        self.left_end(chunk)
+        self.right_end(chunk)
+
+    def near_left(self, chunk):
+        @pl.when(self.col == 1)
+        def _():
+            for shard in (3, 2):
+                self.onward(1, chunk, shard)
+
+    def near_right(self, chunk):
+        @pl.when(self.col == 2)
+        def _():
+            for shard in (0, 1):
+                self.onward(2, chunk, shard)
+
+    def near(self, chunk):
+        self.near_left(chunk)
+        self.near_right(chunk)
+
+    def far(self, chunk):
+        @pl.when(self.col == 1)
+        def _():
+            self.onward(1, chunk, 0)
+
+        @pl.when(self.col == 2)
+        def _():
+            self.onward(2, chunk, 3)
+
+    def clear_ends(self):
+        for c, slot in ((0, 0), (LINE - 1, LINE)):
+
+            @pl.when(self.col == c)
+            def _():
+                for chunk in range(self.chunks):
+                    box = self.box(slot, chunk)
+                    box[...] = jnp.zeros(box.shape, jnp.bfloat16)
+
+    def wait_own(self, chunk):
+        @pl.when(self.col > 0)
+        def _():
+            self.got(chunk, self.col)
+
+        @pl.when(self.col < LINE - 1)
+        def _():
+            self.got(chunk, LINE)
+
+    def own(self, chunk):
+        self.wait_own(chunk)
+        refs = (self.share(chunk, self.col), self.box(self.col, chunk), self.box(LINE, chunk))
+        return sum(ref[...].astype(jnp.float32) for ref in refs)
+
+    def finish(self):
+        for c in range(LINE):
+
+            @pl.when(self.col == c)
+            def _():
+                @pl.loop(0, self.chunks)
+                def _(chunk):
+                    for shard in range(LINE):
+                        if shard != c:
+                            self.copy(c, chunk, shard).wait_send()
+
+
 def mlp_kernel(
     n2,
     cot_full,
     hid,
-    aux_all,
     own_gate,
     own_up,
     own_down,
     peer_gate,
     peer_up,
     peer_down,
-    out_part,
     left_out,
-    right_out,
-    grad_mid,
-    grad_gain,
+    n2_out,
+    result,
+    out_rest,
     gate_w,
     up_w,
     down_w,
-    mixed,
-    g_gate,
-    g_up,
+    hidden_parts,
     n2s,
     cots,
-    parts,
-    coming,
-    stage,
     w_sem,
     cot_sem,
     own_sem,
     ag_send,
     ag_recv,
-    rs_send,
-    rs_recv,
+    left_sem,
+    n2_sem,
+    shares,
+    boxes,
+    stage,
+    out_send,
+    out_recv,
     out_sem,
-    left_sem,
-    right_sem,
 ):
     f32, bf16 = jnp.float32, jnp.bfloat16
     dp, row, col = lax.axis_index("dp"), lax.axis_index("row"), lax.axis_index("col")
     part = n2.shape[0]
-    piece = part // 2
     hidden, half = own_gate.shape
     tiles = hidden_tiles(hidden)
-    partner = (dp, 1 - row, col)
-    greet([(dp, row, lax.rem(col + k, LINE)) for k in range(1, LINE)] + [partner])
-
-    def slot_rows(slot):
-        return rows_at(slot * piece, piece)
-
-    def hand_on(c, way, q, source=None):
-        to = c + 1 - 2 * way
-        src = n2s.at[slot_rows(SLOTS[c][q])] if source is None else source
-        return remote(
-            src, n2s.at[slot_rows(SLOTS[to][q])], ag_send.at[way, q], ag_recv.at[q], (dp, row, to)
-        )
-
-    def got(c, q):
-        rows_here = n2s.at[slot_rows(SLOTS[c][q])]
-        remote(rows_here, rows_here, ag_send.at[0, q], ag_recv.at[q], partner).wait_recv()
-
-    def ways(c):
-        return [way for way in (0, 1) if 0 <= c + 1 - 2 * way < LINE]
-
-    for c in range(LINE):
-
-        @pl.when(col == c)
-        def _():
-            for way in ways(c):
-                hand_on(c, way, 2 * c, n2.at[pl.ds(0, piece)]).start()
-            if c in (0, LINE - 1):
-                hand_on(c, ways(c)[0], 2 * c + 1, n2.at[pl.ds(piece, piece)]).start()
-
-    own_copy = pltpu.make_async_copy(n2, n2s.at[pl.ds(0, part)], own_sem)
+    greet([(dp, row, lax.rem(col + k, LINE)) for k in range(1, LINE)])
+    chain = RowChain((dp, row, col), n2, n2s, ag_send, ag_recv, LINE, 2)
+    for chunk in range(2):
+        chain.start_own(chunk)
+    own_copy = pltpu.make_async_copy(n2, n2s.at[rows_at(col * part, part)], own_sem)
     own_copy.start()
+
+    def cot_copy(tick):
+        here = rows_at(pick(col, [order[tick] for order in ORDER]) * part, part)
+        return pltpu.make_async_copy(cot_full.at[here], cots.at[here], cot_sem.at[tick])
 
     def load_copies(index, first, count):
         rows_here = pl.ds(first, count)
         copies = []
-        for k, (own, peer, whole) in enumerate(
-            (
-                (own_gate, peer_gate, gate_w),
-                (own_up, peer_up, up_w),
-                (own_down, peer_down, down_w),
-            )
+        for own, peer, whole in (
+            (own_gate, peer_gate, gate_w),
+            (own_up, peer_up, up_w),
+            (own_down, peer_down, down_w),
         ):
             for side, src in ((row, own), (1 - row, peer)):
                 copies.append((src.at[rows_here], whole.at[rows_here, lanes_at(side * half, half)]))
@@ -1101,125 +1179,65 @@
             for k, (src, dst) in enumerate(copies)
         ]
 
-    def cot_copy(slot):
-        q = pick(col, [order[slot] for order in TICKS])
-        return pltpu.make_async_copy(
-            cot_full.at[slot_rows(q)], cots.at[slot_rows(slot)], cot_sem.at[slot]
-        )
-
-    for slot in range(2):
-        cot_copy(slot).start()
+    cot_copy(0).start()
     for index, (first, count) in enumerate(tiles):
         for copy in load_copies(index, first, count):
             copy.start()
-    for slot in range(2, 2 * LINE):
-        cot_copy(slot).start()
-    for h in range(2):
-
-        @pl.when(col == 0)
-        def _():
-            coming[h] = jnp.zeros(coming.shape[1:], bf16)
-
-        @pl.when(col == LINE - 1)
-        def _():
-            coming[2 * LINE + h] = jnp.zeros(coming.shape[1:], bf16)
-
+    for tick in range(1, LINE):
+        cot_copy(tick).start()
+    hidden_parts[:, :, :, hidden:] = jnp.zeros(
+        hidden_parts.shape[:3] + (hidden_parts.shape[3] - hidden,), bf16
+    )
     own_copy.wait()
-    for ref in (mixed, g_gate, g_up):
-        ref[:, hidden:] = jnp.zeros((ref.shape[0], ref.shape[1] - hidden), bf16)
-
-    def onward(f):
-        for c in (1, 2):
-            for way in (0, 1):
-                if f < len(ONWARD[way][c]):
-                    q = ONWARD[way][c][f]
-
-                    @pl.when(col == c)
-                    def _():
-                        if q // 2 != c:
-                            got(c, q)
-                        hand_on(c, way, q).start()
-
-    def sum_copy(c, q, way):
-        to = c + 1 - 2 * way
-        place = 2 * LINE + q % 2 if way == 1 and q // 2 == to else q
-        return remote(
-            parts.at[slot_rows(SLOTS[c][q])],
-            coming.at[place],
-            rs_send.at[q],
-            rs_recv.at[place],
-            (dp, row, to),
-        )
-
-    def sum_start(e, c):
-        q, way = SUMS[c][e]
-        sum_copy(c, q, way).start()
-
-    def sum_ends(e):
-        for c in (0, LINE - 1):
-
-            @pl.when(col == c)
-            def _():
-                sum_start(e, c)
-
-    def sum_mids(e):
-        @pl.when((col == 1) | (col == 2))
-        def _():
-            q = jnp.where(col == 1, SUMS[1][e][0], SUMS[2][e][0])
-            slot = jnp.where(col == 1, SLOTS[1][SUMS[1][e][0]], SLOTS[2][SUMS[2][e][0]])
-            here = slot_rows(slot)
-            remote(parts.at[here], coming.at[q], rs_send.at[q], rs_recv.at[q], partner).wait_recv()
-            parts[here, :] = (parts[here, :].astype(f32) + coming[q].astype(f32)).astype(bf16)
-            for c in (1, 2):
-
-                @pl.when(col == c)
-                def _():
-                    sum_start(e, c)
-
-    def out_copies(tick):
-        copies = []
-        for h in range(2):
-            q = pick(
-                tick, [pick(col, [order[2 * t + h] for order in TICKS]) for t in range(LINE)]
+    width = D // LINE
+    line = LineSum(
+        (dp, row, col),
+        lambda chunk, shard: shares.at[chunk + 1, :, lanes_at(shard * width, width)],
+        lambda slot, chunk: boxes.at[slot, chunk],
+        out_send,
+        out_recv,
+        2,
+    )
+    line.clear_ends()
+    is_end = (col == 0) | (col == LINE - 1)
+
+    def left_copies(tick):
+        shard = pick(tick, [pick(col, [order[t] for order in ORDER]) for t in range(LINE)])
+        here = rows_at(shard * part, part)
+        slot = lax.rem(tick, 2)
+        return [
+            pltpu.make_async_copy(
+                hidden_parts.at[slot, k], left_out.at[k, here], left_sem.at[slot, k]
             )
-            copies.append(
-                pltpu.make_async_copy(
-                    stage.at[lax.rem(tick, 2), pl.ds(h * piece, piece)],
-                    out_part.at[slot_rows(q)],
-                    out_sem.at[lax.rem(tick, 2), h],
-                )
-            )
-        return copies
-
-    def left_copies(tick):
-        here = rows_at(tick * part, part)
-        return [
-            pltpu.make_async_copy(ref.at[here], left_out.at[k, here], left_sem.at[tick, k])
-            for k, ref in enumerate((mixed, g_gate, g_up))
+            for k in range(3)
         ]
-
-    def right_copy(slot):
-        return pltpu.make_async_copy((cots, n2s)[slot], right_out.at[slot], right_sem.at[slot])
-
-    lane_tiles = [(k * 512, 512) for k in range(D // 512)]
 
     @pl.loop(0, LINE)
     def _(tick):
-        here = rows_at(tick * part, part)
-        for c in (0, LINE - 1):
-            for t in range(1, LINE):
-
-                @pl.when((col == c) & (tick == t))
-                def _():
-                    for h in range(2):
-                        got(c, TICKS[c][2 * t + h])
-
-        for h in range(2):
-            pltpu.make_async_copy(
-                cot_full.at[pl.ds(0, piece)],
-                cots.at[slot_rows(2 * tick + h)],
-                cot_sem.at[2 * tick + h],
-            ).wait()
+        @pl.when(tick == 1)
+        def _():
+            for chunk in range(2):
+                chain.step(1, chunk)
+
+        @pl.when(((tick == 2) & is_end) | ((tick == 3) & jnp.logical_not(is_end)))
+        def _():
+            for chunk in range(2):
+                chain.step(2, chunk)
+
+        @pl.when((tick == 3) & is_end)
+        def _():
+            for chunk in range(2):
+                chain.step(3, chunk)
+
+        shard = pick(tick, [pick(col, [order[t] for order in ORDER]) for t in range(LINE)])
+        here = rows_at(shard * part, part)
+        slot = lax.rem(tick, 2)
+        pltpu.make_async_copy(cot_full.at[here], cots.at[here], cot_sem.at[tick]).wait()
+
+        @pl.when(tick >= 2)
+        def _():
+            for copy in left_copies(tick - 2):
+                copy.wait()
 
         for index, (first, count) in enumerate(tiles):
 
@@ -1234,199 +1252,118 @@
             grad = matmul_nt(cots[here, :], down_w[rows_here, :])
             sigmoid = jax.nn.sigmoid(gate)
             silu = gate * sigmoid
-            mixed[here, lanes] = (silu * up).astype(bf16)
-            g_gate[here, lanes] = (grad * up * sigmoid * (1.0 + gate * (1.0 - sigmoid))).astype(
-                bf16
-            )
-            g_up[here, lanes] = (grad * silu).astype(bf16)
-            if index == 2:
-
-                @pl.when(tick == 0)
-                def _():
-                    onward(0)
-
-                @pl.when(tick == 1)
-                def _():
-                    onward(2)
-
-                @pl.when(tick == 3)
-                def _():
-                    sum_mids(1)
-
+            hidden_parts[slot, 0, :, lanes] = (silu * up).astype(bf16)
+            hidden_parts[slot, 1, :, lanes] = (
+                grad * up * sigmoid * (1.0 + gate * (1.0 - sigmoid))
+            ).astype(bf16)
+            hidden_parts[slot, 2, :, lanes] = (grad * silu).astype(bf16)
         for copy in left_copies(tick):
             copy.start()
-        for first, count in lane_tiles:
-            lanes = slice(first, first + count)
-            total = matmul(g_gate[here, :hidden], gate_w[:, lanes])
-            total = total + matmul(g_up[here, :hidden], up_w[:, lanes])
-            parts[here, lanes] = total.astype(bf16)
-
-        @pl.when(tick == 0)
-        def _():
-            onward(1)
+        own = jnp.where(tick == 0, 1.0, 0.0)
+        for first in range(0, D, 512):
+            lanes = slice(first, first + 512)
+            total = matmul(hidden_parts[slot, 0, :, :hidden], down_w[:, lanes])
+            shares[shard, :, lanes] = (total + hid[:, lanes] * own).astype(bf16)
 
         @pl.when(tick == 1)
         def _():
-            onward(3)
-            onward(4)
-            sum_ends(0)
-            sum_ends(1)
+            line.left_end(0)
+            line.right_end(1)
 
         @pl.when(tick == 2)
         def _():
-            sum_ends(2)
-            sum_ends(3)
-            sum_mids(0)
-
-        @pl.when(tick == 3)
-        def _():
-            sum_ends(4)
-            sum_ends(5)
-            sum_mids(2)
-            sum_mids(3)
-
-        @pl.when(tick >= 2)
-        def _():
-            for copy in out_copies(tick - 2):
-                copy.wait()
-
-        own = jnp.where(tick == 0, 1.0, 0.0)
-        for first, count in lane_tiles:
-            lanes = slice(first, first + count)
-            total = matmul(mixed[here, :hidden], down_w[:, lanes]) + hid[:, lanes] * own
-            stage[lax.rem(tick, 2), :, lanes] = total.astype(bf16)
-        for copy in out_copies(tick):
-            copy.start()
-
-    for slot in range(2):
-        right_copy(slot).start()
-    sum_mids(4)
-    sum_mids(5)
-
-    for h in range(2):
-        for c in range(LINE):
-
-            @pl.when(col == c)
-            def _():
-                for way in ways(c):
-                    place = 2 * c + h if way == 1 else 2 * LINE + h
-                    remote(
-                        coming.at[place],
-                        coming.at[place],
-                        rs_send.at[0],
-                        rs_recv.at[place],
-                        partner,
-                    ).wait_recv()
-
-    width = aux_all.shape[2]
-    squares = jnp.zeros((part, 1), f32)
-    inner = jnp.zeros((part, 1), f32)
-    for shard in range(LINE):
-        lanes = slice(shard * width, (shard + 1) * width)
-        middle = hid[:, lanes]
-        from_left = jnp.concatenate([coming[2 * col + h, :, lanes] for h in range(2)])
-        from_right = jnp.concatenate([coming[2 * LINE + h, :, lanes] for h in range(2)])
-        total = parts[:part, lanes].astype(f32) + from_left.astype(f32)
-        total = total + from_right.astype(f32)
-        grad_mid[:, lanes] = total
-        squares = squares + jnp.sum(middle * middle, axis=1, keepdims=True)
-        scaled = total * aux_all[shard, 1:2, :]
-        inner = inner + jnp.sum(scaled * middle, axis=1, keepdims=True)
-    inverse = lax.rsqrt(squares / D + eps)
-    factor = inverse * inverse * inverse * inner / D
-    for shard in range(LINE):
-        lanes = slice(shard * width, (shard + 1) * width)
-        middle, total = hid[:, lanes], grad_mid[:, lanes]
-        gain = jnp.sum(total * middle * inverse, axis=0, keepdims=True)
-        grad_gain[:, lanes] = jnp.broadcast_to(gain, (8, width))
-        grad_mid[:, lanes] = (
-            cots[:part, lanes].astype(f32)
-            + inverse * total * aux_all[shard, 1:2, :]
-            - middle * factor
-        )
-
-    for slot in range(2):
-        right_copy(slot).wait()
-
-    @pl.loop(0, LINE)
-    def _(tick):
+            line.left_end(1)
+            line.right_end(0)
+            line.near_left(0)
+            line.near_right(1)
+
+    rest_copies = [
+        pltpu.make_async_copy(shares.at[shard], out_rest.at[k], out_sem.at[2 + k])
+        for k, shard in enumerate((0, LINE - 1))
+    ]
+    for copy in rest_copies:
+        copy.start()
+    n2_copy = pltpu.make_async_copy(n2s, n2_out, n2_sem)
+    n2_copy.start()
+    line.near_left(1)
+    line.near_right(0)
+    for chunk in range(2):
+        line.far(chunk)
+    result_copies = []
+    for chunk in range(2):
+        stage[chunk] = line.own(chunk).astype(bf16)
+        result_copies.append(
+            pltpu.make_async_copy(
+                stage.at[chunk], result.at[pl.ds((chunk + 1) * part, part)], out_sem.at[chunk]
+            )
+        )
+        result_copies[chunk].start()
+    for tick in (LINE - 2, LINE - 1):
         for copy in left_copies(tick):
             copy.wait()
-
-    for tick in (LINE - 2, LINE - 1):
-        for copy in out_copies(tick):
-            copy.wait()
-    for c in range(LINE):
-
-        @pl.when(col == c)
-        def _():
-            for way in ways(c):
-                hand_on(c, way, 2 * c, n2.at[pl.ds(0, piece)]).wait_send()
-                if c in (0, LINE - 1):
-                    hand_on(c, way, 2 * c + 1, n2.at[pl.ds(piece, piece)]).wait_send()
-                for q in ONWARD[way][c]:
-                    hand_on(c, way, q).wait_send()
-            for q, way in SUMS[c]:
-                sum_copy(c, q, way).wait_send()
-
-
-def mlp(n2, cot_full, hid, aux_all, own, peer):
-    f32, bf16 = jnp.float32, jnp.bfloat16
+    n2_copy.wait()
+    chain.finish()
+    line.finish()
+    for copy in rest_copies + result_copies:
+        copy.wait()
+
+
+def mlp(n2, cot_full, hid, own, peer):
+    bf16 = jnp.bfloat16
     rows = cot_full.shape[0]
     part = n2.shape[0]
-    hidden, half = own[0].shape
+    hidden = own[0].shape[0]
     shape = jax.ShapeDtypeStruct
     dma = pltpu.SemaphoreType.DMA
-    outs = [(shape((rows, D), bf16), any_spec())]
     padded = -(-hidden // TILE) * TILE
-    outs += [(shape((3, rows, padded), bf16), any_spec())]
-    outs += [(shape((2, rows, D), bf16), any_spec())]
-    outs += [(shape((part, D), f32), vmem_spec()), (shape((8, D), f32), vmem_spec())]
     wide = pltpu.VMEM((hidden, D), bf16)
-    tall = pltpu.VMEM((rows, padded), bf16)
     full = pltpu.VMEM((rows, D), bf16)
     return pl.pallas_call(
         mlp_kernel,
-        out_shape=[o[0] for o in outs],
-        in_specs=[any_spec(), any_spec(), vmem_spec(), vmem_spec()] + [any_spec()] * 6,
-        out_specs=[o[1] for o in outs],
+        out_shape=[
+            shape((3, rows, padded), bf16),
+            shape((rows, D), bf16),
+            shape((rows, D // LINE), bf16),
+            shape((2, part, D), bf16),
+        ],
+        in_specs=[any_spec()] * 2 + [vmem_spec()] + [any_spec()] * 6,
+        out_specs=[any_spec()] * 4,
         scratch_shapes=[
             wide,
             wide,
             wide,
-            tall,
-            tall,
-            tall,
+            pltpu.VMEM((2, 3, part, padded), bf16),
             full,
             full,
-            full,
-            pltpu.VMEM((2 * LINE + 2, part // 2, D), bf16),
-            pltpu.VMEM((2, part, D), bf16),
             dma((len(hidden_tiles(hidden)), 6)),
-            dma((2 * LINE,)),
+            dma((LINE,)),
             dma,
-            dma((2, 2 * LINE)),
-            dma((2 * LINE,)),
-            dma((2 * LINE,)),
-            dma((2 * LINE + 2,)),
-            dma((2, 2)),
-            dma((LINE, 3)),
-            dma((2,)),
+            dma((2, LINE - 1, 2)),
+            dma((LINE, 2)),
+            dma((2, 3)),
+            dma,
+            pltpu.VMEM((LINE, part, D), bf16),
+            pltpu.VMEM((LINE + 1, 2, part, D // LINE), bf16),
+            pltpu.VMEM((2, part, D // LINE), bf16),
+            dma((LINE, 2)),
+            dma((LINE + 1, 2)),
+            dma((4,)),
         ],
         compiler_params=pltpu.CompilerParams(
-            collective_id=2, has_side_effects=True, vmem_limit_bytes=62 * 2**20
+            collective_id=2, has_side_effects=True, vmem_limit_bytes=56 * 2**20
         ),
         cost_estimate=pl.CostEstimate(
-            flops=64 * 10**9, bytes_accessed=60 * 10**6, transcendentals=10**7
+            flops=21 * 10**9, bytes_accessed=60 * 10**6, transcendentals=10**7
         ),
         name="mlp",
-    )(n2, cot_full, hid, aux_all, *own, *peer)
+    )(n2, cot_full, hid, *own, *peer)
 
 
 CHUNK = 320
 TAIL = 960
-LAG = 2
-RING = 12
+LAG = 1
+RING = 7
+HALF_TILE = 384
 
 
 class AllReduce:
@@ -1528,24 +1465,18 @@
                             self.copy(chunk, kind, sent, True).wait_send()
 
 
-class RowChain(Chain):
-    def block(self, shard, chunk):
-        shard_rows = self.full.shape[0] // self.count
-        count = shard_rows // self.chunks
-        return self.full.at[rows_at(shard * shard_rows + chunk * count, count)]
-
-    def copy(self, way, step, shard, chunk):
-        self.rows = self.full.shape[0] // self.count // self.chunks
-        return super().copy(way, step, shard, chunk)
-
-
 def back_kernel(
     heads,
     lefts,
-    rights,
-    grad_mid,
+    n2_in,
+    cot_in,
+    hid_in,
+    rest_in,
+    own_gate,
+    own_up,
+    peer_gate,
+    peer_up,
     aux_all,
-    gain_in,
     wof_in,
     wall_in,
     n1_in,
@@ -1557,7 +1488,9 @@
     trig_in,
     attl_in,
     lengths,
+    result_in,
     grad_x,
+    result,
     sums_out,
     gq_out,
     gkv_out,
@@ -1568,37 +1501,40 @@
     got_buf,
     tiles,
     y,
-    big,
-    wall,
-    x,
+    wt,
+    acc,
+    parts,
+    boxes,
     kv,
     q,
-    att,
-    lse,
-    trig,
     att_low,
+    mid,
     low,
     ga_send,
     ga,
-    dkv,
     kv_give,
     kv_got,
-    mate_give,
     mate_got,
-    gqk,
-    gn1,
+    gkv,
     gain_sum,
     gains,
     gains_got,
     load_sem,
     y_sem,
     tile_sem,
+    wt_sem,
+    att_sem,
     credit,
+    free_sem,
     swap_send,
     swap_recv,
     ar_send,
     ar_recv,
-    result_sem,
+    own_sem,
+    gn_send,
+    gn_recv,
+    out_send,
+    out_recv,
     ga_ssem,
     ga_rsem,
     gm_send,
@@ -1610,15 +1546,17 @@
     gain_ssem,
     gain_rsem,
     end_sem,
+    rest_sem,
+    wall_sem,
 ):
     f32, bf16 = jnp.float32, jnp.bfloat16
     dp, row, col = lax.axis_index("dp"), lax.axis_index("row"), lax.axis_index("col")
     place = (dp, row, col)
-    part = grad_mid.shape[0]
+    part = hid_in.shape[0]
     rows = LINE * part
     width = heads * HEAD_WIDTH
     half = TILE
-    hidden = (total.shape[0] - TAIL) // 3
+    hidden = own_gate.shape[0]
     member = lax.rem(col, 2)
     mate = (dp, row, col + 1 - 2 * member)
     partner = (dp, 1 - row, col)
@@ -1629,39 +1567,109 @@
         + [partner, (dp + 1 - 2 * bit_x, row, col), (dp + 2 - 4 * bit_y, row, col)]
     )
     chunks = total.shape[0] // CHUNK
-    reduce = AllReduce(place, total, inbox, ar_send, ar_recv, sums_out, result_sem, chunks)
-
-    y_copies = [pltpu.make_async_copy(rights.at[k], y.at[k], y_sem.at[k]) for k in range(2)]
-
-    def tile_copy(index):
+    reduce = AllReduce(place, total, inbox, ar_send, ar_recv, sums_out, own_sem, chunks)
+
+    n2_copy = pltpu.make_async_copy(n2_in, y.at[0], y_sem.at[0])
+    cot_copy = pltpu.make_async_copy(cot_in, y.at[1], y_sem.at[1])
+    rest_copies = [
+        pltpu.make_async_copy(rest_in.at[k], y.at[1, pl.ds(k * part, part)], rest_sem.at[k])
+        for k in range(2)
+    ]
+
+    products, early, jobs = 6, 3, 9
+    steps = products + jobs - early
+
+    def tile_copy(step):
+        job = jnp.where(step < products, step, step - products + early)
         return pltpu.make_async_copy(
-            lefts.at[index // 3, :, lanes_at(lax.rem(index, 3) * TILE, TILE)],
-            tiles.at[lax.rem(index, 3)],
-            tile_sem.at[lax.rem(index, 3)],
-        )
-
-    y_copies[0].start()
-    for index in range(3):
-        tile_copy(index).start()
-    y_copies[1].start()
+            lefts.at[lax.rem(job // 3 + 1, 3), :, lanes_at(lax.rem(job, 3) * TILE, TILE)],
+            tiles.at[lax.rem(step, 3)],
+            tile_sem.at[lax.rem(step, 3)],
+        )
+
+    def weight_copies(index, act):
+        slot = lax.rem(index, 2)
+        last = hidden - 2 * TILE
+        for k, pair in enumerate(((own_gate, peer_gate), (own_up, peer_up))):
+            for tail, count in ((0, TILE), (1, last)):
+
+                @pl.when((index // 3 == k) & (lax.rem(index, 3) // 2 == tail))
+                def _():
+                    here = rows_at(lax.rem(index, 3) * TILE, count)
+                    for n, (side, src) in enumerate(((row, pair[0]), (1 - row, pair[1]))):
+                        dst = wt.at[slot, pl.ds(0, count), lanes_at(side * half, half)]
+                        act(pltpu.make_async_copy(src.at[here], dst, wt_sem.at[slot, n]))
+
+    for copy in rest_copies:
+        copy.start()
+    tile_copy(0).start()
+    weight_copies(jnp.int32(0), lambda copy: copy.start())
+    n2_copy.start()
+    weight_copies(jnp.int32(1), lambda copy: copy.start())
+    for step in range(1, 3):
+        tile_copy(step).start()
     loads = [
         pltpu.make_async_copy(src, dst, load_sem.at[k])
         for k, (src, dst) in enumerate(
             (
-                (wof_in, big),
-                (wall_in, wall),
-                (x_in, x),
+                (hid_in, mid),
                 (kv_in, kv),
                 (q_in, q),
-                (att_in, att),
-                (lse_in, lse),
-                (trig_in, trig),
                 (attl_in, att_low),
             )
         )
     ]
     for copy in loads:
         copy.start()
+    acc[...] = jnp.zeros_like(acc)
+
+    grain = part // LINE
+
+    gn = LineSum(
+        place,
+        lambda chunk, shard: parts.at[rows_at(shard * part + chunk * grain, grain)],
+        lambda slot, chunk: boxes.at[slot, rows_at(chunk * grain, grain)],
+        gn_send,
+        gn_recv,
+        LINE,
+    )
+    def out_box(slot, chunk):
+        if isinstance(slot, int) and slot == LINE:
+            return ga_send.at[chunk]
+        place_of = slot * 2 + chunk
+        return y.at[
+            1,
+            rows_at(2 * part + place_of // LINE * part, part),
+            lanes_at(lax.rem(place_of, LINE) * width, width),
+        ]
+
+    out = LineSum(
+        place,
+        lambda chunk, shard: y.at[1, rows_at(chunk * part, part), lanes_at(shard * width, width)],
+        out_box,
+        out_send,
+        out_recv,
+        2,
+    )
+    fin = LineSum(
+        place,
+        lambda chunk, shard: wt.at[
+            chunk // 2, rows_at(lax.rem(chunk, 2) * part, part), lanes_at(shard * width, width)
+        ],
+        lambda slot, chunk: tiles.at[
+            slot // 2, rows_at(chunk * part, part), lanes_at(lax.rem(slot, 2) * width, width)
+        ],
+        fin_send,
+        fin_recv,
+        LINE,
+    )
+
+    gn.clear_ends()
+    out.clear_ends()
+    for copy in rest_copies:
+        copy.wait()
+    for chunk in range(2):
+        out.ends(chunk)
 
     theirs, ours = lanes_at((1 - row) * half, half), lanes_at(row * half, half)
 
@@ -1675,78 +1683,264 @@
             partner,
         )
 
-    jobs = 9
-    y_copies[0].wait()
-
-    @pl.loop(0, jobs + 1)
-    def _(index):
-        @pl.when(index == 3)
-        def _():
-            y_copies[1].wait()
-
-        @pl.when(index < jobs)
-        def _():
-            tile_copy(index).wait()
-
-            @pl.when(index >= 2)
+    n2_copy.wait()
+
+    @pl.loop(0, steps + 1)
+    def _(step):
+        @pl.when(step < steps)
+        def _():
+            tile_copy(step).wait()
+
+        @pl.when(step < products)
+        def _():
+            weight_copies(step, lambda copy: copy.wait())
+
+            @pl.loop(0, 2)
+            def _(side):
+                here = rows_at(side * 2 * part, 2 * part)
+                for lane in range(0, D, 512):
+                    lanes = slice(lane, lane + 512)
+                    acc[here, lanes] += matmul(
+                        tiles[lax.rem(step, 3), here, :], wt[lax.rem(step, 2), :, lanes]
+                    )
+
+            @pl.when(step + 2 < products)
+            def _():
+                weight_copies(step + 2, lambda copy: copy.start())
+
+        @pl.when(step == products)
+        def _():
+            @pl.loop(0, LINE)
+            def _(shard):
+                here = rows_at(shard * part, part)
+                parts[here, :] = acc[here, :].astype(bf16)
+
+            @pl.loop(0, LINE)
+            def _(chunk):
+                gn.ends(chunk)
+
+        @pl.when((step < early) | ((step >= products) & (step < steps)))
+        def _():
+            job = jnp.where(step < early, step, step - products + early)
+
+            @pl.when(job >= 2)
             def _():
                 pl.semaphore_wait(credit, 1)
-                swap_copy(index - 2).wait_send()
-
-            side = jnp.minimum(index // 3, 1)
-            product = matmul_tn(tiles[lax.rem(index, 3)], y[side, :, theirs])
-            give_buf[rows_at(lax.rem(index, 2) * TILE, TILE), :] = product.astype(bf16)
-            swap_copy(index).start()
-
-        @pl.when(index >= 1)
-        def _():
-            last = index - 1
-            side = jnp.minimum(last // 3, 1)
-            product = matmul_tn(tiles[lax.rem(last, 3)], y[side, :, ours])
-            swap_copy(last).wait_recv()
-            product = product + got_buf[rows_at(lax.rem(last, 2) * TILE, TILE), :].astype(f32)
-            first = (last // 3) * hidden + lax.rem(last, 3) * TILE
-            total[rows_at(first, TILE), :] = product.astype(bf16)
+                swap_copy(job - 2).wait_send()
+
+            for first in range(0, TILE, HALF_TILE):
+                lanes = slice(first, first + HALF_TILE)
+                product = matmul_tn(tiles[lax.rem(step, 3), :, lanes], y[job // 6, :, theirs])
+                here = rows_at(lax.rem(job, 2) * TILE + first, HALF_TILE)
+                give_buf[here, :] = product.astype(bf16)
+            swap_copy(job).start()
+
+        @pl.when(((step >= 1) & (step <= early)) | (step >= products + 1))
+        def _():
+            job = jnp.where(step <= early, step - 1, step - products + early - 1)
+            swap_copy(job).wait_recv()
+            base_row = (job // 3) * hidden + lax.rem(job, 3) * TILE
+            for first in range(0, TILE, HALF_TILE):
+                lanes = slice(first, first + HALF_TILE)
+                product = matmul_tn(tiles[lax.rem(step + 2, 3), :, lanes], y[job // 6, :, ours])
+                here = rows_at(lax.rem(job, 2) * TILE + first, HALF_TILE)
+                product = product + got_buf[here, :].astype(f32)
+                total[rows_at(base_row + first, HALF_TILE), :] = product.astype(bf16)
             pl.semaphore_signal(credit, inc=1, device_id=partner, device_id_type=MESH)
 
-            @pl.when(last + 3 < jobs)
+        @pl.when((step >= 1) & (step + 2 < steps))
+        def _():
+            tile_copy(step + 2).start()
+
+        for number, when in enumerate((1, 2, 3, 5, 7, 9, 11)):
+
+            @pl.when(step == when)
             def _():
-                tile_copy(last + 3).start()
-
-        @pl.when(lax.rem(index, 2) == 1)
-        def _():
-            reduce.step(index // 2)
-
+                reduce.step(number)
+
+        @pl.when(step == 3)
+        def _():
+            out.near(0)
+
+        @pl.when(step == 5)
+        def _():
+            out.near(1)
+            out.far(0)
+
+        @pl.when(step == 7)
+        def _():
+            gn.near(0)
+            out.far(1)
+            out.finish()
+            for chunk in range(2):
+                low[:, chunk * width : (chunk + 1) * width] = out.own(chunk).astype(bf16)
+            cot_copy.start()
+
+        @pl.when(step == 8)
+        def _():
+            cot_copy.wait()
+
+        @pl.when(step == 10)
+        def _():
+            gn.near(1)
+            gn.far(0)
+
+        @pl.when(step == 12)
+        def _():
+            gn.near(2)
+            gn.far(1)
+
+    wof_copies = [
+        pltpu.make_async_copy(
+            wof_in.at[shard],
+            wt.at[shard // 2, pl.ds(shard % 2 * width, width)],
+            att_sem.at[shard],
+        )
+        for shard in range(LINE)
+    ]
+    for copy in wof_copies:
+        copy.start()
+    own_rows = rows_at(col * part, part)
+    rest_copies = [
+        pltpu.make_async_copy(
+            low.at[:, pl.ds(chunk * width, width)],
+            result.at[pl.ds(chunk * (LINE - 1) * part, part)],
+            rest_sem.at[chunk],
+        )
+        for chunk in range(2)
+    ]
+    for copy in rest_copies:
+        copy.start()
+    for copy in rest_copies:
+        copy.wait()
+    low[...] = y[1, own_rows, :]
+    n1_copy = pltpu.make_async_copy(n1_in, y.at[1], y_sem.at[1])
+    n1_copy.start()
     for copy in loads:
         copy.wait()
-    for piece in range(LINE):
-        lanes = slice(piece * width, (piece + 1) * width)
-        low[:, lanes] = grad_mid[:, lanes].astype(bf16)
+    gn.near(3)
+    gn.far(2)
+    reduce.step(7)
+    gn.far(3)
+    reduce.step(8)
+
+    gain_sum[...] = jnp.zeros_like(gain_sum)
+
+    @pl.loop(0, LINE)
+    def _(chunk):
+        gn.wait_own(chunk)
+        here = rows_at(chunk * grain, grain)
+        squares = jnp.zeros((grain, 1), f32)
+        inner = jnp.zeros((grain, 1), f32)
+        grads = []
+        for shard in range(LINE):
+            lanes = slice(shard * width, (shard + 1) * width)
+            middle = mid[here, lanes]
+            grad = parts[rows_at(col * part + chunk * grain, grain), lanes].astype(f32)
+            grad = grad + boxes[col, here, lanes].astype(f32)
+            grad = grad + boxes[LINE, here, lanes].astype(f32)
+            grads.append(grad)
+            squares = squares + jnp.sum(middle * middle, axis=1, keepdims=True)
+            inner = inner + jnp.sum(
+                grad * aux_all[shard, 1:2, :] * middle, axis=1, keepdims=True
+            )
+        inverse = lax.rsqrt(squares / D + eps)
+        factor = inverse * inverse * inverse * inner / D
+        for shard in range(LINE):
+            lanes = slice(shard * width, (shard + 1) * width)
+            middle, grad = mid[here, lanes], grads[shard]
+            gain_sum[1:2, lanes] += jnp.sum(grad * middle * inverse, axis=0, keepdims=True)
+            new = inverse * grad * aux_all[shard, 1:2, :] - middle * factor
+            new = new + low[here, lanes].astype(f32)
+            mid[here, lanes] = new
+            low[here, lanes] = new.astype(bf16)
+
+    @pl.when(col > 0)
+    def _():
+        pl.semaphore_signal(
+            free_sem.at[1], inc=1, device_id=(dp, row, col - 1), device_id_type=MESH
+        )
+
+    @pl.when(col < LINE - 1)
+    def _():
+        pl.semaphore_signal(
+            free_sem.at[0], inc=1, device_id=(dp, row, col + 1), device_id_type=MESH
+        )
 
     def ga_copy(k):
         to = lax.rem(col + k, LINE)
         return remote(
             ga_send.at[k - 1],
-            ga.at[rows_at(col * part, part)],
+            ga.at[own_rows],
             ga_ssem.at[k - 1],
             ga_rsem.at[k - 1],
             (dp, row, to),
         )
 
+    for copy in wof_copies:
+        copy.wait()
     for k in (1, 2, 3, 0):
         shard = lax.rem(col + k, LINE)
-        block = matmul_nt(low[...], big[shard]).astype(bf16)
+        weights = wt[shard // 2, rows_at(lax.rem(shard, 2) * width, width), :]
+        block = matmul_nt(low[...], weights).astype(bf16)
         if k:
             ga_send[k - 1] = block
             ga_copy(k).start()
         else:
-            ga[rows_at(col * part, part), :] = block
-    n1_copy = pltpu.make_async_copy(n1_in, y.at[1], y_sem.at[1])
-    reduce.step(5)
+            ga[own_rows, :] = block
+    reduce.step(9)
+
+    held = [att_in.at[h] for h in range(heads)] + [trig_in.at[0], trig_in.at[1], lse_in]
+    att_copies = [
+        pltpu.make_async_copy(src, acc.at[:, pl.ds(512 + k * HEAD_WIDTH, HEAD_WIDTH)], att_sem.at[k])
+        for k, src in enumerate(held)
+    ]
+    trig_lanes = [
+        slice(512 + (heads + k) * HEAD_WIDTH, 512 + (heads + k + 1) * HEAD_WIDTH) for k in range(2)
+    ]
+    lse_lanes = 512 + (heads + 2) * HEAD_WIDTH
+    for copy in att_copies:
+        copy.start()
+    acc[:, :512] = jnp.zeros((rows, 512), f32)
+    gn.finish()
+    wall_width = width + 2 * HEAD_WIDTH
+    wall_copies = [
+        pltpu.make_async_copy(
+            wall_in.at[pl.ds(shard * width, width)],
+            parts.at[
+                pl.ds(shard % 2 * width, width), pl.ds(shard // 2 * wall_width, wall_width)
+            ],
+            wall_sem.at[shard],
+        )
+        for shard in range(LINE)
+    ]
+    for copy in wall_copies:
+        copy.start()
+    y[0, own_rows, :] = low[...]
+
+    chain = RowChain(place, low, y.at[0], gm_send, gm_recv, LINE, 2)
+
+    @pl.when(col > 0)
+    def _():
+        pl.semaphore_wait(free_sem.at[0], 1)
+
+    @pl.when(col < LINE - 1)
+    def _():
+        pl.semaphore_wait(free_sem.at[1], 1)
+
+    for chunk in range(2):
+        chain.start_own(chunk)
 
     span = min(512, rows)
-    dkv[...] = jnp.zeros_like(dkv)
-    chain = RowChain(place, low, y.at[0], gm_send, gm_recv, LINE, 2)
+    per_side = rows // span
+    for copy in att_copies:
+        copy.wait()
+
+    def key_rows(index):
+        return rows_at(lax.rem(index, per_side) * span, span)
+
+    def key_lanes(index, which):
+        return lanes_at(index // per_side * 2 * HEAD_WIDTH + which * HEAD_WIDTH, HEAD_WIDTH)
 
     @pl.loop(0, LINE)
     def _(turn):
@@ -1763,11 +1957,19 @@
         back = jnp.concatenate(
             [ga[here, h * HEAD_WIDTH : (h + 1) * HEAD_WIDTH] for h in range(heads)], axis=0
         )
-        attended = att[:, here, :].reshape(heads * part, HEAD_WIDTH)
-        log_total = jnp.concatenate([lse[here, h : h + 1] for h in range(heads)], axis=0)
+        attended = jnp.concatenate(
+            [
+                acc[here, 512 + h * HEAD_WIDTH : 512 + (h + 1) * HEAD_WIDTH]
+                for h in range(heads)
+            ],
+            axis=0,
+        )
+        log_total = jnp.concatenate(
+            [acc[here, lse_lanes + h : lse_lanes + h + 1] for h in range(heads)], axis=0
+        )
         delta = jnp.sum(back.astype(f32) * attended, axis=1, keepdims=True)
 
-        def body(index, acc):
+        def body(index, grad):
             keys = rows_at(index * span, span)
             key, value = kv[keys, :HEAD_WIDTH], kv[keys, HEAD_WIDTH:]
             scores = matmul_nt(query, key) * SCALE
@@ -1776,133 +1978,113 @@
             probs = jnp.where(allowed[None], probs, 0.0).reshape(heads * part, span)
             grads = matmul_nt(back, value)
             grad_scores = (probs * (grads - delta)).astype(bf16)
-            dkv[keys, :HEAD_WIDTH] += matmul_tn(grad_scores, query)
-            dkv[keys, HEAD_WIDTH:] += matmul_tn(probs.astype(bf16), back)
-            return acc + matmul(grad_scores, key)
+            acc[key_rows(index), key_lanes(index, 0)] += matmul_tn(grad_scores, query)
+            acc[key_rows(index), key_lanes(index, 1)] += matmul_tn(probs.astype(bf16), back)
+            return grad + matmul(grad_scores, key)
 
         blocks = (first_query + part + span - 1) // span
-        acc = lax.fori_loop(0, blocks, body, jnp.zeros((heads * part, HEAD_WIDTH), f32))
-        cosine, sine = trig[0, here, :], -trig[1, here, :]
+        grad = lax.fori_loop(0, blocks, body, jnp.zeros((heads * part, HEAD_WIDTH), f32))
+        cosine, sine = acc[here, trig_lanes[0]], -acc[here, trig_lanes[1]]
         for h in range(heads):
-            grad = acc[h * part : (h + 1) * part] * SCALE
             lanes = slice(h * HEAD_WIDTH, (h + 1) * HEAD_WIDTH)
-            gqk[here, lanes] = rotate(grad, cosine, sine).astype(bf16)
-        reduce.step(6 + turn)
-
-    y[0, rows_at(col * part, part), :] = low[...]
-    for chunk in range(2):
-        chain.start_own(chunk)
-    n1_copy.start()
-
-    other = rows_at((1 - row) * rows, rows)
-    kv_give[...] = dkv[other, :].astype(bf16)
+            turned = rotate(grad[h * part : (h + 1) * part] * SCALE, cosine, sine)
+            ga[here, lanes] = turned.astype(bf16)
+        reduce.step(10 + turn)
+
+        @pl.when(turn == LINE - 1)
+        def _():
+            for chunk in range(2):
+                chain.step(1, chunk)
+
+    kv_give[...] = acc[:, lanes_at((1 - row) * 2 * HEAD_WIDTH, 2 * HEAD_WIDTH)].astype(bf16)
     kv_copy = remote(kv_give, kv_got, kv_sem.at[0], kv_sem.at[1], partner)
     kv_copy.start()
-    reduce.step(10)
-    kv_copy.wait_recv()
+    reduce.step(14)
+    kv_copy.wait()
     lane = lax.broadcasted_iota(jnp.int32, (1, HEAD_WIDTH), 1)
     low_lanes = lane < HEAD_WIDTH // 2
     turn_by = HEAD_WIDTH // 2
+    mate_give = kv_give.at[:, pl.ds(0, HEAD_WIDTH)]
     mate_copy = remote(mate_give, mate_got, mate_sem.at[0], mate_sem.at[1], mate)
+    own_lanes = lanes_at(row * 2 * HEAD_WIDTH, 2 * HEAD_WIDTH)
 
     @pl.loop(0, LINE)
     def _(chunk):
         here = rows_at(chunk * part, part)
-        there = rows_at(row * rows + chunk * part, part)
-        both = dkv[there, :] + kv_got[here, :].astype(f32)
-        key = rotate(both[:, :HEAD_WIDTH] * SCALE, trig[0, here, :], -trig[1, here, :])
+        both = acc[here, own_lanes] + kv_got[here, :].astype(f32)
+        key = rotate(
+            both[:, :HEAD_WIDTH] * SCALE, acc[here, trig_lanes[0]], -acc[here, trig_lanes[1]]
+        )
         value = both[:, HEAD_WIDTH:]
         first = jnp.where(low_lanes, key, pltpu.roll(value, turn_by, 1))
         second = jnp.where(low_lanes, pltpu.roll(key, turn_by, 1), value)
         is_first = jnp.where(member == 0, 1.0, 0.0)
         kept = first * is_first + second * (1.0 - is_first)
         given = second * is_first + first * (1.0 - is_first)
-        dkv[there, :HEAD_WIDTH] = kept
-        mate_give[here, :] = given.astype(bf16)
+        acc[here, 512 : 512 + HEAD_WIDTH] = kept
+        kv_give[here, :HEAD_WIDTH] = given.astype(bf16)
 
     mate_copy.start()
-    for chunk in range(2):
-        chain.step(1, chunk)
-    reduce.step(11)
+    reduce.step(15)
     mate_copy.wait_recv()
 
     @pl.loop(0, LINE)
     def _(chunk):
         here = rows_at(chunk * part, part)
-        there = rows_at(row * rows + chunk * part, part)
-        kept = dkv[there, :HEAD_WIDTH] + mate_got[here, :].astype(f32)
-        gqk[here, width:] = kept.astype(bf16)
-
-    def share_at(chunk, shard):
-        return big.at[chunk, pl.ds(0, part), lanes_at(shard * width, width)]
-
-    def box_rows(slot, chunk):
-        return tiles.at[
-            slot // 2, rows_at(chunk * part, part), lanes_at(lax.rem(slot, 2) * width, width)
-        ]
-
-    def fin_copy(chunk, shard, way):
-        to = col + 1 - 2 * way
-        slot = jnp.where((way == 1) & (shard == to), LINE, shard)
-        return remote(
-            share_at(chunk, shard),
-            box_rows(slot, chunk),
-            fin_send.at[shard, chunk],
-            fin_recv.at[slot, chunk],
-            (dp, row, to),
-        )
-
-    def fin_got(chunk, slot):
-        remote(
-            box_rows(slot, chunk),
-            box_rows(slot, chunk),
-            fin_send.at[0, chunk],
-            fin_recv.at[slot, chunk],
-            partner,
-        ).wait_recv()
-
-    def fin_add(chunk, shard):
-        fin_got(chunk, shard)
-        share = share_at(chunk, shard)
-        share[...] = (share[...].astype(f32) + box_rows(shard, chunk)[...].astype(f32)).astype(bf16)
-
-    def fin_ends(chunk):
-        @pl.when(col == 0)
-        def _():
-            for shard in (3, 2, 1):
-                fin_copy(chunk, shard, 0).start()
-
-        @pl.when(col == LINE - 1)
-        def _():
-            for shard in (0, 1, 2):
-                fin_copy(chunk, shard, 1).start()
-
-    def fin_near(chunk):
+        kept = acc[here, 512 : 512 + HEAD_WIDTH] + mate_got[here, :].astype(f32)
+        gkv[here, :] = kept.astype(bf16)
+
+    n1_copy.wait()
+    base = 3 * hidden
+    first_kv, first_out = half // 2, half // 2 + HEAD_WIDTH
+    first_small = first_out + width
+
+    def projections(side_lanes, store):
+        product = matmul_tn(y[1, :, side_lanes], ga[...])
         for k in range(2):
-
-            @pl.when(col == 1)
-            def _():
-                fin_add(chunk, 3 - k)
-                fin_copy(chunk, 3 - k, 0).start()
-
-            @pl.when(col == 2)
-            def _():
-                fin_add(chunk, k)
-                fin_copy(chunk, k, 1).start()
-
-    def fin_far(chunk):
-        @pl.when(col == 1)
-        def _():
-            fin_add(chunk, 0)
-            fin_copy(chunk, 0, 1).start()
-
-        @pl.when(col == 2)
-        def _():
-            fin_add(chunk, 3)
-            fin_copy(chunk, 3, 0).start()
-
-    gain_sum[...] = jnp.zeros_like(gain_sum)
-    kv_lanes = lanes_at(width + member * HEAD_WIDTH, HEAD_WIDTH)
+            store(
+                0,
+                half // 2,
+                slice(k * width, (k + 1) * width),
+                product[k * half // 2 : (k + 1) * half // 2],
+            )
+        product = matmul_tn(y[1, :, side_lanes], gkv[...])
+        for k in range(half // HEAD_WIDTH):
+            store(
+                first_kv,
+                HEAD_WIDTH,
+                slice(k * HEAD_WIDTH, (k + 1) * HEAD_WIDTH),
+                product[k * HEAD_WIDTH : (k + 1) * HEAD_WIDTH],
+            )
+
+    for k in range(2):
+        swap_copy(jobs - 2 + k).wait_send()
+    pl.semaphore_wait(credit, 2)
+
+    def store_give(first, count, lanes, value):
+        give_buf[first : first + count, lanes] = value.astype(bf16)
+
+    def store_keep(first, count, lanes, value):
+        got = got_buf[first : first + count, lanes].astype(f32)
+        total[base + first : base + first + count, lanes] = (got + value).astype(bf16)
+
+    projections(theirs, store_give)
+    tail = pl.ds(0, first_out)
+    tail_copy = remote(give_buf.at[tail], got_buf.at[tail], end_sem.at[0], end_sem.at[1], partner)
+    tail_copy.start()
+    for chunk in range(2):
+        chain.step(2, chunk)
+    reduce.step(16)
+    tail_copy.wait_recv()
+    projections(ours, store_keep)
+    x_copy = pltpu.make_async_copy(x_in, y.at[1], y_sem.at[1])
+    x_copy.start()
+
+    fin.clear_ends()
+
+    for copy in wall_copies:
+        copy.wait()
+    x_copy.wait()
 
     @pl.loop(0, LINE + 2)
     def _(chunk):
@@ -1913,37 +2095,39 @@
             inner = jnp.zeros((part, 1), f32)
             for shard in range(LINE):
                 lanes = slice(shard * width, (shard + 1) * width)
-                grad = matmul_nt(gqk[here, :width], wall[lanes, :width])
-                grad = grad + matmul_nt(gqk[here, width:], wall[lanes, kv_lanes])
-                gn1[:, lanes] = grad
-                value = x[here, lanes].astype(f32)
+                there = slice(shard % 2 * width, (shard % 2 + 1) * width)
+                first = shard // 2 * wall_width
+                kv_lanes = lanes_at(first + width + member * HEAD_WIDTH, HEAD_WIDTH)
+                grad = matmul_nt(ga[here, :], parts[there, first : first + width])
+                grad = grad + matmul_nt(gkv[here, :], parts[there, kv_lanes])
+                acc[:part, lanes] = grad
+                value = y[1, here, lanes].astype(f32)
                 squares = squares + jnp.sum(value * value, axis=1, keepdims=True)
                 scaled = grad * aux_all[shard, 0:1, :]
                 inner = inner + jnp.sum(scaled * value, axis=1, keepdims=True)
             inverse = lax.rsqrt(squares / D + eps)
             factor = inverse * inverse * inverse * inner / D
             own = jnp.where(chunk == col, 1.0, 0.0)
+            there = rows_at(lax.rem(chunk, 2) * part, part)
             for shard in range(LINE):
                 lanes = slice(shard * width, (shard + 1) * width)
-                grad, value = gn1[:, lanes], x[here, lanes].astype(f32)
-                gain_sum[:, lanes] += jnp.sum(grad * value * inverse, axis=0, keepdims=True)
-                result = inverse * grad * aux_all[shard, 0:1, :] - value * factor
-                result = result + grad_mid[:, lanes] * own
-                big[chunk, :part, lanes] = result.astype(bf16)
-            fin_ends(chunk)
+                grad, value = acc[:part, lanes], y[1, here, lanes].astype(f32)
+                gain_sum[0:1, lanes] += jnp.sum(grad * value * inverse, axis=0, keepdims=True)
+                share = inverse * grad * aux_all[shard, 0:1, :] - value * factor
+                share = share + mid[:, lanes] * own
+                wt[chunk // 2, there, lanes] = share.astype(bf16)
+            fin.ends(chunk)
+            reduce.step(17 + chunk)
 
         @pl.when((chunk >= 1) & (chunk <= LINE))
         def _():
-            fin_near(chunk - 1)
+            fin.near(chunk - 1)
 
         @pl.when(chunk >= 2)
         def _():
-            fin_far(chunk - 2)
-
-        reduce.step(12 + chunk)
-
-    gains[...] = gain_in[...]
-    gains[0:1, :] = gain_sum[...]
+            fin.far(chunk - 2)
+
+    gains[...] = gain_sum[...]
 
     def gain_copy(k):
         to = lax.rem(col + k, LINE)
@@ -1957,21 +2141,15 @@
 
     for k in range(1, LINE):
         gain_copy(k).start()
-
-    for step in (2, 3):
-        for chunk in range(2):
-            chain.step(step, chunk)
-    n1_copy.wait()
-    reduce.step(18)
+    reduce.step(21)
+    bias = jnp.concatenate(
+        [jnp.sum(ref[...].astype(f32), axis=0, keepdims=True) for ref in (ga, gkv)], axis=1
+    )
     for k in range(1, LINE):
         gain_copy(k).wait_recv()
     gain_total = gains[:, lanes_at(col * width, width)]
     for k in range(1, LINE):
         gain_total = gain_total + gains_got[k - 1]
-    bias = jnp.zeros((1, width + HEAD_WIDTH), f32)
-    for chunk in range(LINE):
-        piece = gqk[chunk * part : (chunk + 1) * part, :].astype(f32)
-        bias = bias + jnp.sum(piece, axis=0, keepdims=True)
     small = jnp.concatenate(
         [
             jnp.concatenate([gain_total, jnp.zeros((8, half - width), f32)], axis=1),
@@ -1985,76 +2163,41 @@
         ],
         axis=0,
     )
-    base = 3 * hidden
-    first_q, first_kv, first_small = width, width + half // 2, width + half // 2 + HEAD_WIDTH
-
-    def projections(side_lanes, store):
-        store(0, width, slice(0, half), matmul_tn(att_low[...], y[0, :, side_lanes]))
-        product = matmul_tn(y[1, :, side_lanes], gqk[...])
-        for k in range(2):
-            store(
-                first_q,
-                half // 2,
-                slice(k * width, (k + 1) * width),
-                product[k * half // 2 : (k + 1) * half // 2, :width],
-            )
-        for k in range(half // HEAD_WIDTH):
-            store(
-                first_kv,
-                HEAD_WIDTH,
-                slice(k * HEAD_WIDTH, (k + 1) * HEAD_WIDTH),
-                product[k * HEAD_WIDTH : (k + 1) * HEAD_WIDTH, width:],
-            )
-        store(first_small, 16, slice(0, half), small)
-        store(first_small + 16, TAIL - first_small - 16, slice(0, half), None)
-
-    for k in range(2):
-        swap_copy(jobs - 2 + k).wait_send()
-    pl.semaphore_wait(credit, 2)
-
-    def store_give(first, count, lanes, value):
-        if value is None:
-            value = jnp.zeros((count, half), f32)
-        give_buf[first : first + count, lanes] = value.astype(bf16)
-
-    def store_keep(first, count, lanes, value):
-        got = got_buf[first : first + count, lanes].astype(f32)
-        if value is not None:
-            got = got + value
-        total[base + first : base + first + count, lanes] = got.astype(bf16)
-
-    projections(theirs, store_give)
-    tail = pl.ds(0, TAIL)
-    tail_copy = remote(give_buf.at[tail], got_buf.at[tail], end_sem.at[0], end_sem.at[1], partner)
-    tail_copy.start()
-    reduce.step(19)
-    tail_copy.wait_recv()
-    projections(ours, store_keep)
-    reduce.step(20)
-
-    for c in range(LINE):
-
-        @pl.when(col == c)
-        def _():
-            @pl.loop(0, LINE)
-            def _(chunk):
-                here = rows_at(chunk * part, part)
-                result = big[chunk, :part, c * width : (c + 1) * width].astype(f32)
-                if c > 0:
-                    fin_got(chunk, c)
-                    result = result + box_rows(c, chunk)[...].astype(f32)
-                if c < LINE - 1:
-                    fin_got(chunk, LINE)
-                    result = result + box_rows(LINE, chunk)[...].astype(f32)
-                grad_x[here, :] = result.astype(bf16)
-
-    @pl.loop(21, chunks + 4 * LAG)
+    small_rows = pl.ds(first_out, width + 16)
+    for chunk in range(2):
+        chain.step(3, chunk)
+    product = matmul_tn(att_low[...], y[0, :, theirs])
+    give_buf[first_out:first_small, :] = product.astype(bf16)
+    give_buf[first_small : first_small + 16, :] = small.astype(bf16)
+    small_copy = remote(
+        give_buf.at[small_rows], got_buf.at[small_rows], end_sem.at[2], end_sem.at[3], partner
+    )
+    small_copy.start()
+    product = matmul_tn(att_low[...], y[0, :, ours])
+    small_copy.wait_recv()
+    product = product + got_buf[first_out:first_small, :].astype(f32)
+    total[base + first_out : base + first_small, :] = product.astype(bf16)
+    small = small + got_buf[first_small : first_small + 16, :].astype(f32)
+    total[base + first_small : base + first_small + 16, :] = small.astype(bf16)
+    rest = TAIL - first_small - 16
+    total[base + first_small + 16 : base + TAIL, :] = jnp.zeros((rest, half), bf16)
+    for number in (22, 23):
+        reduce.step(number)
+
+    @pl.loop(0, LINE)
+    def _(chunk):
+        ga[rows_at(chunk * part, part), :] = fin.own(chunk).astype(bf16)
+
+    grad_copy = pltpu.make_async_copy(ga, grad_x, att_sem.at[1])
+    grad_copy.start()
+
+    @pl.loop(24, chunks + 4 * LAG)
     def _(number):
         reduce.step(number)
 
     outs = [
         pltpu.make_async_copy(
-            sums_out.at[pl.ds(base + first_q, half // 2), pl.ds(k * width, width)],
+            sums_out.at[pl.ds(base, half // 2), pl.ds(k * width, width)],
             gq_out.at[pl.ds(k * half // 2, half // 2)],
             load_sem.at[k],
         )
@@ -2077,37 +2220,28 @@
         copy.start()
 
     chain.finish()
+    fin.finish()
     for k in range(1, LINE):
         ga_copy(k).wait_send()
         gain_copy(k).wait_send()
-    kv_copy.wait_send()
-    mate_copy.wait_send()
-    tail_copy.wait_send()
-    for c in range(LINE):
-
-        @pl.when(col == c)
-        def _():
-            for shard in range(LINE):
-                if shard != c:
-
-                    @pl.loop(0, LINE)
-                    def _(chunk):
-                        fin_copy(chunk, shard, 0 if shard > c else 1).wait_send()
-
-    for copy in outs:
+    for copy in (mate_copy, tail_copy, small_copy):
+        copy.wait_send()
+    for copy in outs + [grad_copy]:
         copy.wait()
 
 
-def back(lefts, rights, grad_mid, aux_all, gain_in, wof, wall, n1, x, kv, q, att, lse, trig, att_low, lengths, hidden):
+def back(lefts, n2, cot, hid, rest, result, own, peer, aux_all, wof, wall, n1, x, kv, q, att, lse, trig, att_low, lengths):
     f32, bf16 = jnp.float32, jnp.bfloat16
     shape = jax.ShapeDtypeStruct
     dma = pltpu.SemaphoreType.DMA
     heads, rows, _ = q.shape
     width = heads * HEAD_WIDTH
-    part = grad_mid.shape[0]
+    part = hid.shape[0]
+    hidden = own[0].shape[0]
     total_rows = 3 * hidden + TAIL
     outs = [
-        (shape((rows, width), bf16), vmem_spec()),
+        (shape((rows, width), bf16), any_spec()),
+        (shape((rows, width), bf16), any_spec()),
         (shape((total_rows, TILE), bf16), any_spec()),
         (shape((TILE, width), bf16), any_spec()),
         (shape((TILE, HEAD_WIDTH), bf16), any_spec()),
@@ -2117,10 +2251,10 @@
     return pl.pallas_call(
         functools.partial(back_kernel, heads),
         out_shape=[o[0] for o in outs],
-        in_specs=[any_spec()] * 2
-        + [vmem_spec()] * 3
+        in_specs=[any_spec()] * 9
+        + [vmem_spec()]
         + [any_spec()] * 10
-        + [pl.BlockSpec(memory_space=pltpu.SMEM)],
+        + [pl.BlockSpec(memory_space=pltpu.SMEM), any_spec()],
         out_specs=[o[1] for o in outs],
         scratch_shapes=[
             vmem((total_rows, TILE), bf16),
@@ -2129,37 +2263,40 @@
             vmem((2 * TILE, TILE), bf16),
             vmem((3, rows, TILE), bf16),
             vmem((2, rows, D), bf16),
-            vmem(wof.shape, bf16),
-            vmem(wall.shape, bf16),
-            vmem(x.shape, bf16),
+            vmem((2, TILE, D), bf16),
+            vmem((rows, D), f32),
+            vmem((rows, D), bf16),
+            vmem((LINE + 1, part, D), bf16),
             vmem(kv.shape, bf16),
             vmem(q.shape, bf16),
-            vmem(att.shape, f32),
-            vmem(lse.shape, f32),
-            vmem(trig.shape, f32),
             vmem(att_low.shape, bf16),
+            vmem((part, D), f32),
             vmem((part, D), bf16),
             vmem((LINE - 1, part, width), bf16),
             vmem((rows, width), bf16),
-            vmem(kv.shape, f32),
             vmem((rows, 2 * HEAD_WIDTH), bf16),
             vmem((rows, 2 * HEAD_WIDTH), bf16),
             vmem((rows, HEAD_WIDTH), bf16),
             vmem((rows, HEAD_WIDTH), bf16),
-            vmem((rows, width + HEAD_WIDTH), bf16),
-            vmem((part, D), f32),
-            vmem((1, D), f32),
+            vmem((8, D), f32),
             vmem((8, D), f32),
             vmem((LINE - 1, 8, width), f32),
             dma((9,)),
             dma((2,)),
             dma((3,)),
+            dma((2, 2)),
+            dma((6,)),
             pltpu.SemaphoreType.REGULAR,
+            pltpu.SemaphoreType.REGULAR((2,)),
             dma((2,)),
             dma((2,)),
             dma((RING, 2, 5)),
             dma((RING, 2, 5)),
             dma((RING, 2)),
+            dma((LINE, LINE)),
+            dma((LINE + 1, LINE)),
+            dma((LINE, 2)),
+            dma((LINE + 1, 2)),
             dma((LINE - 1,)),
             dma((LINE - 1,)),
             dma((2, LINE - 1, 2)),
@@ -2170,7 +2307,9 @@
             dma((LINE + 1, LINE)),
             dma((LINE - 1,)),
             dma((LINE - 1,)),
+            dma((4,)),
             dma((2,)),
+            dma((LINE,)),
         ],
         compiler_params=pltpu.CompilerParams(
             collective_id=3, has_side_effects=True, vmem_limit_bytes=63 * 2**20
@@ -2178,8 +2317,11 @@
         cost_estimate=pl.CostEstimate(
             flops=64 * 10**9, bytes_accessed=60 * 10**6, transcendentals=10**7
         ),
+        input_output_aliases={21: 1},
         name="back",
-    )(lefts, rights, grad_mid, aux_all, gain_in, wof, wall, n1, x, kv, q, att, lse, trig, att_low, lengths)
+    )(
+        lefts, n2, cot, hid, rest, *own[:2], *peer[:2], aux_all, wof, wall, n1, x, kv, q, att, lse, trig, att_low, lengths, result
+    )
 
 
 def per_device(
@@ -2242,15 +2384,17 @@
         seq_lengths,
         freq,
     )
-    out_part, lefts, rights, grad_mid, grad_gain_two = mlp(
-        normed_two, cot_full, hidden_mid, aux_all, own, peer
-    )
-    grad_inputs, sums, grad_w_query, grad_kv, small = back(
+    lefts, normed_full, result, rest = mlp(normed_two, cot_full, hidden_mid, own, peer)
+    grad_inputs, result, sums, grad_w_query, grad_kv, small = back(
         lefts,
-        rights,
-        grad_mid,
+        normed_full,
+        cot_full,
+        hidden_mid,
+        rest,
+        result,
+        own,
+        peer,
         aux_all,
-        grad_gain_two,
         wof,
         wall,
         normed_one,
@@ -2262,13 +2406,12 @@
         trig,
         att_low.reshape(rows, width),
         seq_lengths,
-        hidden,
-    )
-    result = lax.psum_scatter(out_part, "col", scatter_dimension=1, tiled=True)
-    grad_w_down, grad_w_gate, grad_w_up = (
+    )
+    grad_w_gate, grad_w_up, grad_w_down = (
         sums[k * hidden : (k + 1) * hidden].astype(f32) for k in range(3)
     )
-    grad_w_out = sums[3 * hidden : 3 * hidden + width].astype(f32)
+    first = 3 * hidden + TILE // 2 + HEAD_WIDTH
+    grad_w_out = sums[first : first + width].astype(f32)
     grad_kv = grad_kv.astype(f32)
     small = small.astype(f32)
     bias = small[8]

time: 569 us -> 540 us (0.949)
  between operations: 14.6 us -> 1.16 us
  local copies, waits for them, and re-layouts: 20.2 us -> 14.1 us
  Pallas kernels: 509 us -> 503 us
    pallas_call x1, Pallas kernels: 93.5 us -> 70 us  [mlp(): pl.pallas_call(mlp_kernel, out_shape=[shape((3, rows, padded), bf16), sha...]
    pallas_call x1, Pallas kernels: 268 us -> 285 us  [back(): pl.pallas_call(functools.partial(back_kernel, heads), out_shape=[o[0] for...]
    unnamed x19 -> x20, local copies, waits for them, and re-layouts: 15.8 us -> 9.72 us
  transfers between devices with their start and end apart: 1 -> 0, of which waited for: 0 -> 0; matrix products, arithmetic and copies ran while one was open for 3% -> 0% of each run, Pallas kernels for 48% -> 0%
where the time goes in v5:
time: 540 us; the launch traced here: 534 us
  Pallas kernels  503 us (93%)
  other arithmetic  16 us (3%)
  local copies, waits for them, and re-layouts  14.1 us (3%)
    pallas_call x1, Pallas kernels, back(): pl.pallas_call(functools.partial(back_kernel, heads), out_shape=[o[0] for...  285 us
    pallas_call x1, Pallas kernels, front(): pl.pallas_call(functools.partial(front_kernel, heads, dims), out_shape=[o...  148 us
    pallas_call x1, Pallas kernels, mlp(): pl.pallas_call(mlp_kernel, out_shape=[shape((3, rows, padded), bf16), sha...  70 us

profile of v5, /device:TPU:0, one launch (start us, length us, event | category | flops | bytes accessed | tf_op | source)
XLA Modules:
  0.0 534.1 jit_solution(12796197644377062932)
XLA Ops:
  0.7 0.1 maximum_bitcast_fusion.freq
  0.7 0.7 stack.21
  1.4 0.7 reshape.39
  2.1 0.7 stack.22
  2.8 0.7 fusion.3
  3.6 1.1 copy.30
  4.6 1.1 copy.31
  5.7 0.1 pad_maximum_fusion.wkv
  5.8 0.0 copy-start
  5.8 1.1 copy-done
  6.9 1.1 copy-done.1
  7.9 0.0 copy-start.2
  8.0 0.7 copy-done.2
  8.6 147.6 %front.1 = (bf16[1024,1536]{1,0:T(8,128)(2,1)}, bf16[1024,1536]{1,0:T(8,128)(2,1)}, bf16[1024,1536]{1,0:T(8,128)(2,1)}, bf16[3,1024,128]{2,1,0:T(8,128)(2,1)}, b...) custom-call(f32[8,384]{1,0:T(8,128)S(1)} %select_maximum_fusion.aux,, ...), custom_call_target="tpu_custom_call" | custom-call | flops 10000000000 | bytes 60000000 | tf_op jit(solution)/shard_map/front/pallas_call | solution.py:940
  156.2 0.0 copy-start.3
  156.2 0.8 copy-done.3
  157.0 0.6 copy-done.4
  157.6 70.0 %mlp.1 = (bf16[3,1024,2304]{2,1,0:T(8,128)(2,1)}, bf16[1024,1536]{1,0:T(8,128)(2,1)}, bf16[1024,384]{1,0:T(8,128)(2,1)}, bf16[2,256,1536]{2,1,0:T(8,128)(2,1)}) custom-call(bf16[256,1536]{1,0:T(8,128)(2,1)} %get-tuple-element.41.n2, bf16[1024,1536]{1,0:T(8,128)(2,1)} %get-tuple-element.42.cot_full.cot_in, f32[256,1536]{1,0:T(8,128)} %get-tuple-element.43.hid.hid_in, ...), custom_call_target="tpu_custom_call" | custom-call | flops 20999999488 | bytes 60000000 | tf_op jit(solution)/shard_map/mlp/pallas_call | solution.py:1321
  227.5 285.2 %back.1 = (bf16[1024,384]{1,0:T(8,128)(2,1)}, bf16[1024,384]{1,0:T(8,128)(2,1)}, bf16[7680,768]{1,0:T(8,128)(2,1)}, bf16[768,384]{1,0:T(8,128)(2,1)}, bf16[768,128]{1,0:T(8,128)(2,1)}, /*index=5*/bf16[16,768]{1,0:T(8,128)(2,1)}) custom-call(bf16[3,1024,2304]{2,1,0:T(8,128)(2,1)} %get-tuple-element.47.lefts, ...), custom_call_target="tpu_custom_call", output_to_operand_aliasing={{1}: (21, {})} | custom-call | flops 64000000000 | bytes 60000000 | tf_op jit(solution)/shard_map/back/pallas_call | solution.py:2251
  512.8 0.7 convert_element_type.23
  513.5 0.6 slice_bitcast_fusion
  514.1 0.6 slice_reduce_fusion
  514.7 1.1 fusion.4
  515.9 0.8 copy.33
  516.7 0.8 copy.32
  517.5 2.2 convert_element_type.24
  519.7 2.2 slice_convert_fusion.1
  521.8 10.0 %slice_convert_fusion = (f32[2240,768]{1,0:T(8,128)}, f32[768,2240]{0,1:T(8,128)}, f32[768,2240]{0,1:T(8,128)}) fusion(bf16[7680,768]{1,0:T(8,128)(2,1)} %get-tuple-element.67), kind=kLoop, calls=%fused_computation.2 | loop fusion | flops 5160960 | bytes 30965760 | tf_op jit(solution)/shard_map/convert_element_type | solution.py:2411
  531.8 0.0 copy-done.6
  531.9 0.9 copy.37
  532.7 0.0 copy-done.5
  532.7 0.9 copy.38
  (7 shorter events, 0.0 us)
Async XLA Ops:
  5.8 1.1 copy-start
  6.9 1.1 copy-start.1
  7.9 0.7 copy-start.2
  156.2 0.8 copy-start.3
  157.0 0.6 copy-start.4
  521.8 10.0 %copy-start.6 = (bf16[1024,384]{1,0:T(8,128)(2,1)S(1)}, bf16[1024,384]{1,0:T(8,128)(2,1)}, u32[]{:S(2)}) copy-start(bf16[1024,384]{1,0:T(8,128)(2,1)} %get-tuple-element.106) | copy-start | bytes 2359300
  521.8 10.9 %copy-start.5 = (bf16[1024,384]{1,0:T(8,128)(2,1)S(1)}, bf16[1024,384]{1,0:T(8,128)(2,1)}, u32[]{:S(2)}) copy-start(bf16[1024,384]{1,0:T(8,128)(2,1)} %get-tuple-element.107) | copy-start | bytes 2359300

commit v6 on v5

--- a/solution.py
+++ b/solution.py
@@ -539,7 +539,7 @@
     cot_out,
     q_out,
     kv_out,
-    att_out,
+    att_hbm,
     lse_out,
     attl_out,
     hid_out,
@@ -547,8 +547,8 @@
     trig_out,
     att_low,
     aux_out,
-    wall_out,
-    wof_out,
+    wall_hbm,
+    wof_hbm,
     peer_gate,
     peer_up,
     peer_down,
@@ -576,6 +576,10 @@
     a2a_recv,
     m_send,
     m_recv,
+    att_out,
+    wall_out,
+    wof_out,
+    out_sem,
 ):
     count, planes = dims
     f32, bf16 = jnp.float32, jnp.bfloat16
@@ -744,6 +748,8 @@
     n1_copy.start()
     x_copy = pltpu.make_async_copy(x_full, x_out, local_sem.at[6])
     x_copy.start()
+    wall_copy = pltpu.make_async_copy(wall_out, wall_hbm, out_sem.at[0])
+    wall_copy.start()
 
     copy_o.wait()
     for k in range(1, count):
@@ -835,6 +841,8 @@
         chain_c.step(1, block)
 
     attl_out[:, own_lanes] = att_low[col]
+    att_copy = pltpu.make_async_copy(att_out, att_hbm, out_sem.at[1])
+    att_copy.start()
     for step in range(2, count - 1):
 
         @pl.loop(0, count)
@@ -853,6 +861,9 @@
     for k in range(planes):
         other = wof_blocks(lax.rem(dp + planes - k, planes), 1 - row)
         remote(other, other, r_send.at[k], r_recv.at[k], partner).wait_recv()
+
+    wof_copy = pltpu.make_async_copy(wof_out, wof_hbm, out_sem.at[2])
+    wof_copy.start()
 
     @pl.loop(0, count)
     def _(block):
@@ -904,7 +915,7 @@
         def _():
             a2a_copy(chunk).wait_send()
 
-    for copy in (n1_copy, x_copy, c_copy):
+    for copy in (n1_copy, x_copy, c_copy, wall_copy, att_copy, wof_copy):
         copy.wait()
 
 
@@ -922,7 +933,7 @@
         (shape((rows, D), bf16), any_spec()),
         (shape((heads, rows, HEAD_WIDTH), bf16), vmem_spec()),
         (shape((2 * rows, 2 * HEAD_WIDTH), bf16), vmem_spec()),
-        (shape((heads, rows, HEAD_WIDTH), f32), vmem_spec()),
+        (shape((heads, rows, HEAD_WIDTH), f32), any_spec()),
         (shape((rows, HEAD_WIDTH), f32), vmem_spec()),
         (shape((part, D), bf16), vmem_spec()),
         (shape((part, D), f32), vmem_spec()),
@@ -930,8 +941,8 @@
         (shape((2, rows, HEAD_WIDTH), f32), vmem_spec()),
         (shape((count, part, width), bf16), vmem_spec()),
         (shape((count,) + aux.shape, f32), vmem_spec()),
-        (shape((D, wall), bf16), vmem_spec()),
-        (shape((count, wout.shape[0], D), bf16), vmem_spec()),
+        (shape((D, wall), bf16), any_spec()),
+        (shape((count, wout.shape[0], D), bf16), any_spec()),
         (shape(w_gate.shape, bf16), any_spec()),
         (shape(w_up.shape, bf16), any_spec()),
         (shape(w_down.shape, bf16), any_spec()),
@@ -968,6 +979,10 @@
             dma((count,)),
             dma((count,)),
             dma((3,)),
+            dma((3,)),
+            pltpu.VMEM((heads, rows, HEAD_WIDTH), f32),
+            pltpu.VMEM((D, wall), bf16),
+            pltpu.VMEM((count, wout.shape[0], D), bf16),
             dma((3,)),
         ],
         compiler_params=pltpu.CompilerParams(
@@ -1752,12 +1767,6 @@
         def _():
             tile_copy(step + 2).start()
 
-        for number, when in enumerate((1, 2, 3, 5, 7, 9, 11)):
-
-            @pl.when(step == when)
-            def _():
-                reduce.step(number)
-
         @pl.when(step == 3)
         def _():
             out.near(0)
@@ -1789,6 +1798,12 @@
         def _():
             gn.near(2)
             gn.far(1)
+
+        for number, when in enumerate((1, 2, 3, 5, 7, 9, 11)):
+
+            @pl.when(step == when)
+            def _():
+                reduce.step(number)
 
     wof_copies = [
         pltpu.make_async_copy(
@@ -1820,8 +1835,8 @@
         copy.wait()
     gn.near(3)
     gn.far(2)
+    gn.far(3)
     reduce.step(7)
-    gn.far(3)
     reduce.step(8)
 
     gain_sum[...] = jnp.zeros_like(gain_sum)
@@ -1989,12 +2004,12 @@
             lanes = slice(h * HEAD_WIDTH, (h + 1) * HEAD_WIDTH)
             turned = rotate(grad[h * part : (h + 1) * part] * SCALE, cosine, sine)
             ga[here, lanes] = turned.astype(bf16)
-        reduce.step(10 + turn)
-
         @pl.when(turn == LINE - 1)
         def _():
             for chunk in range(2):
                 chain.step(1, chunk)
+
+        reduce.step(10 + turn)
 
     kv_give[...] = acc[:, lanes_at((1 - row) * 2 * HEAD_WIDTH, 2 * HEAD_WIDTH)].astype(bf16)
     kv_copy = remote(kv_give, kv_got, kv_sem.at[0], kv_sem.at[1], partner)
@@ -2117,15 +2132,18 @@
                 share = share + mid[:, lanes] * own
                 wt[chunk // 2, there, lanes] = share.astype(bf16)
             fin.ends(chunk)
+
+        @pl.when((chunk >= 1) & (chunk <= LINE))
+        def _():
+            fin.near(chunk - 1)
+
+        @pl.when(chunk >= 2)
+        def _():
+            fin.far(chunk - 2)
+
+        @pl.when(chunk < LINE)
+        def _():
             reduce.step(17 + chunk)
-
-        @pl.when((chunk >= 1) & (chunk <= LINE))
-        def _():
-            fin.near(chunk - 1)
-
-        @pl.when(chunk >= 2)
-        def _():
-            fin.far(chunk - 2)
 
     gains[...] = gain_sum[...]
 

time: 540 us -> 536 us (level)
  no operation moved by 1% of the time
where the time goes in v6:
time: 536 us; the launch traced here: 529 us
  Pallas kernels  498 us (93%)
  other arithmetic  16 us (3%)
  local copies, waits for them, and re-layouts  14.1 us (3%)
    pallas_call x1, Pallas kernels, back(): pl.pallas_call(functools.partial(back_kernel, heads), out_shape=[o[0] for...  283 us
    pallas_call x1, Pallas kernels, front(): pl.pallas_call(functools.partial(front_kernel, heads, dims), out_shape=[o...  145 us
    pallas_call x1, Pallas kernels, mlp(): pl.pallas_call(mlp_kernel, out_shape=[shape((3, rows, padded), bf16), sha...  70 us

profile of v6, /device:TPU:0, one launch (start us, length us, event | category | flops | bytes accessed | tf_op | source)
XLA Modules:
  0.0 529.3 jit_solution(4783932232252831625)
XLA Ops:
  0.7 0.1 maximum_bitcast_fusion.freq
  0.7 0.7 stack.21
  1.4 0.7 reshape.39
  2.1 0.7 stack.22
  2.8 0.7 fusion.3
  3.6 1.1 copy.30
  4.6 1.1 copy.31
  5.7 0.1 pad_maximum_fusion.wkv
  5.8 0.0 copy-start
  5.8 1.1 copy-done
  6.9 0.0 copy-start.1
  6.9 1.1 copy-done.1
  8.0 0.7 copy-done.2
  8.6 145.1 %front.1 = (bf16[1024,1536]{1,0:T(8,128)(2,1)}, bf16[1024,1536]{1,0:T(8,128)(2,1)}, bf16[1024,1536]{1,0:T(8,128)(2,1)}, bf16[3,1024,128]{2,1,0:T(8,128)(2,1)}, b...) custom-call(f32[8,384]{1,0:T(8,128)S(1)} %select_maximum_fusion.aux,, ...), custom_call_target="tpu_custom_call" | custom-call | flops 10000000000 | bytes 60000000 | tf_op jit(solution)/shard_map/front/pallas_call | solution.py:951
  153.7 0.0 copy-start.3
  153.7 0.8 copy-done.3
  154.5 0.6 copy-done.4
  155.1 70.0 %mlp.1 = (bf16[3,1024,2304]{2,1,0:T(8,128)(2,1)}, bf16[1024,1536]{1,0:T(8,128)(2,1)}, bf16[1024,384]{1,0:T(8,128)(2,1)}, bf16[2,256,1536]{2,1,0:T(8,128)(2,1)}) custom-call(bf16[256,1536]{1,0:T(8,128)(2,1)} %get-tuple-element.41.n2, bf16[1024,1536]{1,0:T(8,128)(2,1)} %get-tuple-element.42.cot_full.cot_in, f32[256,1536]{1,0:T(8,128)} %get-tuple-element.43.hid.hid_in, ...), custom_call_target="tpu_custom_call" | custom-call | flops 20999999488 | bytes 60000000 | tf_op jit(solution)/shard_map/mlp/pallas_call | solution.py:1336
  225.1 283.0 %back.1 = (bf16[1024,384]{1,0:T(8,128)(2,1)}, bf16[1024,384]{1,0:T(8,128)(2,1)}, bf16[7680,768]{1,0:T(8,128)(2,1)}, bf16[768,384]{1,0:T(8,128)(2,1)}, bf16[768,128]{1,0:T(8,128)(2,1)}, /*index=5*/bf16[16,768]{1,0:T(8,128)(2,1)}) custom-call(bf16[3,1024,2304]{2,1,0:T(8,128)(2,1)} %get-tuple-element.47.lefts, ...), custom_call_target="tpu_custom_call", output_to_operand_aliasing={{1}: (21, {})} | custom-call | flops 64000000000 | bytes 60000000 | tf_op jit(solution)/shard_map/back/pallas_call | solution.py:2269
  508.1 0.7 convert_element_type.23
  508.8 0.6 slice_bitcast_fusion
  509.4 0.6 slice_reduce_fusion
  510.0 1.1 fusion.4
  511.1 0.8 copy.33
  512.0 0.8 copy.32
  512.8 2.2 convert_element_type.24
  514.9 2.2 slice_convert_fusion.1
  517.1 10.0 %slice_convert_fusion = (f32[2240,768]{1,0:T(8,128)}, f32[768,2240]{0,1:T(8,128)}, f32[768,2240]{0,1:T(8,128)}) fusion(bf16[7680,768]{1,0:T(8,128)(2,1)} %get-tuple-element.67), kind=kLoop, calls=%fused_computation.2 | loop fusion | flops 5160960 | bytes 30965760 | tf_op jit(solution)/shard_map/convert_element_type | solution.py:2429
  527.1 0.0 copy-done.6
  527.1 0.9 copy.37
  528.0 0.0 copy-done.5
  528.0 0.9 copy.38
  (7 shorter events, 0.0 us)
Async XLA Ops:
  5.8 1.1 copy-start
  6.9 1.1 copy-start.1
  7.9 0.7 copy-start.2
  153.7 0.8 copy-start.3
  154.5 0.6 copy-start.4
  517.1 10.0 %copy-start.6 = (bf16[1024,384]{1,0:T(8,128)(2,1)S(1)}, bf16[1024,384]{1,0:T(8,128)(2,1)}, u32[]{:S(2)}) copy-start(bf16[1024,384]{1,0:T(8,128)(2,1)} %get-tuple-element.106) | copy-start | bytes 2359300
  517.1 10.9 %copy-start.5 = (bf16[1024,384]{1,0:T(8,128)(2,1)S(1)}, bf16[1024,384]{1,0:T(8,128)(2,1)}, u32[]{:S(2)}) copy-start(bf16[1024,384]{1,0:T(8,128)(2,1)} %get-tuple-element.107) | copy-start | bytes 2359300

commit v7 on v6

--- a/solution.py
+++ b/solution.py
@@ -843,12 +843,6 @@
     attl_out[:, own_lanes] = att_low[col]
     att_copy = pltpu.make_async_copy(att_out, att_hbm, out_sem.at[1])
     att_copy.start()
-    for step in range(2, count - 1):
-
-        @pl.loop(0, count)
-        def _(chunk):
-            chain_c.step(step, chunk)
-
     for k in range(1, planes):
         remote(
             wof_blocks(dp, row),
@@ -858,6 +852,12 @@
             partner,
         ).wait_recv()
         r_copies[k].start()
+    for step in range(2, count - 1):
+
+        @pl.loop(0, count)
+        def _(chunk):
+            chain_c.step(step, chunk)
+
     for k in range(planes):
         other = wof_blocks(lax.rem(dp + planes - k, planes), 1 - row)
         remote(other, other, r_send.at[k], r_recv.at[k], partner).wait_recv()
@@ -2371,7 +2371,7 @@
     biases = jnp.pad(biases, (0, width - 2 * kv_cols))
     aux = jnp.stack([gain_one, gain_two, b_query.astype(f32), biases])
     aux = jnp.pad(aux, ((0, 4), (0, 0)))
-    own_kv = jnp.concatenate([w_key, w_value], axis=1)
+    own_kv = jnp.concatenate([w_key.T, w_value.T], axis=0).T
     own = (w_gate.T, w_up.T, w_down)
     (
         x_full,

time: 536 us -> 536 us (level)
  no operation moved by 1% of the time
where the time goes in v7:
time: 536 us; the launch traced here: 529 us
  Pallas kernels  498 us (93%)
  other arithmetic  16 us (3%)
  local copies, waits for them, and re-layouts  14.1 us (3%)
    pallas_call x1, Pallas kernels, back(): pl.pallas_call(functools.partial(back_kernel, heads), out_shape=[o[0] for...  283 us
    pallas_call x1, Pallas kernels, front(): pl.pallas_call(functools.partial(front_kernel, heads, dims), out_shape=[o...  145 us
    pallas_call x1, Pallas kernels, mlp(): pl.pallas_call(mlp_kernel, out_shape=[shape((3, rows, padded), bf16), sha...  70 us

profile of v7, /device:TPU:0, one launch (start us, length us, event | category | flops | bytes accessed | tf_op | source)
XLA Modules:
  0.0 529.3 jit_solution(6623835806795641249)
XLA Ops:
  0.7 0.1 maximum_bitcast_fusion.1.freq
  0.7 0.7 stack.21
  1.4 0.7 reshape.39
  2.1 0.7 stack.22
  2.8 0.7 fusion.3
  3.6 1.1 copy.30
  4.6 1.1 copy.31
  5.7 0.1 maximum_bitcast_fusion.wkv
  5.8 0.0 copy-start
  5.8 1.1 copy-done
  6.9 0.0 copy-start.1
  6.9 1.1 copy-done.1
  8.0 0.7 copy-done.2
  8.6 145.1 %front.1 = (bf16[1024,1536]{1,0:T(8,128)(2,1)}, bf16[1024,1536]{1,0:T(8,128)(2,1)}, bf16[1024,1536]{1,0:T(8,128)(2,1)}, bf16[3,1024,128]{2,1,0:T(8,128)(2,1)}, b...) custom-call(f32[8,384]{1,0:T(8,128)S(1)} %select_maximum_fusion.aux,, ...), custom_call_target="tpu_custom_call" | custom-call | flops 10000000000 | bytes 60000000 | tf_op jit(solution)/shard_map/front/pallas_call | solution.py:951
  153.7 0.0 copy-start.3
  153.7 0.8 copy-done.3
  154.5 0.6 copy-done.4
  155.1 70.0 %mlp.1 = (bf16[3,1024,2304]{2,1,0:T(8,128)(2,1)}, bf16[1024,1536]{1,0:T(8,128)(2,1)}, bf16[1024,384]{1,0:T(8,128)(2,1)}, bf16[2,256,1536]{2,1,0:T(8,128)(2,1)}) custom-call(bf16[256,1536]{1,0:T(8,128)(2,1)} %get-tuple-element.41.n2, bf16[1024,1536]{1,0:T(8,128)(2,1)} %get-tuple-element.42.cot_full.cot_in, f32[256,1536]{1,0:T(8,128)} %get-tuple-element.43.hid.hid_in, ...), custom_call_target="tpu_custom_call" | custom-call | flops 20999999488 | bytes 60000000 | tf_op jit(solution)/shard_map/mlp/pallas_call | solution.py:1336
  225.1 283.0 %back.1 = (bf16[1024,384]{1,0:T(8,128)(2,1)}, bf16[1024,384]{1,0:T(8,128)(2,1)}, bf16[7680,768]{1,0:T(8,128)(2,1)}, bf16[768,384]{1,0:T(8,128)(2,1)}, bf16[768,128]{1,0:T(8,128)(2,1)}, /*index=5*/bf16[16,768]{1,0:T(8,128)(2,1)}) custom-call(bf16[3,1024,2304]{2,1,0:T(8,128)(2,1)} %get-tuple-element.47.lefts, ...), custom_call_target="tpu_custom_call", output_to_operand_aliasing={{1}: (21, {})} | custom-call | flops 64000000000 | bytes 60000000 | tf_op jit(solution)/shard_map/back/pallas_call | solution.py:2269
  508.0 0.7 convert_element_type.23
  508.8 0.6 slice_bitcast_fusion
  509.4 0.6 slice_reduce_fusion
  510.0 1.1 fusion.4
  511.1 0.8 copy.33
  511.9 0.8 copy.32
  512.8 2.2 convert_element_type.24
  514.9 2.2 slice_convert_fusion.1
  517.1 10.0 %slice_convert_fusion = (f32[2240,768]{1,0:T(8,128)}, f32[768,2240]{0,1:T(8,128)}, f32[768,2240]{0,1:T(8,128)}) fusion(bf16[7680,768]{1,0:T(8,128)(2,1)} %get-tuple-element.67), kind=kLoop, calls=%fused_computation.2 | loop fusion | flops 5160960 | bytes 30965760 | tf_op jit(solution)/shard_map/convert_element_type | solution.py:2429
  527.1 0.0 copy-done.6
  527.1 0.9 copy.37
  528.0 0.0 copy-done.5
  528.0 0.9 copy.38
  (7 shorter events, 0.0 us)
Async XLA Ops:
  5.8 1.1 copy-start
  6.9 1.1 copy-start.1
  7.9 0.7 copy-start.2
  153.7 0.8 copy-start.3
  154.5 0.6 copy-start.4
  517.1 10.0 %copy-start.6 = (bf16[1024,384]{1,0:T(8,128)(2,1)S(1)}, bf16[1024,384]{1,0:T(8,128)(2,1)}, u32[]{:S(2)}) copy-start(bf16[1024,384]{1,0:T(8,128)(2,1)} %get-tuple-element.106) | copy-start | bytes 2359300
  517.1 10.9 %copy-start.5 = (bf16[1024,384]{1,0:T(8,128)(2,1)S(1)}, bf16[1024,384]{1,0:T(8,128)(2,1)}, u32[]{:S(2)}) copy-start(bf16[1024,384]{1,0:T(8,128)(2,1)} %get-tuple-element.107) | copy-start | bytes 2359300
